TPU v7x, 512 devices: a whole 4x8x8 slice. The times are simulated.
512 devices in a mesh: ops: 32 (over y, x), sec: 16 (over z, core).
Axes of the slice: x: 4, y: 8, z: 8, core: 2. Of those that a mesh axis runs over, the one named last changes fastest.
Arguments:
- wavefunction: bfloat16 [32, 256, 256], P('sec'), may hold values from -6 to 6
- left_ops: bfloat16 [256, 32, 256, 256], P('ops', 'sec')
- right_ops: bfloat16 [256, 32, 256, 256], P('ops', 'sec')
- charge: int32 [256], P('ops'), may hold values from 0 to 31
- block_sizes: int32 [32], replicated, may hold values from 64 to 256, as said below
Outputs:
- sigma: bfloat16 [32, 256, 256], P('sec', 'ops')
- residual: bfloat16 [32, 256, 256], P('sec', 'ops')
Inputs may be any that keep to these rules, and one draw needn't show every extreme that they name: `block_sizes`: every sector's live size lies between 64 and 256; rows and columns at or past it are padding; at least one sector is full.
All inputs are finite; a program needn't handle non-finite values.
Results may differ from a plain program's by a relative error of at most 0.005.
Values may be sent and summed in bfloat16 or wider, within the bound.
No kernel may reach another device: no remote copies, remote signals or barrier semaphores. Data moves between devices by JAX's collectives and lax.ppermute only.
A program may use at most 64 MiB of HBM per device.

v0:
```python
import jax
import jax.numpy as jnp
from jax import lax
from jax.sharding import PartitionSpec as P


def local(wavefunction, left_ops, right_ops, charge, block_sizes):
    sec_count = wavefunction.shape[0]
    block_width = wavefunction.shape[1]
    ops_count = lax.axis_size("ops")
    row_count = block_width // ops_count
    operator_slot = lax.axis_index("ops")
    sec_place = lax.axis_index("sec")
    sector_total = block_sizes.shape[0]
    slot_positions = jnp.arange(block_width, dtype=jnp.int32)
    live_all = (slot_positions[None, :] < block_sizes[:, None]).astype(jnp.bfloat16)
    gathered = lax.all_gather(wavefunction, "sec", axis=0, tiled=True)
    masked = gathered * live_all[:, :, None] * live_all[:, None, :]
    targets = sec_place * sec_count + jnp.arange(sec_count, dtype=jnp.int32)
    sources = (targets[None, :] + charge[:, None]) % sector_total
    selected_rows = jnp.take(masked, sources, axis=0)
    split_pieces = jnp.einsum(
        "pkab,pkbc->pkac", left_ops, selected_rows, preferred_element_type=jnp.float32
    ).astype(jnp.bfloat16)
    partial_sum = jnp.einsum(
        "pkac,pkdc->kad", split_pieces, right_ops, preferred_element_type=jnp.float32
    )
    summed = lax.psum(partial_sum, "ops")
    summed = lax.dynamic_slice_in_dim(summed, operator_slot * row_count, row_count, 1)
    factor = float(charge.shape[0] * ops_count) ** (-0.5)
    own_live = lax.dynamic_slice_in_dim(live_all, sec_place * sec_count, sec_count, 0).astype(
        jnp.float32
    )
    row_live = lax.dynamic_slice_in_dim(own_live, operator_slot * row_count, row_count, 1)
    sigma_block = summed * factor * row_live[:, :, None] * own_live[:, None, :]
    own_rows = lax.dynamic_slice_in_dim(
        wavefunction, operator_slot * row_count, row_count, 1
    ).astype(jnp.float32)
    own_rows = own_rows * row_live[:, :, None] * own_live[:, None, :]
    correlation, norm_sq = lax.psum(
        (jnp.sum(own_rows * sigma_block), jnp.sum(own_rows * own_rows)), ("ops", "sec")
    )
    ritz_value = correlation / norm_sq
    return (
        sigma_block.astype(jnp.bfloat16),
        (sigma_block - ritz_value * own_rows).astype(jnp.bfloat16),
    )


def solution(mesh):
    placed = (
        P("sec", None, None),
        P("ops", "sec", None, None),
        P("ops", "sec", None, None),
        P("ops"),
        P(),
    )
    return jax.shard_map(
        local,
        mesh=mesh,
        in_specs=placed,
        out_specs=(P("sec", "ops", None), P("sec", "ops", None)),
        check_vma=False,
    )
```

profile of v0, /device:TPU:1, one launch (start us, length us, event | category | flops | bytes accessed | tf_op | source)
XLA Modules:
  0.0 341.9 jit_solution(5086231256536438574)
XLA Ops:
  7.2 0.0 copy-start
  7.2 0.0 all-gather.2.cloned.1.call-start
  7.2 0.7 all-gather.2.cloned.1.call-update
  7.9 0.0 all-reduce.3.cloned.1.call-start
  8.0 0.7 compare_select_fusion
  8.7 0.1 reshape.154
  8.8 0.7 compare_and_fusion
  9.5 0.7 fusion.23
  10.3 51.5 %all-gather.2.cloned.1.call-done = bf16[32,256,256]{2,1,0:T(8,128)(2,1)} async-done(((bf16[2,256,256]{2,1,0:T(8,128)(2,1)}), bf16[32,256,256]{2,1,0:T(8,128)(2,1)}) %all-gather.2.cloned.1.call-update) | async-done | bytes 4194320 | tf_op jit(solution)/shard_map/all_gather | solution.py:17
  61.8 4.1 %multiply_multiply_fusion = bf16[32,256,256]{2,1,0:T(8,128)(2,1)} fusion(bf16[32,256,256]{2,1,0:T(8,128)(2,1)} %all-gather.2.cloned.1.call-done, bf16[32,256]{1,0:T(8,128)(2,1)S(1)} %fusion.23), kind=kLoop, calls=%fused_computation.1 | loop fusion | flops 4194304 | bytes 8404992 | tf_op jit(solution)/shard_map/mul | solution.py:18
  65.9 4.2 %gather_fusion = bf16[16,256,256]{2,1,0:T(8,128)(2,1)} fusion(bf16[32,256,256]{2,1,0:T(8,128)(2,1)} %multiply_multiply_fusion, s32[1024]{0:T(1024)S(1)} %pad_clamp_fusion), kind=kCustom, calls=%fused_computation | custom fusion | bytes 4194368 | tf_op jit(solution)/shard_map/jit(_take)/gather | solution.py:21
  70.1 3.9 %copy.9 = bf16[8,2,256,256]{2,3,0,1:T(8,128)(2,1)} copy(bf16[8,2,256,256]{3,2,1,0:T(8,128)(2,1)} %bitcast.11) | data formatting | bytes 4194304 | tf_op jit(solution)/shard_map/jit(_take)/gather | solution.py:21
  74.0 0.0 copy-done
  74.0 4.3 %fusion.8 = f32[2,256,256]{2,1,0:T(8,128)} fusion(bf16[8,2,256,256]{3,2,1,0:T(8,128)(2,1)S(1)} %copy-done, bf16[8,2,256,256]{3,2,1,0:T(8,128)(2,1)} %param.6, bf16[8,2,256,256]{2,3,0,1:T(8,128)(2,1)} %copy.9, pred[8,2]{0,1:T(4,128)(4,1)S(1)} %compare_and_fusion), kind=kOutput, calls=%fused_computation.10 | convolution fusion | flops 1075838976 | bytes 6815760 | tf_op jit(solution)/shard_map/pkac,pkdc->kad/dot_general | solution.py:25
  78.3 0.0 all-reduce.3.cloned.1.call-update
  78.4 0.1 broadcast_multiply_fusion
  78.5 151.5 %all-reduce.3.cloned.1.call-done = f32[2,256,256]{2,1,0:T(8,128)} async-done(((f32[2,256,256]{2,1,0:T(8,128)}), f32[2,256,256]{2,1,0:T(8,128)}) %all-reduce.3.cloned.1.call-update) | async-done | bytes 524304 | tf_op jit(solution)/shard_map/psum | solution.py:28
  230.0 1.4 multiply_reduce_fusion
  231.4 100.9 %all-reduce = (f32[]{:T(128)}, f32[]{:T(128)}) all-reduce(f32[]{:T(128)} %get-tuple-element.3, f32[]{:T(128)} %get-tuple-element.2), channel_id=1, replica_groups=mesh['ops'=32,'sec'=16] {'ops','sec'}, use_global_device_ids=true, to_apply=%region_2.3 | all-reduce | flops 2 | bytes 16 | tf_op jit(solution)/shard_map/psum | solution.py:40
  333.6 1.4 subtract_convert_fusion
  (3 shorter events, 0.0 us)
Async XLA Ops:
  7.2 66.8 %copy-start = (bf16[8,2,256,256]{3,2,1,0:T(8,128)(2,1)S(1)}, bf16[8,2,256,256]{3,2,1,0:T(8,128)(2,1)}, u32[]{:S(2)}) copy-start(bf16[8,2,256,256]{3,2,1,0:T(8,128)(2,1)} %param.7) | copy-start | bytes 6291460
  7.2 54.6 %all-gather.2.cloned.1.call-start = ((), (), s32[]{:S(2)}) async-start(), calls=%async_computation | async-start | bytes 4456448 | tf_op jit(solution)/shard_map/all_gather | solution.py:17
  7.9 222.1 %all-reduce.3.cloned.1.call-start = ((), (), s32[]{:S(2)}) async-start(), calls=%async_computation.1 | async-start | bytes 1048576 | tf_op jit(solution)/shard_map/psum | solution.py:28
Sparse Core Ops, SparseCore 0:
  10.1 51.5 all-gather.1
  78.5 151.4 all-reduce.2
where the time goes:
time: 342 us
  waiting for transfers between devices  204 us (60%)
  blocking collectives  101 us (30%)
  between operations  15.4 us (5%)
  other arithmetic  9.26 us (3%)
  local copies, waits for them, and re-layouts  8.21 us (2%)
  matrix products  4.34 us (1%)
    psum x1, waiting for transfers between devices, local(): summed = lax.psum(partial_sum, 'ops')  152 us
    psum x1, blocking collectives, local(): lax.psum((jnp.sum(own_rows * sigma_block), jnp.sum(own_rows * own_rows)),...  101 us
    all_gather x1, waiting for transfers between devices, local(): gathered = lax.all_gather(wavefunction, 'sec', axis=0, tiled=True)  51.5 us
    gather x2, local copies, waits for them, and re-layouts, local(): selected_rows = jnp.take(masked, sources, axis=0)  8.12 us
  transfers between devices with their start and end apart: 2, of which 2 were waited for; matrix products, arithmetic and copies ran while one was open for 1% of the time, Pallas kernels for 0%

commit v1 on v0

v1 whole, which is shorter than its diff:
```python
import jax
import jax.numpy as jnp
from jax import lax
from jax.experimental import pallas as pl
from jax.experimental.pallas import tpu as pltpu
from jax.sharding import PartitionSpec as P

LANES = 128


def sigma_kernel(pairs, targets_here, sectors, rows, factor):
    def body(
        sec_ref, charge_ref, sizes_ref, psi_ref, left_ref, right_ref,
        out_ref, psi_buf, left_buf, right_buf, psi_sem, left_sem, right_sem,
    ):
        first = sec_ref[0] * targets_here
        block = left_buf.shape[-1]

        def source(p, k):
            return lax.rem(first + k + charge_ref[p], sectors)

        copies = []
        for p in range(pairs):
            left = pltpu.make_async_copy(left_ref.at[p], left_buf.at[p], left_sem.at[p])
            right = pltpu.make_async_copy(right_ref.at[p], right_buf.at[p], right_sem.at[p])
            blocks = [
                pltpu.make_async_copy(
                    psi_ref.at[source(p, k)], psi_buf.at[p * targets_here + k],
                    psi_sem.at[p * targets_here + k],
                )
                for k in range(targets_here)
            ]
            copies.append((left, right, blocks))
            for copy in (*blocks, left, right):
                copy.start()
        own = pairs * targets_here
        own_copies = [
            pltpu.make_async_copy(psi_ref.at[first + k], psi_buf.at[own + k], psi_sem.at[own + k])
            for k in range(targets_here)
        ]
        for copy in own_copies:
            copy.start()
        row = lax.broadcasted_iota(jnp.int32, (block, block), 0)
        column = lax.broadcasted_iota(jnp.int32, (block, block), 1)
        farthest = jnp.maximum(row, column)
        totals = [jnp.zeros((block, block), jnp.float32) for _ in range(targets_here)]
        for p, (left, right, blocks) in enumerate(copies):
            for copy in (*blocks, left, right):
                copy.wait()
            for k in range(targets_here):
                size = sizes_ref[source(p, k)]
                psi = jnp.where(farthest < size, psi_buf[p * targets_here + k], 0)
                half = jnp.dot(
                    left_buf[p, k], psi, preferred_element_type=jnp.float32
                ).astype(jnp.bfloat16)
                totals[k] += lax.dot_general(
                    half, right_buf[p, k], (((1,), (1,)), ((), ())),
                    preferred_element_type=jnp.float32,
                )
        correlation = jnp.zeros((1, 1), jnp.float32)
        for copy in own_copies:
            copy.wait()
        for k in range(targets_here):
            size = sizes_ref[first + k]
            total = totals[k] * factor
            psi = jnp.where(farthest < size, psi_buf[own + k], 0).astype(jnp.float32)
            correlation += jnp.sum(psi * total, keepdims=True)
            out_ref[:, k * rows : (k + 1) * rows, :block] = total.reshape(
                block // rows, rows, block
            ).astype(jnp.bfloat16)
        high = correlation.astype(jnp.bfloat16).astype(jnp.float32)
        middle = (correlation - high).astype(jnp.bfloat16).astype(jnp.float32)
        low = correlation - high - middle
        lane = lax.broadcasted_iota(jnp.int32, (targets_here * rows, LANES), 1)
        up = lax.broadcasted_iota(jnp.int32, (targets_here * rows, LANES), 0)
        words = jnp.where(lane == 0, high, jnp.where(lane == 1, middle, jnp.where(lane == 2, low, 0.0)))
        words = jnp.where(up == 0, words, 0.0).astype(jnp.bfloat16)
        out_ref[:, :, block:] = jnp.broadcast_to(words[None], (block // rows, *words.shape))

    return body


def local(wavefunction, left_ops, right_ops, charge, block_sizes):
    sec_count, block, _ = wavefunction.shape
    pairs = left_ops.shape[0]
    ops_count = lax.axis_size("ops")
    sec_total = lax.axis_size("sec")
    sectors = block_sizes.shape[0]
    rows = block // ops_count
    operator_slot = lax.axis_index("ops")
    sec_place = lax.axis_index("sec")
    factor = float(pairs * ops_count) ** (-0.5)

    gathered = lax.all_gather(wavefunction, "sec", axis=0, tiled=True)
    vmem, smem, anywhere = pltpu.VMEM, pltpu.SMEM, pl.ANY
    count = pairs * sec_count + sec_count
    pieces = pl.pallas_call(
        sigma_kernel(pairs, sec_count, sectors, rows, factor),
        out_shape=jax.ShapeDtypeStruct((ops_count, sec_count * rows, block + LANES), jnp.bfloat16),
        in_specs=[pl.BlockSpec(memory_space=smem)] * 3 + [pl.BlockSpec(memory_space=anywhere)] * 3,
        out_specs=pl.BlockSpec(memory_space=vmem),
        scratch_shapes=[
            pltpu.VMEM((count, block, block), jnp.bfloat16),
            pltpu.VMEM(left_ops.shape, jnp.bfloat16),
            pltpu.VMEM(right_ops.shape, jnp.bfloat16),
            pltpu.SemaphoreType.DMA((count,)),
            pltpu.SemaphoreType.DMA((pairs,)),
            pltpu.SemaphoreType.DMA((pairs,)),
        ],
        compiler_params=pltpu.CompilerParams(vmem_limit_bytes=32 * 2**20),
        cost_estimate=pl.CostEstimate(
            flops=4 * pairs * sec_count * block**3, bytes_accessed=7 * 2**20, transcendentals=0
        ),
    )(sec_place.reshape(1), charge, block_sizes, gathered, left_ops, right_ops)
    received = lax.all_to_all(pieces, "ops", 0, 0)
    summed = jnp.sum(received.astype(jnp.float32), axis=0)

    positions = jnp.arange(block, dtype=jnp.int32)
    own_sizes = lax.dynamic_slice_in_dim(block_sizes, sec_place * sec_count, sec_count, 0)
    live = (positions[None, :] < own_sizes[:, None]).astype(jnp.float32)
    masked = wavefunction.astype(jnp.float32) * live[:, :, None] * live[:, None, :]
    norm_here = jnp.sum(masked * masked)
    correlation_here = jnp.sum(summed[:, block:])
    both = jnp.stack([jnp.full((LANES,), correlation_here), jnp.full((LANES,), norm_here)])
    both = jnp.broadcast_to(both[None], (sec_total, 2, LANES))
    both = jnp.sum(lax.all_to_all(both, "sec", 0, 0), axis=0)
    ritz_value = both[0, 0] / both[1, 0]

    row_live = lax.dynamic_slice_in_dim(live, operator_slot * rows, rows, 1)
    sigma = summed[:, :block].reshape(sec_count, rows, block)
    sigma = sigma * row_live[:, :, None] * live[:, None, :]
    own_rows = lax.dynamic_slice_in_dim(masked, operator_slot * rows, rows, 1)
    return (
        sigma.astype(jnp.bfloat16),
        (sigma - ritz_value * own_rows).astype(jnp.bfloat16),
    )


def solution(mesh):
    placed = (
        P("sec", None, None),
        P("ops", "sec", None, None),
        P("ops", "sec", None, None),
        P("ops"),
        P(),
    )
    return jax.shard_map(
        local,
        mesh=mesh,
        in_specs=placed,
        out_specs=(P("sec", "ops", None), P("sec", "ops", None)),
        check_vma=False,
    )
```

time: 342 us -> 126 us (0.37)
  waiting for transfers between devices: 204 us -> 74.9 us
  blocking collectives: 101 us -> 0 us
  starting transfers between devices: 0.08 us -> 15.7 us
  Pallas kernels: 0 us -> 7.58 us
  other arithmetic: 9.26 us -> 2.26 us
  matrix products: 4.34 us -> 0 us
    psum x1 -> x0, waiting for transfers between devices: 152 us -> none  [local(): summed = lax.psum(partial_sum, 'ops')]
    psum x1 -> x0, blocking collectives: 101 us -> none  [local(): lax.psum((jnp.sum(own_rows * sigma_block), jnp.sum(own_rows * own_rows)),...]
    all_to_all x0 -> x2, waiting for transfers between devices: none -> 20.4 us  [the longest x1 13.1 us: local(): received = lax.all_to_all(pieces, 'ops', 0, 0)]
    all_to_all x0 -> x2, starting transfers between devices: none -> 15.6 us  [the longest x1 9.27 us: local(): received = lax.all_to_all(pieces, 'ops', 0, 0)]
    gather x2 -> x0, local copies, waits for them, and re-layouts: 8.12 us -> none  [local(): selected_rows = jnp.take(masked, sources, axis=0)]
    pallas_call x0 -> x1, Pallas kernels: none -> 7.58 us  [local(): pl.pallas_call(sigma_kernel(pairs, sec_count, sectors, rows, factor), out...]
    unnamed x2 -> x14, local copies, waits for them, and re-layouts: 0.01 us -> 6.69 us
    dot_general x1 -> x0, matrix products: 4.34 us -> none  [local(): jnp.einsum('pkac,pkdc->kad', split_pieces, right_ops, preferred_element_t...]
  transfers between devices with their start and end apart: 2 -> 3, of which waited for: 2 -> 3; matrix products, arithmetic and copies ran while one was open for 1% -> 1% of each run, Pallas kernels for 0% -> 0%
where the time goes in v1:
time: 126 us; the launch traced here: 125 us
  waiting for transfers between devices  74.9 us (59%)
  starting transfers between devices  15.7 us (12%)
  between operations  15.4 us (12%)
  local copies, waits for them, and re-layouts  9.32 us (7%)
  Pallas kernels  7.58 us (6%)
  other arithmetic  2.26 us (2%)
    all_gather x1, waiting for transfers between devices, local(): gathered = lax.all_gather(wavefunction, 'sec', axis=0, tiled=True)  53.8 us
    all_to_all x1, waiting for transfers between devices, local(): received = lax.all_to_all(pieces, 'ops', 0, 0)  13.1 us
    all_to_all x1, starting transfers between devices, local(): received = lax.all_to_all(pieces, 'ops', 0, 0)  9.27 us
    pallas_call x1, Pallas kernels, local(): pl.pallas_call(sigma_kernel(pairs, sec_count, sectors, rows, factor), out...  7.58 us
    all_to_all x1, waiting for transfers between devices, local(): both = jnp.sum(lax.all_to_all(both, 'sec', 0, 0), axis=0)  7.26 us
    unnamed x14, local copies, waits for them, and re-layouts  6.69 us
    all_to_all x1, starting transfers between devices, local(): both = jnp.sum(lax.all_to_all(both, 'sec', 0, 0), axis=0)  6.35 us
  transfers between devices with their start and end apart: 3, of which 3 were waited for; matrix products, arithmetic and copies ran while one was open for 1% of the time, Pallas kernels for 0%

profile of v1, /device:TPU:1, one launch (start us, length us, event | category | flops | bytes accessed | tf_op | source)
XLA Modules:
  0.0 125.1 jit_solution(3684400533263124987)
XLA Ops:
  7.2 0.0 all-gather.2.cloned.1.call-start
  7.2 0.7 all-gather.2.cloned.1.call-update
  7.9 53.8 %all-gather.2.cloned.1.call-done.psi_ref = bf16[32,256,256]{2,1,0:T(8,128)(2,1)} async-done(((bf16[2,256,256]{2,1,0:T(8,128)(2,1)}), bf16[32,256,256]{2,1,0:T(8,128)(2,1)}) %all-gather.2.cloned.1.call-update) | async-done | bytes 4194320 | tf_op jit(solution)/shard_map/all_gather | solution.py:94
  61.7 0.0 copy-start
  61.7 2.2 %copy-done = bf16[32,256,256]{2,1,0:T(8,128)(2,1)S(1)} copy-done((bf16[32,256,256]{2,1,0:T(8,128)(2,1)S(1)}, bf16[32,256,256]{2,1,0:T(8,128)(2,1)}, u32[]{:S(2)}) %copy-start) | copy-done | bytes 4194328
  63.9 0.0 copy-start.1
  63.9 1.6 %copy-done.1 = bf16[8,2,256,256]{3,2,1,0:T(8,128)(2,1)S(1)} copy-done((bf16[8,2,256,256]{3,2,1,0:T(8,128)(2,1)S(1)}, bf16[8,2,256,256]{3,2,1,0:T(8,128)(2,1)}, u32[]{:S(2)}) %copy-start.1) | copy-done | bytes 2097176
  65.5 0.0 copy-start.2
  65.5 1.6 %copy-done.2 = bf16[8,2,256,256]{3,2,1,0:T(8,128)(2,1)S(1)} copy-done((bf16[8,2,256,256]{3,2,1,0:T(8,128)(2,1)S(1)}, bf16[8,2,256,256]{3,2,1,0:T(8,128)(2,1)}, u32[]{:S(2)}) %copy-start.2) | copy-done | bytes 2097176
  67.1 0.0 copy-start.3
  67.1 0.7 copy-done.3
  67.8 0.0 copy-start.4
  67.8 0.7 copy-done.4
  68.4 0.0 copy-start.5
  68.4 0.0 copy-start.6
  68.4 7.6 %shard_map.68 = bf16[32,16,384]{2,1,0:T(8,128)(2,1)} custom-call(s32[1]{0:T(128)} %bitcast.sec_ref, s32[8]{0:T(128)S(1)} %copy-done.3, s32[32]{0:T(128)S(1)} %copy-done.4, bf16[32,256,256]{2,1,0:T(8,128)(2,1)S(1)} %copy-done, bf16[8,2,256,256]{3,2,1,0:T(8,128)(2,1)S(1)} %copy-done.1, bf16[8,2,256,256]{3,2,1,0:T(8,128)(2,1)S(1)} %copy-done.2), custom_call_target="tpu_custom_call" | custom-call | flops 1073741824 | bytes 7340032 | tf_op jit(solution)/shard_map/pallas_call | solution.py:97
  76.0 9.3 %all-to-all-start = ((bf16[32,16,384]{2,1,0:T(8,128)(2,1)}), bf16[32,16,384]{2,1,0:T(8,128)(2,1)S(1)}, u32[]{:S(2)}, u32[]{:S(2)}) async-start(bf16[32,16,384]{2,1,0:T(8,128)(2,1)} %shard_map.68), calls=%async_computation | async-start | bytes 786432 | tf_op jit(solution)/shard_map/all_to_all | solution.py:115
  85.3 0.0 copy-done.5
  85.3 0.1 dynamic_slice.9
  85.4 0.1 compare_convert_fusion
  85.5 0.0 copy-done.6
  85.5 0.8 multiply_reduce_fusion
  86.3 13.1 %all-to-all-done = bf16[32,16,384]{2,1,0:T(8,128)(2,1)S(1)} async-done(((bf16[32,16,384]{2,1,0:T(8,128)(2,1)}), bf16[32,16,384]{2,1,0:T(8,128)(2,1)S(1)}, u32[]{:S(2)}, u32[]{:S(2)}) %all-to-all-start) | async-done | bytes 393248 | tf_op jit(solution)/shard_map/all_to_all | solution.py:115
  99.4 0.1 convert_reduce_fusion
  99.5 0.6 slice_reduce_fusion
  100.1 1.3 %stack.3 = f32[2]{0:T(128)S(1)} pad(f32[1]{0:T(128)} %bitcast.2, f32[]{:T(128)} %get-tuple-element.2), padding=0_1 | pad | bytes 16 | tf_op jit(solution)/shard_map/stack | solution.py:124
  101.4 0.7 broadcast_in_dim.2
  102.0 6.4 %all-to-all-start.1 = ((f32[16,2,128]{2,1,0:T(2,128)}), f32[16,2,128]{2,1,0:T(2,128)S(1)}, u32[]{:S(2)}, u32[]{:S(2)}) async-start(f32[16,2,128]{2,1,0:T(2,128)} %broadcast_in_dim.2), calls=%async_computation.1 | async-start | bytes 32768 | tf_op jit(solution)/shard_map/all_to_all | solution.py:126
  108.4 0.1 constant_dynamic-slice_fusion
  108.5 7.3 %all-to-all-done.1 = f32[16,2,128]{2,1,0:T(2,128)S(1)} async-done(((f32[16,2,128]{2,1,0:T(2,128)}), f32[16,2,128]{2,1,0:T(2,128)S(1)}, u32[]{:S(2)}, u32[]{:S(2)}) %all-to-all-start.1) | async-done | bytes 16416 | tf_op jit(solution)/shard_map/all_to_all | solution.py:126
  115.8 0.5 fusion.3
  117.6 0.7 subtract_convert_fusion
  (1 shorter events, 0.0 us)
Async XLA Ops:
  7.2 54.6 %all-gather.2.cloned.1.call-start = ((), (), s32[]{:S(2)}) async-start(), calls=%async_computation.2 | async-start | bytes 4456448 | tf_op jit(solution)/shard_map/all_gather | solution.py:94
  61.7 2.2 %copy-start = (bf16[32,256,256]{2,1,0:T(8,128)(2,1)S(1)}, bf16[32,256,256]{2,1,0:T(8,128)(2,1)}, u32[]{:S(2)}) copy-start(bf16[32,256,256]{2,1,0:T(8,128)(2,1)} %all-gather.2.cloned.1.call-done.psi_ref) | copy-start | bytes 12582916
  63.9 1.6 %copy-start.1 = (bf16[8,2,256,256]{3,2,1,0:T(8,128)(2,1)S(1)}, bf16[8,2,256,256]{3,2,1,0:T(8,128)(2,1)}, u32[]{:S(2)}) copy-start(bf16[8,2,256,256]{3,2,1,0:T(8,128)(2,1)} %left_ref.1) | copy-start | bytes 6291460
  65.5 1.6 %copy-start.2 = (bf16[8,2,256,256]{3,2,1,0:T(8,128)(2,1)S(1)}, bf16[8,2,256,256]{3,2,1,0:T(8,128)(2,1)}, u32[]{:S(2)}) copy-start(bf16[8,2,256,256]{3,2,1,0:T(8,128)(2,1)} %right_ref.1) | copy-start | bytes 6291460
  67.1 0.7 copy-start.3
  67.8 0.7 copy-start.4
  68.4 16.9 %copy-start.5 = (s32[32]{0:T(128)S(1)}, s32[32]{0:T(128)}, u32[]{:S(2)}) copy-start(s32[32]{0:T(128)} %sizes_ref.1) | copy-start | bytes 388
  68.4 17.0 %copy-start.6 = (bf16[2,256,256]{2,1,0:T(8,128)(2,1)S(1)}, bf16[2,256,256]{2,1,0:T(8,128)(2,1)}, u32[]{:S(2)}) copy-start(bf16[2,256,256]{2,1,0:T(8,128)(2,1)} %param.5) | copy-start | bytes 786436
  76.0 23.4 %all-to-all-start = ((bf16[32,16,384]{2,1,0:T(8,128)(2,1)}), bf16[32,16,384]{2,1,0:T(8,128)(2,1)S(1)}, u32[]{:S(2)}, u32[]{:S(2)}) async-start(bf16[32,16,384]{2,1,0:T(8,128)(2,1)} %shard_map.68), calls=%async_computation | async-start | bytes 786432 | tf_op jit(solution)/shard_map/all_to_all | solution.py:115
  102.0 13.7 %all-to-all-start.1 = ((f32[16,2,128]{2,1,0:T(2,128)}), f32[16,2,128]{2,1,0:T(2,128)S(1)}, u32[]{:S(2)}, u32[]{:S(2)}) async-start(f32[16,2,128]{2,1,0:T(2,128)} %broadcast_in_dim.2), calls=%async_computation.1 | async-start | bytes 32768 | tf_op jit(solution)/shard_map/all_to_all | solution.py:126
Sparse Core Ops, SparseCore 0:
  10.1 51.5 all-gather.1

commit v2 on v0

v2 whole, which is shorter than its diff:
```python
import jax
import jax.numpy as jnp
from jax import lax
from jax.experimental import pallas as pl
from jax.experimental.pallas import tpu as pltpu
from jax.sharding import PartitionSpec as P

LANES = 128
SUBLANES = 8
X_SIZE = 4
COLOURS = 4
VMEM_LIMIT = 56 * 2**20


def sigma_kernel(pairs, here, sectors, rows, factor):
    def body(
        place_ref, charge_ref, sizes_ref, psi_ref, near_ref, far_ref, near_other_ref, far_other_ref,
        left_ref, right_ref, out_ref, norm_ref, own_buf, psi_buf, left_buf, right_buf, half_buf,
        own_sem, psi_sem, left_sem, right_sem,
    ):
        sec, core, colour = place_ref[0], place_ref[1], place_ref[2]
        first = sec * here
        block = left_buf.shape[-1]
        quarter = block // COLOURS

        def fetch(p, k):
            source = lax.rem(first + k + charge_ref[p], sectors)
            place = lax.div(source, 2 * here) * here + lax.rem(source, here)
            other = lax.rem(lax.div(source, here), 2) != core
            slot = p * here + k

            def start(near, far):
                def copy(src, relative):
                    at = pl.multiple_of(lax.rem(colour + relative, COLOURS) * quarter, quarter)
                    pltpu.make_async_copy(
                        src, psi_buf.at[slot, pl.ds(at, quarter)], psi_sem.at[slot]
                    ).start()

                copy(near.at[place], 0)
                copy(far.at[place, pl.ds(0, quarter)], 1)
                copy(far.at[place, pl.ds(quarter, quarter)], 3)
                copy(far.at[place, pl.ds(2 * quarter, quarter)], 2)

            pl.when(other)(lambda: start(near_other_ref, far_other_ref))
            pl.when(jnp.logical_not(other))(lambda: start(near_ref, far_ref))

        own_copy = pltpu.make_async_copy(psi_ref, own_buf, own_sem)
        lefts = [
            pltpu.make_async_copy(left_ref.at[p], left_buf.at[p], left_sem.at[p])
            for p in range(pairs)
        ]
        rights = [
            pltpu.make_async_copy(
                right_ref.at[p, k], right_buf.at[k, :, pl.ds(p * block, block)],
                right_sem.at[p * here + k],
            )
            for p in range(pairs) for k in range(here)
        ]
        for p in range(pairs):
            lefts[p].start()
            for k in range(here):
                fetch(p, k)
        for copy in rights:
            copy.start()
        own_copy.start()
        row = lax.broadcasted_iota(jnp.int32, (block, block), 0)
        column = lax.broadcasted_iota(jnp.int32, (block, block), 1)
        farthest = jnp.maximum(row, column)
        for p in range(pairs):
            lefts[p].wait()
            for k in range(here):
                slot = p * here + k
                pltpu.make_async_copy(psi_buf.at[slot], psi_buf.at[slot], psi_sem.at[slot]).wait()
            for k in range(here):
                half_buf[k, :, p * block : (p + 1) * block] = jnp.dot(
                    left_buf[p, k], psi_buf[p * here + k], preferred_element_type=jnp.float32
                ).astype(jnp.bfloat16)
        for copy in rights:
            copy.wait()
        own_copy.wait()
        correlation = jnp.zeros((1, 1), jnp.float32)
        norm = jnp.zeros((1, 1), jnp.float32)
        for k in range(here):
            total = factor * lax.dot_general(
                half_buf[k], right_buf[k], (((1,), (1,)), ((), ())),
                preferred_element_type=jnp.float32,
            )
            psi = jnp.where(farthest < sizes_ref[first + k], own_buf[k], 0).astype(jnp.float32)
            correlation += jnp.sum(psi * total, keepdims=True)
            norm += jnp.sum(psi * psi, keepdims=True)
            out_ref[:, k * rows : (k + 1) * rows, :block] = total.reshape(
                block // rows, rows, block
            ).astype(jnp.bfloat16)
        high = correlation.astype(jnp.bfloat16).astype(jnp.float32)
        middle = (correlation - high).astype(jnp.bfloat16).astype(jnp.float32)
        low = correlation - high - middle
        lane = lax.broadcasted_iota(jnp.int32, (here * rows, LANES), 1)
        up = lax.broadcasted_iota(jnp.int32, (here * rows, LANES), 0)
        words = jnp.where(
            lane == 0, high, jnp.where(lane == 1, middle, jnp.where(lane == 2, low, 0.0))
        )
        words = jnp.where(up == 0, words, 0.0).astype(jnp.bfloat16)
        out_ref[:, :, block:] = jnp.broadcast_to(words[None], (block // rows, *words.shape))
        norm_ref[...] = jnp.broadcast_to(norm, norm_ref.shape)

    return body


def live_of(place_ref, sizes_ref, here, rows, block, k):
    size = sizes_ref[place_ref[0] * here + k]
    row = lax.broadcasted_iota(jnp.int32, (rows, block), 0) + place_ref[3] * rows
    column = lax.broadcasted_iota(jnp.int32, (rows, block), 1)
    return jnp.maximum(row, column) < size


def sum_kernel(here, rows, block):
    def body(place_ref, sizes_ref, received_ref, norm_ref, sigma_ref, wide_ref, both_ref):
        summed = jnp.sum(received_ref[...].astype(jnp.float32), axis=0)
        for k in range(here):
            part = summed[k * rows : (k + 1) * rows, :block]
            part = jnp.where(live_of(place_ref, sizes_ref, here, rows, block, k), part, 0.0)
            wide_ref[k] = part
            sigma_ref[k] = part.astype(jnp.bfloat16)
        correlation = jnp.sum(summed[:, block:], keepdims=True)
        up = lax.broadcasted_iota(jnp.int32, (SUBLANES, LANES), 0)
        both = jnp.where(up == 0, correlation, norm_ref[...])
        both_ref[...] = jnp.broadcast_to(both[None], both_ref.shape)

    return body


def residual_kernel(here, rows, block):
    def body(place_ref, sizes_ref, both_ref, wide_ref, own_ref, out_ref):
        both = jnp.sum(both_ref[...], axis=0)
        ritz_value = both[0:1, 0:1] / both[1:2, 0:1]
        for k in range(here):
            own = own_ref[k].astype(jnp.float32)
            own = jnp.where(live_of(place_ref, sizes_ref, here, rows, block, k), own, 0.0)
            out_ref[k] = (wide_ref[k] - ritz_value * own).astype(jnp.bfloat16)

    return body


def local(wavefunction, left_ops, right_ops, charge, block_sizes):
    here, block, _ = wavefunction.shape
    pairs = left_ops.shape[0]
    ops_count = lax.axis_size("ops")
    sec_total = lax.axis_size("sec")
    sectors = block_sizes.shape[0]
    rows = block // ops_count
    quarter = block // COLOURS
    operator_slot = lax.axis_index("ops")
    sec_place = lax.axis_index("sec")
    factor = float(pairs * ops_count) ** (-0.5)
    chips_z = sec_total // 2
    y_size = ops_count // X_SIZE
    colour = lax.rem(operator_slot % X_SIZE + 2 * (operator_slot // X_SIZE), COLOURS)
    place = jnp.stack([sec_place, sec_place % 2, colour, operator_slot])

    positions = jnp.arange(block, dtype=jnp.int32)
    own_sizes = lax.dynamic_slice_in_dim(block_sizes, sec_place * here, here, 0)
    live = positions[None, :] < own_sizes[:, None]
    own_quarter = lax.dynamic_slice_in_dim(wavefunction, colour * quarter, quarter, 1)
    row_live = lax.dynamic_slice_in_dim(live, colour * quarter, quarter, 1)
    own_quarter = jnp.where(row_live[:, :, None] & live[:, None, :], own_quarter, 0)
    spread = jnp.broadcast_to(own_quarter[None], (chips_z, *own_quarter.shape))
    same_core = [[2 * z + core for z in range(chips_z)] for core in range(2)]
    near = lax.all_to_all(spread, "sec", 0, 0, axis_index_groups=same_core)
    near = near.reshape(chips_z * here, quarter, block)

    def from_x(step):
        return [(y * X_SIZE + (x + step) % X_SIZE, y * X_SIZE + x)
                for y in range(y_size) for x in range(X_SIZE)]

    def from_y(step):
        return [((y + step) % y_size * X_SIZE + x, y * X_SIZE + x)
                for y in range(y_size) for x in range(X_SIZE)]

    swap = [(s, s ^ 1) for s in range(sec_total)]
    x_next = lax.ppermute(near, "ops", from_x(1))
    x_last = lax.ppermute(near, "ops", from_x(-1))
    y_next = lax.ppermute(near[:, : quarter // 2], "ops", from_y(1))
    y_last = lax.ppermute(near[:, quarter // 2 :], "ops", from_y(-1))
    near_other = lax.ppermute(near, "sec", swap)
    far = jnp.concatenate([x_next, x_last, y_next, y_last], axis=1)
    far_other = lax.ppermute(far, "sec", swap)

    smem = pl.BlockSpec(memory_space=pltpu.SMEM)
    vmem = pl.BlockSpec(memory_space=pltpu.VMEM)
    anywhere = pl.BlockSpec(memory_space=pl.ANY)
    count = pairs * here
    pieces, norm = pl.pallas_call(
        sigma_kernel(pairs, here, sectors, rows, factor),
        out_shape=(
            jax.ShapeDtypeStruct((ops_count, here * rows, block + LANES), jnp.bfloat16),
            jax.ShapeDtypeStruct((SUBLANES, LANES), jnp.float32),
        ),
        in_specs=[smem] * 3 + [anywhere] * 7,
        out_specs=(vmem, vmem),
        scratch_shapes=[
            pltpu.VMEM((here, block, block), jnp.bfloat16),
            pltpu.VMEM((count, block, block), jnp.bfloat16),
            pltpu.VMEM(left_ops.shape, jnp.bfloat16),
            pltpu.VMEM((here, block, pairs * block), jnp.bfloat16),
            pltpu.VMEM((here, block, pairs * block), jnp.bfloat16),
            pltpu.SemaphoreType.DMA,
            pltpu.SemaphoreType.DMA((count,)),
            pltpu.SemaphoreType.DMA((pairs,)),
            pltpu.SemaphoreType.DMA((count,)),
        ],
        compiler_params=pltpu.CompilerParams(vmem_limit_bytes=VMEM_LIMIT),
        cost_estimate=pl.CostEstimate(
            flops=4 * count * block**3, bytes_accessed=7 * 2**20, transcendentals=0
        ),
    )(place, charge, block_sizes, wavefunction, near, far, near_other, far_other, left_ops, right_ops)
    received = lax.all_to_all(pieces, "ops", 0, 0)

    sigma, wide, both = pl.pallas_call(
        sum_kernel(here, rows, block),
        out_shape=(
            jax.ShapeDtypeStruct((here, rows, block), jnp.bfloat16),
            jax.ShapeDtypeStruct((here, rows, block), jnp.float32),
            jax.ShapeDtypeStruct((sec_total, SUBLANES, LANES), jnp.float32),
        ),
        in_specs=[smem, smem, vmem, vmem],
        out_specs=(vmem, vmem, vmem),
    )(place, block_sizes, received, norm)
    both = lax.all_to_all(both, "sec", 0, 0)
    own_rows = lax.dynamic_slice_in_dim(wavefunction, operator_slot * rows, rows, 1)
    residual = pl.pallas_call(
        residual_kernel(here, rows, block),
        out_shape=jax.ShapeDtypeStruct((here, rows, block), jnp.bfloat16),
        in_specs=[smem, smem, vmem, vmem, vmem],
        out_specs=vmem,
    )(place, block_sizes, both, wide, own_rows)
    return sigma, residual


def solution(mesh):
    placed = (
        P("sec", None, None),
        P("ops", "sec", None, None),
        P("ops", "sec", None, None),
        P("ops"),
        P(),
    )
    return jax.shard_map(
        local,
        mesh=mesh,
        in_specs=placed,
        out_specs=(P("sec", "ops", None), P("sec", "ops", None)),
        check_vma=False,
    )
```

time: 342 us -> 105 us (0.31)
  waiting for transfers between devices: 204 us -> 14.3 us
  blocking collectives: 101 us -> 47.7 us
  starting transfers between devices: 0.08 us -> 26.5 us
  between operations: 15.4 us -> 0.83 us
  Pallas kernels: 0 us -> 9.96 us
  other arithmetic: 9.26 us -> 1.66 us
  local copies, waits for them, and re-layouts: 8.21 us -> 3.69 us
  matrix products: 4.34 us -> 0 us
    psum x1 -> x0, waiting for transfers between devices: 152 us -> none  [local(): summed = lax.psum(partial_sum, 'ops')]
    psum x1 -> x0, blocking collectives: 101 us -> none  [local(): lax.psum((jnp.sum(own_rows * sigma_block), jnp.sum(own_rows * own_rows)),...]
    all_gather x1 -> x0, waiting for transfers between devices: 51.5 us -> none  [local(): gathered = lax.all_gather(wavefunction, 'sec', axis=0, tiled=True)]
    all_to_all x0 -> x2, blocking collectives: none -> 47.7 us  [the longest x1 26.7 us: local(): near = lax.all_to_all(spread, 'sec', 0, 0, axis_index_groups=same_core)]
    ppermute x0 -> x6, starting transfers between devices: none -> 21 us  [the longest x1 5.78 us: local(): far_other = lax.ppermute(far, 'sec', swap)]
    pallas_call x0 -> x3, Pallas kernels: none -> 9.96 us  [the longest x1 6.61 us: local(): pl.pallas_call(sigma_kernel(pairs, here, sectors, rows, factor), out_shap...]
    gather x2 -> x0, local copies, waits for them, and re-layouts: 8.12 us -> none  [local(): selected_rows = jnp.take(masked, sources, axis=0)]
    ppermute x0 -> x6, waiting for transfers between devices: none -> 7.77 us  [the longest x1 4.72 us: local(): x_last = lax.ppermute(near, 'ops', from_x(-1))]
  transfers between devices with their start and end apart: 2 -> 7, of which waited for: 2 -> 4; matrix products, arithmetic and copies ran while one was open for 1% -> 2% of each run, Pallas kernels for 0% -> 0%
where the time goes in v2:
time: 105 us
  blocking collectives  47.7 us (45%)
  starting transfers between devices  26.5 us (25%)
  waiting for transfers between devices  14.3 us (14%)
  Pallas kernels  9.96 us (9%)
  local copies, waits for them, and re-layouts  3.69 us (4%)
  other arithmetic  1.66 us (2%)
    all_to_all x1, blocking collectives, local(): near = lax.all_to_all(spread, 'sec', 0, 0, axis_index_groups=same_core)  26.7 us
    all_to_all x1, blocking collectives, local(): received = lax.all_to_all(pieces, 'ops', 0, 0)  21 us
    pallas_call x1, Pallas kernels, local(): pl.pallas_call(sigma_kernel(pairs, here, sectors, rows, factor), out_shap...  6.61 us
    all_to_all x1, waiting for transfers between devices, local(): both = lax.all_to_all(both, 'sec', 0, 0)  6.55 us
    ppermute x1, starting transfers between devices, local(): far_other = lax.ppermute(far, 'sec', swap)  5.78 us
    all_to_all x1, starting transfers between devices, local(): both = lax.all_to_all(both, 'sec', 0, 0)  5.53 us
    ppermute x1, starting transfers between devices, local(): y_next = lax.ppermute(near[:, :quarter // 2], 'ops', from_y(1))  5.1 us
    ppermute x1, waiting for transfers between devices, local(): x_last = lax.ppermute(near, 'ops', from_x(-1))  4.72 us
  transfers between devices with their start and end apart: 7, of which 4 were waited for; matrix products, arithmetic and copies ran while one was open for 2% of the time, Pallas kernels for 0%

profile of v2, /device:TPU:1, one launch (start us, length us, event | category | flops | bytes accessed | tf_op | source)
XLA Modules:
  0.0 104.7 jit_solution(15110744889640016101)
XLA Ops:
  0.7 0.7 dynamic_slice.12
  1.4 0.1 iota_compare_fusion
  1.5 0.1 constant_dynamic-slice_fusion.1
  1.6 0.9 and_select_fusion
  2.5 26.7 %all_to_all.15 = bf16[8,2,64,256]{3,2,1,0:T(8,128)(2,1)S(1)} all-to-all(bf16[8,2,64,256]{3,2,1,0:T(8,128)(2,1)S(1)} %broadcast_in_dim.7), channel_id=1, replica_groups={{0,2,4,6,8,10,12,14},{1,3,5,7,9,11,13,15},{16,18,20,22,24,26,28,30},{17..., dimensions={0} | all-to-all | bytes 1048576 | tf_op jit(solution)/shard_map/all_to_all | solution.py:168
  29.2 0.0 copy-start
  29.2 4.4 %collective-permute-start = (bf16[16,64,256]{2,1,0:T(8,128)(2,1)S(1)}, bf16[16,64,256]{2,1,0:T(8,128)(2,1)S(1)}, u32[]{:S(2)}, u32[]{:S(2)}) collective-permute-start(bf16[16,64,256]{2,1,0:T(8,128)(2,1)S(1)} %bitcast.5), channel_id=1, source_target_pairs={{16,0},{32,16},{48,32},{0,48},{80,64},{96,80},{112,96},{64,112},{1... | collective-permute-start | bytes 1572872 | tf_op jit(solution)/shard_map/ppermute | solution.py:180
  33.6 1.9 %collective-permute-start.1 = (bf16[16,64,256]{2,1,0:T(8,128)(2,1)S(1)}, bf16[16,64,256]{2,1,0:T(8,128)(2,1)S(1)}, u32[]{:S(2)}, u32[]{:S(2)}) collective-permute-start(bf16[16,64,256]{2,1,0:T(8,128)(2,1)S(1)} %bitcast.6), channel_id=1, source_target_pairs={{48,0},{0,16},{16,32},{32,48},{112,64},{64,80},{80,96},{96,112},{1... | collective-permute-start | bytes 1572872 | tf_op jit(solution)/shard_map/ppermute | solution.py:181
  35.5 5.1 %collective-permute-start.2 = (bf16[16,32,256]{2,1,0:T(8,128)(2,1)S(1)}, bf16[16,32,256]{2,1,0:T(8,128)(2,1)S(1)}, u32[]{:S(2)}, u32[]{:S(2)}) collective-permute-start(bf16[16,32,256]{2,1,0:T(8,128)(2,1)S(1)} %get-tuple-element.13), channel_id=1, source_target_pairs={{64,0},{80,16},{96,32},{112,48},{128,64},{144,80},{160,96},{176,11... | collective-permute-start | bytes 786440 | tf_op jit(solution)/shard_map/ppermute | solution.py:182
  40.7 1.9 %collective-permute-start.3 = (bf16[16,32,256]{2,1,0:T(8,128)(2,1)S(1)}, bf16[16,32,256]{2,1,0:T(8,128)(2,1)S(1)}, u32[]{:S(2)}, u32[]{:S(2)}) collective-permute-start(bf16[16,32,256]{2,1,0:T(8,128)(2,1)S(1)} %get-tuple-element.12), channel_id=1, source_target_pairs={{448,0},{464,16},{480,32},{496,48},{0,64},{16,80},{32,96},{48,112}... | collective-permute-start | bytes 786440 | tf_op jit(solution)/shard_map/ppermute | solution.py:183
  42.6 0.0 collective-permute-done
  42.6 4.7 %collective-permute-done.1 = bf16[16,64,256]{2,1,0:T(8,128)(2,1)S(1)} collective-permute-done((bf16[16,64,256]{2,1,0:T(8,128)(2,1)S(1)}, bf16[16,64,256]{2,1,0:T(8,128)(2,1)S(1)}, u32[]{:S(2)}, u32[]{:S(2)}) %collective-permute-start.1) | collective-permute-done | bytes 524320 | tf_op jit(solution)/shard_map/ppermute | solution.py:181
  47.4 0.0 collective-permute-done.2
  47.4 1.8 %collective-permute-done.3 = bf16[16,32,256]{2,1,0:T(8,128)(2,1)S(1)} collective-permute-done((bf16[16,32,256]{2,1,0:T(8,128)(2,1)S(1)}, bf16[16,32,256]{2,1,0:T(8,128)(2,1)S(1)}, u32[]{:S(2)}, u32[]{:S(2)}) %collective-permute-start.3) | collective-permute-done | bytes 262176 | tf_op jit(solution)/shard_map/ppermute | solution.py:183
  49.3 0.0 copy-start.1
  49.3 5.8 %collective-permute-start.5 = (bf16[16,192,256]{2,1,0:T(8,128)(2,1)S(1)}, bf16[16,192,256]{2,1,0:T(8,128)(2,1)}, u32[]{:S(2)}, u32[]{:S(2)}) collective-permute-start(bf16[16,192,256]{2,1,0:T(8,128)(2,1)S(1)} %constant_dynamic-update-slice_fusion.far_ref), channel_id=1, source_target_pairs={{0,1},{1,0},{2,3},{3,2},{4,5},{5,4},{6,7},{7,6},{8,9},{9,8},{10,11... | collective-permute-start | bytes 4718600 | tf_op jit(solution)/shard_map/ppermute | solution.py:186
  55.1 0.0 copy-done
  55.1 1.9 %collective-permute-start.4 = (bf16[16,64,256]{2,1,0:T(8,128)(2,1)S(1)}, bf16[16,64,256]{2,1,0:T(8,128)(2,1)S(1)}, u32[]{:S(2)}, u32[]{:S(2)}) collective-permute-start(bf16[16,64,256]{2,1,0:T(8,128)(2,1)S(1)} %bitcast.8), channel_id=1, source_target_pairs={{0,1},{1,0},{2,3},{3,2},{4,5},{5,4},{6,7},{7,6},{8,9},{9,8},{10,11... | collective-permute-start | bytes 1572872 | tf_op jit(solution)/shard_map/ppermute | solution.py:184
  57.0 0.7 pad_add_fusion.place_ref
  57.7 1.2 %collective-permute-done.4.near_other_ref = bf16[16,64,256]{2,1,0:T(8,128)(2,1)S(1)} collective-permute-done((bf16[16,64,256]{2,1,0:T(8,128)(2,1)S(1)}, bf16[16,64,256]{2,1,0:T(8,128)(2,1)S(1)}, u32[]{:S(2)}, u32[]{:S(2)}) %collective-permute-start.4) | collective-permute-done | bytes 524320 | tf_op jit(solution)/shard_map/ppermute | solution.py:184
  58.9 0.0 copy-start.2
  58.9 0.0 collective-permute-done.5.far_other_ref
  58.9 0.0 copy-done.1
  58.9 0.8 copy-done.2
  59.7 6.6 %shard_map.68 = (bf16[32,16,384]{2,1,0:T(8,128)(2,1)}, f32[8,128]{1,0:T(8,128)}) custom-call(s32[4]{0:T(128)} %pad_add_fusion.place_ref, s32[8]{0:T(128)} %charge_ref.1, s32[32]{0:T(128)} %sizes_ref.5, bf16[2,256,256]{2,1,0:T(8,128)(2,1)} %psi_ref.1, bf16[16,64,256]{2,1,0:T(8,128)(2,1)} %bitcast.9, bf16[16,192,256]{2,1,0:T(8,128)(2,1)} %copy-done.1, ...), custom_call_target="tpu_custom_call" | custom-call | flops 1073741824 | bytes 7340032 | tf_op jit(solution)/shard_map/pallas_call | solution.py:192
  66.3 21.0 %all_to_all.16.received_ref = bf16[32,16,384]{2,1,0:T(8,128)(2,1)} all-to-all(bf16[32,16,384]{2,1,0:T(8,128)(2,1)} %get-tuple-element.7), channel_id=1, replica_groups=mesh['ops'=32,'sec'=16] {'ops'}, dimensions={0} | all-to-all | bytes 786432 | tf_op jit(solution)/shard_map/all_to_all | solution.py:216
  87.3 1.8 %shard_map.69 = (bf16[2,8,256]{2,1,0:T(8,128)(2,1)}, f32[2,8,256]{2,1,0:T(8,128)}, f32[16,8,128]{2,1,0:T(8,128)}) custom-call(s32[4]{0:T(128)} %pad_add_fusion.place_ref, s32[32]{0:T(128)} %sizes_ref.5, bf16[32,16,384]{2,1,0:T(8,128)(2,1)} %all_to_all.16.received_ref, f32[8,128]{1,0:T(8,128)} %get-tuple-element.8.norm_ref), custom_call_target="tpu_custom_call" | custom-call | tf_op jit(solution)/shard_map/pallas_call | solution.py:218
  89.1 5.5 %all-to-all-start.2 = ((f32[16,8,128]{2,1,0:T(8,128)}), f32[16,8,128]{2,1,0:T(8,128)S(1)}, u32[]{:S(2)}, u32[]{:S(2)}) async-start(f32[16,8,128]{2,1,0:T(8,128)} %get-tuple-element.10), calls=%async_computation.2 | async-start | bytes 131072 | tf_op jit(solution)/shard_map/all_to_all | solution.py:228
  94.7 1.3 %constant_dynamic-slice_fusion.own_ref = bf16[2,8,256]{2,1,0:T(8,128)(2,1)} fusion(bf16[2,256,256]{2,1,0:T(8,128)(2,1)} %psi_ref.1, s32[]{:T(128)S(6)} %select_n.35), kind=kLoop, calls=%fused_computation.6 | loop fusion | bytes 16388 | tf_op jit(solution)/shard_map/dynamic_slice | solution.py:229
  96.0 6.5 %all-to-all-done.2.both_ref = f32[16,8,128]{2,1,0:T(8,128)S(1)} async-done(((f32[16,8,128]{2,1,0:T(8,128)}), f32[16,8,128]{2,1,0:T(8,128)S(1)}, u32[]{:S(2)}, u32[]{:S(2)}) %all-to-all-start.2) | async-done | bytes 65568 | tf_op jit(solution)/shard_map/all_to_all | solution.py:228
  102.5 0.0 copy-start.3
  102.5 0.6 copy-done.3
  103.1 1.5 %shard_map.70 = bf16[2,8,256]{2,1,0:T(8,128)(2,1)} custom-call(s32[4]{0:T(128)} %pad_add_fusion.place_ref, s32[32]{0:T(128)} %sizes_ref.5, f32[16,8,128]{2,1,0:T(8,128)} %copy-done.3, f32[2,8,256]{2,1,0:T(8,128)} %get-tuple-element.11.wide_ref, bf16[2,8,256]{2,1,0:T(8,128)(2,1)} %constant_dynamic-slice_fusion.own_ref), custom_call_target="tpu_custom_call" | custom-call | tf_op jit(solution)/shard_map/pallas_call | solution.py:230
  (6 shorter events, 0.2 us)
Async XLA Ops:
  29.2 25.9 %copy-start = (bf16[8,2,64,256]{3,2,1,0:T(8,128)(2,1)}, bf16[8,2,64,256]{3,2,1,0:T(8,128)(2,1)S(1)}, u32[]{:S(2)}) copy-start(bf16[8,2,64,256]{3,2,1,0:T(8,128)(2,1)S(1)} %all_to_all.15) | copy-start | bytes 1572868
  29.2 13.4 %collective-permute-start = (bf16[16,64,256]{2,1,0:T(8,128)(2,1)S(1)}, bf16[16,64,256]{2,1,0:T(8,128)(2,1)S(1)}, u32[]{:S(2)}, u32[]{:S(2)}) collective-permute-start(bf16[16,64,256]{2,1,0:T(8,128)(2,1)S(1)} %bitcast.5), channel_id=1, source_target_pairs={{16,0},{32,16},{48,32},{0,48},{80,64},{96,80},{112,96},{64,112},{1... | collective-permute-start | bytes 1572872 | tf_op jit(solution)/shard_map/ppermute | solution.py:180
  33.6 13.8 %collective-permute-start.1 = (bf16[16,64,256]{2,1,0:T(8,128)(2,1)S(1)}, bf16[16,64,256]{2,1,0:T(8,128)(2,1)S(1)}, u32[]{:S(2)}, u32[]{:S(2)}) collective-permute-start(bf16[16,64,256]{2,1,0:T(8,128)(2,1)S(1)} %bitcast.6), channel_id=1, source_target_pairs={{48,0},{0,16},{16,32},{32,48},{112,64},{64,80},{80,96},{96,112},{1... | collective-permute-start | bytes 1572872 | tf_op jit(solution)/shard_map/ppermute | solution.py:181
  35.5 11.9 %collective-permute-start.2 = (bf16[16,32,256]{2,1,0:T(8,128)(2,1)S(1)}, bf16[16,32,256]{2,1,0:T(8,128)(2,1)S(1)}, u32[]{:S(2)}, u32[]{:S(2)}) collective-permute-start(bf16[16,32,256]{2,1,0:T(8,128)(2,1)S(1)} %get-tuple-element.13), channel_id=1, source_target_pairs={{64,0},{80,16},{96,32},{112,48},{128,64},{144,80},{160,96},{176,11... | collective-permute-start | bytes 786440 | tf_op jit(solution)/shard_map/ppermute | solution.py:182
  40.7 8.6 %collective-permute-start.3 = (bf16[16,32,256]{2,1,0:T(8,128)(2,1)S(1)}, bf16[16,32,256]{2,1,0:T(8,128)(2,1)S(1)}, u32[]{:S(2)}, u32[]{:S(2)}) collective-permute-start(bf16[16,32,256]{2,1,0:T(8,128)(2,1)S(1)} %get-tuple-element.12), channel_id=1, source_target_pairs={{448,0},{464,16},{480,32},{496,48},{0,64},{16,80},{32,96},{48,112}... | collective-permute-start | bytes 786440 | tf_op jit(solution)/shard_map/ppermute | solution.py:183
  49.3 9.6 %copy-start.1 = (bf16[16,192,256]{2,1,0:T(8,128)(2,1)}, bf16[16,192,256]{2,1,0:T(8,128)(2,1)S(1)}, u32[]{:S(2)}) copy-start(bf16[16,192,256]{2,1,0:T(8,128)(2,1)S(1)} %constant_dynamic-update-slice_fusion.far_ref) | copy-start | bytes 4718596
  49.3 9.6 %collective-permute-start.5 = (bf16[16,192,256]{2,1,0:T(8,128)(2,1)S(1)}, bf16[16,192,256]{2,1,0:T(8,128)(2,1)}, u32[]{:S(2)}, u32[]{:S(2)}) collective-permute-start(bf16[16,192,256]{2,1,0:T(8,128)(2,1)S(1)} %constant_dynamic-update-slice_fusion.far_ref), channel_id=1, source_target_pairs={{0,1},{1,0},{2,3},{3,2},{4,5},{5,4},{6,7},{7,6},{8,9},{9,8},{10,11... | collective-permute-start | bytes 4718600 | tf_op jit(solution)/shard_map/ppermute | solution.py:186
  55.1 3.8 %collective-permute-start.4 = (bf16[16,64,256]{2,1,0:T(8,128)(2,1)S(1)}, bf16[16,64,256]{2,1,0:T(8,128)(2,1)S(1)}, u32[]{:S(2)}, u32[]{:S(2)}) collective-permute-start(bf16[16,64,256]{2,1,0:T(8,128)(2,1)S(1)} %bitcast.8), channel_id=1, source_target_pairs={{0,1},{1,0},{2,3},{3,2},{4,5},{5,4},{6,7},{7,6},{8,9},{9,8},{10,11... | collective-permute-start | bytes 1572872 | tf_op jit(solution)/shard_map/ppermute | solution.py:184
  58.9 0.8 copy-start.2
  89.1 13.4 %all-to-all-start.2 = ((f32[16,8,128]{2,1,0:T(8,128)}), f32[16,8,128]{2,1,0:T(8,128)S(1)}, u32[]{:S(2)}, u32[]{:S(2)}) async-start(f32[16,8,128]{2,1,0:T(8,128)} %get-tuple-element.10), calls=%async_computation.2 | async-start | bytes 131072 | tf_op jit(solution)/shard_map/all_to_all | solution.py:228
  102.5 0.6 copy-start.3

commit v3 on v0

v3 whole, which is shorter than its diff:
```python
import jax
import jax.numpy as jnp
from jax import lax
from jax.experimental import pallas as pl
from jax.experimental.pallas import tpu as pltpu
from jax.sharding import PartitionSpec as P

LANES = 128
SUBLANES = 8
X_SIZE = 4
COLOURS = 4
VMEM_LIMIT = 24 * 2**20
SMALL = pltpu.CompilerParams(vmem_limit_bytes=4 * 2**20)


def colour_of(slot):
    return lax.rem(lax.rem(slot, X_SIZE) + 2 * lax.div(slot, X_SIZE), COLOURS)


def spread_kernel(sizes_ref, psi_ref, out_ref, buf, sem):
    copies, here, quarter, block = out_ref.shape
    first = lax.axis_index("sec") * here
    start = pl.multiple_of(colour_of(lax.axis_index("ops")) * quarter, quarter)
    copy = pltpu.make_async_copy(psi_ref.at[:, pl.ds(start, quarter)], buf, sem)
    copy.start()
    row = lax.broadcasted_iota(jnp.int32, (quarter, block), 0) + start
    farthest = jnp.maximum(row, lax.broadcasted_iota(jnp.int32, (quarter, block), 1))
    copy.wait()
    for k in range(here):
        part = jnp.where(farthest < sizes_ref[first + k], buf[k], 0)
        for copy_at in range(copies):
            out_ref[copy_at, k] = part


def sigma_kernel(sectors, rows, factor):
    def body(
        charge_ref, sizes_ref, psi_ref, mine_ref, other_ref, left_ref, right_ref,
        out_ref, norm_ref, own_ref, live_ref, half_buf, own_buf,
    ):
        pairs, here, block, _ = left_ref.shape
        sec = lax.axis_index("sec")
        first = sec * here
        start = pl.multiple_of(lax.axis_index("ops") * rows, rows)
        core = lax.rem(sec, 2)
        for p in range(pairs):
            for k in range(here):
                source = lax.rem(first + k + charge_ref[p], sectors)
                place = lax.div(source, 2 * here) * here + lax.rem(source, here)
                across = lax.rem(lax.div(source, here), 2) != core
                psi = jnp.where(across, other_ref[place], mine_ref[place])
                half_buf[k, :, p * block : (p + 1) * block] = jnp.dot(
                    left_ref[p, k], psi, preferred_element_type=jnp.float32
                ).astype(jnp.bfloat16)
        row = lax.broadcasted_iota(jnp.int32, (block, block), 0)
        column = lax.broadcasted_iota(jnp.int32, (block, block), 1)
        farthest = jnp.maximum(row, column)
        part_row = lax.broadcasted_iota(jnp.int32, (rows, block), 0) + start
        part_farthest = jnp.maximum(part_row, lax.broadcasted_iota(jnp.int32, (rows, block), 1))
        correlation = jnp.zeros((1, 1), jnp.float32)
        norm = jnp.zeros((1, 1), jnp.float32)
        for k in range(here):
            size = sizes_ref[first + k]
            total = jnp.zeros((block, block), jnp.float32)
            for p in range(pairs):
                total += lax.dot_general(
                    half_buf[k, :, p * block : (p + 1) * block], right_ref[p, k],
                    (((1,), (1,)), ((), ())), preferred_element_type=jnp.float32,
                )
            total = total * factor
            psi = jnp.where(farthest < size, psi_ref[k], 0).astype(jnp.float32)
            own_buf[k] = psi
            correlation += jnp.sum(psi * total, keepdims=True)
            norm += jnp.sum(psi * psi, keepdims=True)
            out_ref[:, k * rows : (k + 1) * rows, :block] = total.reshape(
                block // rows, rows, block
            ).astype(jnp.bfloat16)
            own_ref[k] = own_buf[k, pl.ds(start, rows)]
            live_ref[k] = jnp.where(part_farthest < size, 1.0, 0.0)
        high = correlation.astype(jnp.bfloat16).astype(jnp.float32)
        middle = (correlation - high).astype(jnp.bfloat16).astype(jnp.float32)
        low = correlation - high - middle
        lane = lax.broadcasted_iota(jnp.int32, (here * rows, LANES), 1)
        up = lax.broadcasted_iota(jnp.int32, (here * rows, LANES), 0)
        words = jnp.where(
            lane == 0, high, jnp.where(lane == 1, middle, jnp.where(lane == 2, low, 0.0))
        )
        words = jnp.where(up == 0, words, 0.0).astype(jnp.bfloat16)
        out_ref[:, :, block:] = jnp.broadcast_to(words[None], (block // rows, *words.shape))
        norm_ref[...] = jnp.broadcast_to(norm, norm_ref.shape)

    return body


def sum_kernel(received_ref, norm_ref, live_ref, sigma_ref, wide_ref, both_ref):
    here, rows, block = wide_ref.shape
    summed = jnp.sum(received_ref[...].astype(jnp.float32), axis=0)
    correlation = jnp.sum(summed[:, block:], keepdims=True)
    up = lax.broadcasted_iota(jnp.int32, both_ref.shape[1:], 0)
    both = jnp.where(up == 0, correlation, norm_ref[...])
    both_ref[...] = jnp.broadcast_to(both[None], both_ref.shape)
    for k in range(here):
        part = jnp.where(live_ref[k] > 0, summed[k * rows : (k + 1) * rows, :block], 0.0)
        wide_ref[k] = part
        sigma_ref[k] = part.astype(jnp.bfloat16)


def residual_kernel(both_ref, wide_ref, own_ref, out_ref):
    both = jnp.sum(both_ref[...], axis=0)
    ritz_value = both[0:1, 0:1] / both[1:2, 0:1]
    for k in range(wide_ref.shape[0]):
        out_ref[k] = (wide_ref[k] - ritz_value * own_ref[k]).astype(jnp.bfloat16)


def local(wavefunction, left_ops, right_ops, charge, block_sizes):
    here, block, _ = wavefunction.shape
    pairs = left_ops.shape[0]
    ops_count = lax.axis_size("ops")
    sec_total = lax.axis_size("sec")
    sectors = block_sizes.shape[0]
    rows = block // ops_count
    quarter = block // COLOURS
    factor = float(pairs * ops_count) ** (-0.5)
    chips_z = sec_total // 2
    y_size = ops_count // X_SIZE
    colour = colour_of(lax.axis_index("ops"))
    smem = pl.BlockSpec(memory_space=pltpu.SMEM)
    vmem = pl.BlockSpec(memory_space=pltpu.VMEM)
    bf16, f32 = jnp.bfloat16, jnp.float32

    spread = pl.pallas_call(
        spread_kernel,
        out_shape=jax.ShapeDtypeStruct((chips_z, here, quarter, block), bf16),
        in_specs=[smem, pl.BlockSpec(memory_space=pl.ANY)],
        out_specs=vmem,
        scratch_shapes=[pltpu.VMEM((here, quarter, block), bf16), pltpu.SemaphoreType.DMA],
        compiler_params=SMALL,
    )(block_sizes, wavefunction)
    same_core = [[2 * z + core for z in range(chips_z)] for core in range(2)]
    near = lax.all_to_all(spread, "sec", 0, 0, axis_index_groups=same_core)
    near = near.reshape(chips_z * here, quarter, block)

    def from_x(step):
        return [(y * X_SIZE + (x + step) % X_SIZE, y * X_SIZE + x)
                for y in range(y_size) for x in range(X_SIZE)]

    def from_y(step):
        return [((y + step) % y_size * X_SIZE + x, y * X_SIZE + x)
                for y in range(y_size) for x in range(X_SIZE)]

    x_next = lax.ppermute(near, "ops", from_x(1))
    x_last = lax.ppermute(near, "ops", from_x(-1))
    y_next = lax.ppermute(near[:, : quarter // 2], "ops", from_y(1))
    y_last = lax.ppermute(near[:, quarter // 2 :], "ops", from_y(-1))
    mine = jnp.zeros((chips_z * here, COLOURS, quarter, block), bf16)
    for piece, relative, at in (
        (near, 0, 0), (x_next, 1, 0), (x_last, 3, 0), (y_next, 2, 0), (y_last, 2, quarter // 2)
    ):
        where = (0, lax.rem(colour + relative, COLOURS), at, 0)
        mine = lax.dynamic_update_slice(mine, piece[:, None], where)
    mine = mine.reshape(chips_z * here, block, block)
    other = lax.ppermute(mine, "sec", [(s, s ^ 1) for s in range(sec_total)])

    part = (here, rows, block)
    pieces, norm, own_rows, live = pl.pallas_call(
        sigma_kernel(sectors, rows, factor),
        out_shape=(
            jax.ShapeDtypeStruct((ops_count, here * rows, block + LANES), bf16),
            jax.ShapeDtypeStruct((SUBLANES, LANES), f32),
            jax.ShapeDtypeStruct(part, f32),
            jax.ShapeDtypeStruct(part, f32),
        ),
        in_specs=[smem] * 2 + [vmem] * 5,
        out_specs=(vmem,) * 4,
        scratch_shapes=[
            pltpu.VMEM((here, block, pairs * block), bf16),
            pltpu.VMEM((here, block, block), f32),
        ],
        compiler_params=pltpu.CompilerParams(vmem_limit_bytes=VMEM_LIMIT),
        cost_estimate=pl.CostEstimate(
            flops=4 * pairs * here * block**3, bytes_accessed=2**20, transcendentals=0
        ),
    )(charge, block_sizes, wavefunction, mine, other, left_ops, right_ops)
    received = lax.all_to_all(pieces, "ops", 0, 0)

    sigma, wide, both = pl.pallas_call(
        sum_kernel,
        out_shape=(
            jax.ShapeDtypeStruct(part, bf16),
            jax.ShapeDtypeStruct(part, f32),
            jax.ShapeDtypeStruct((sec_total, SUBLANES, LANES), f32),
        ),
        in_specs=[vmem] * 3,
        out_specs=(vmem,) * 3,
        compiler_params=SMALL,
    )(received, norm, live)
    both = lax.all_to_all(both, "sec", 0, 0)
    residual = pl.pallas_call(
        residual_kernel,
        out_shape=jax.ShapeDtypeStruct(part, bf16),
        in_specs=[vmem] * 3,
        out_specs=vmem,
        compiler_params=SMALL,
    )(both, wide, own_rows)
    return sigma, residual


def solution(mesh):
    placed = (
        P("sec", None, None),
        P("ops", "sec", None, None),
        P("ops", "sec", None, None),
        P("ops"),
        P(),
    )
    return jax.shard_map(
        local,
        mesh=mesh,
        in_specs=placed,
        out_specs=(P("sec", "ops", None), P("sec", "ops", None)),
        check_vma=False,
    )
```

time: 342 us -> 96.2 us (0.28)
  waiting for transfers between devices: 204 us -> 9.92 us
  blocking collectives: 101 us -> 59.8 us
  starting transfers between devices: 0.08 us -> 19.1 us
  between operations: 15.4 us -> 0.87 us
  other arithmetic: 9.26 us -> 0 us
  local copies, waits for them, and re-layouts: 8.21 us -> 2.11 us
  matrix products: 4.34 us -> 0 us
  Pallas kernels: 0 us -> 4.1 us
    psum x1 -> x0, waiting for transfers between devices: 152 us -> none  [local(): summed = lax.psum(partial_sum, 'ops')]
    psum x1 -> x0, blocking collectives: 101 us -> none  [local(): lax.psum((jnp.sum(own_rows * sigma_block), jnp.sum(own_rows * own_rows)),...]
    all_to_all x0 -> x3, blocking collectives: none -> 59.8 us  [the longest x1 26.7 us: local(): near = lax.all_to_all(spread, 'sec', 0, 0, axis_index_groups=same_core)]
    all_gather x1 -> x0, waiting for transfers between devices: 51.5 us -> none  [local(): gathered = lax.all_gather(wavefunction, 'sec', axis=0, tiled=True)]
    ppermute x0 -> x5, starting transfers between devices: none -> 19.1 us  [the longest x1 5.78 us: local(): other = lax.ppermute(mine, 'sec', [(s, s ^ 1) for s in range(sec_total)])]
    ppermute x0 -> x5, waiting for transfers between devices: none -> 9.92 us  [the longest x1 4.34 us: local(): x_last = lax.ppermute(near, 'ops', from_x(-1))]
    gather x2 -> x0, local copies, waits for them, and re-layouts: 8.12 us -> none  [local(): selected_rows = jnp.take(masked, sources, axis=0)]
    dot_general x1 -> x0, matrix products: 4.34 us -> none  [local(): jnp.einsum('pkac,pkdc->kad', split_pieces, right_ops, preferred_element_t...]
  transfers between devices with their start and end apart: 2 -> 5, of which waited for: 2 -> 3; matrix products, arithmetic and copies ran while one was open for 1% -> 0% of each run, Pallas kernels for 0% -> 0%
where the time goes in v3:
time: 96.2 us; the launch traced here: 95.9 us
  blocking collectives  59.8 us (62%)
  starting transfers between devices  19.1 us (20%)
  waiting for transfers between devices  9.92 us (10%)
  Pallas kernels  4.1 us (4%)
  local copies, waits for them, and re-layouts  2.11 us (2%)
    all_to_all x1, blocking collectives, local(): near = lax.all_to_all(spread, 'sec', 0, 0, axis_index_groups=same_core)  26.7 us
    all_to_all x1, blocking collectives, local(): received = lax.all_to_all(pieces, 'ops', 0, 0)  20.5 us
    all_to_all x1, blocking collectives, local(): both = lax.all_to_all(both, 'sec', 0, 0)  12.6 us
    ppermute x1, starting transfers between devices, local(): other = lax.ppermute(mine, 'sec', [(s, s ^ 1) for s in range(sec_total)])  5.78 us
    ppermute x1, starting transfers between devices, local(): y_next = lax.ppermute(near[:, :quarter // 2], 'ops', from_y(1))  5.1 us
    ppermute x1, starting transfers between devices, local(): x_next = lax.ppermute(near, 'ops', from_x(1))  4.38 us
    ppermute x1, waiting for transfers between devices, local(): x_last = lax.ppermute(near, 'ops', from_x(-1))  4.34 us
    ppermute x1, waiting for transfers between devices, local(): other = lax.ppermute(mine, 'sec', [(s, s ^ 1) for s in range(sec_total)])  3.76 us
  transfers between devices with their start and end apart: 5, of which 3 were waited for; matrix products, arithmetic and copies ran while one was open for 0% of the time, Pallas kernels for 0%

profile of v3, /device:TPU:1, one launch (start us, length us, event | category | flops | bytes accessed | tf_op | source)
XLA Modules:
  0.0 95.9 jit_solution(13714036277987171276)
XLA Ops:
  0.6 0.0 copy-start.2
  0.6 0.9 copy-done.2
  1.6 0.0 copy-start.4
  1.6 0.7 copy-done.4
  2.2 0.7 shard_map.68
  2.9 26.7 %all_to_all.15 = bf16[8,2,64,256]{3,2,1,0:T(8,128)(2,1)S(1)} all-to-all(bf16[8,2,64,256]{3,2,1,0:T(8,128)(2,1)S(1)} %shard_map.68), channel_id=1, replica_groups={{0,2,4,6,8,10,12,14},{1,3,5,7,9,11,13,15},{16,18,20,22,24,26,28,30},{17..., dimensions={0} | all-to-all | bytes 1048576 | tf_op jit(solution)/shard_map/all_to_all | solution.py:139
  29.6 4.4 %collective-permute-start = (bf16[16,64,256]{2,1,0:T(8,128)(2,1)S(1)}, bf16[16,64,256]{2,1,0:T(8,128)(2,1)S(1)}, u32[]{:S(2)}, u32[]{:S(2)}) collective-permute-start(bf16[16,64,256]{2,1,0:T(8,128)(2,1)S(1)} %bitcast.21), channel_id=1, source_target_pairs={{16,0},{32,16},{48,32},{0,48},{80,64},{96,80},{112,96},{64,112},{1... | collective-permute-start | bytes 1572872 | tf_op jit(solution)/shard_map/ppermute | solution.py:150
  34.0 1.9 %collective-permute-start.1 = (bf16[16,64,256]{2,1,0:T(8,128)(2,1)S(1)}, bf16[16,64,256]{2,1,0:T(8,128)(2,1)S(1)}, u32[]{:S(2)}, u32[]{:S(2)}) collective-permute-start(bf16[16,64,256]{2,1,0:T(8,128)(2,1)S(1)} %bitcast.22), channel_id=1, source_target_pairs={{48,0},{0,16},{16,32},{32,48},{112,64},{64,80},{80,96},{96,112},{1... | collective-permute-start | bytes 1572872 | tf_op jit(solution)/shard_map/ppermute | solution.py:151
  36.0 5.1 %collective-permute-start.2 = (bf16[16,32,256]{2,1,0:T(8,128)(2,1)S(1)}, bf16[16,32,256]{2,1,0:T(8,128)(2,1)S(1)}, u32[]{:S(2)}, u32[]{:S(2)}) collective-permute-start(bf16[16,32,256]{2,1,0:T(8,128)(2,1)S(1)} %get-tuple-element.17), channel_id=1, source_target_pairs={{64,0},{80,16},{96,32},{112,48},{128,64},{144,80},{160,96},{176,11... | collective-permute-start | bytes 786440 | tf_op jit(solution)/shard_map/ppermute | solution.py:152
  41.1 1.9 %collective-permute-start.3 = (bf16[16,32,256]{2,1,0:T(8,128)(2,1)S(1)}, bf16[16,32,256]{2,1,0:T(8,128)(2,1)S(1)}, u32[]{:S(2)}, u32[]{:S(2)}) collective-permute-start(bf16[16,32,256]{2,1,0:T(8,128)(2,1)S(1)} %get-tuple-element.16), channel_id=1, source_target_pairs={{448,0},{464,16},{480,32},{496,48},{0,64},{16,80},{32,96},{48,112}... | collective-permute-start | bytes 786440 | tf_op jit(solution)/shard_map/ppermute | solution.py:153
  43.0 0.0 copy-start.3
  43.0 0.2 broadcast_in_dim.15
  43.3 0.0 copy-start
  43.3 0.0 copy-start.1
  43.3 0.0 copy-start.5
  43.3 0.0 copy-start.6
  43.4 0.0 collective-permute-done
  43.4 4.3 %collective-permute-done.1 = bf16[16,64,256]{2,1,0:T(8,128)(2,1)S(1)} collective-permute-done((bf16[16,64,256]{2,1,0:T(8,128)(2,1)S(1)}, bf16[16,64,256]{2,1,0:T(8,128)(2,1)S(1)}, u32[]{:S(2)}, u32[]{:S(2)}) %collective-permute-start.1) | collective-permute-done | bytes 524320 | tf_op jit(solution)/shard_map/ppermute | solution.py:151
  47.8 0.1 bitcast_dynamic-update-slice_fusion
  47.9 0.0 collective-permute-done.2
  47.9 1.8 %collective-permute-done.3 = bf16[16,32,256]{2,1,0:T(8,128)(2,1)S(1)} collective-permute-done((bf16[16,32,256]{2,1,0:T(8,128)(2,1)S(1)}, bf16[16,32,256]{2,1,0:T(8,128)(2,1)S(1)}, u32[]{:S(2)}, u32[]{:S(2)}) %collective-permute-start.3) | collective-permute-done | bytes 262176 | tf_op jit(solution)/shard_map/ppermute | solution.py:153
  49.7 5.8 %collective-permute-start.4 = (bf16[16,256,256]{2,1,0:T(8,128)(2,1)S(1)}, bf16[16,256,256]{2,1,0:T(8,128)(2,1)S(1)}, u32[]{:S(2)}, u32[]{:S(2)}) collective-permute-start(bf16[16,256,256]{2,1,0:T(8,128)(2,1)S(1)} %bitcast.19), channel_id=1, source_target_pairs={{0,1},{1,0},{2,3},{3,2},{4,5},{5,4},{6,7},{7,6},{8,9},{9,8},{10,11... | collective-permute-start | bytes 6291464 | tf_op jit(solution)/shard_map/ppermute | solution.py:161
  55.5 3.8 %collective-permute-done.4.other_ref = bf16[16,256,256]{2,1,0:T(8,128)(2,1)S(1)} collective-permute-done((bf16[16,256,256]{2,1,0:T(8,128)(2,1)S(1)}, bf16[16,256,256]{2,1,0:T(8,128)(2,1)S(1)}, u32[]{:S(2)}, u32[]{:S(2)}) %collective-permute-start.4) | collective-permute-done | bytes 2097184 | tf_op jit(solution)/shard_map/ppermute | solution.py:161
  59.3 0.0 copy-done.3
  59.3 0.0 copy-done
  59.3 0.0 copy-done.1
  59.3 0.0 copy-done.5
  59.3 0.0 copy-done.6
  59.3 2.1 %shard_map.69 = (bf16[32,16,384]{2,1,0:T(8,128)(2,1)S(1)}, f32[8,128]{1,0:T(8,128)S(1)}, f32[2,8,256]{2,1,0:T(8,128)S(1)}, f32[2,8,256]{2,1,0:T(8,128)S(1)}) custom-call(s32[8]{0:T(128)S(1)} %copy-done.6, s32[32]{0:T(128)S(1)} %copy-done.5, bf16[2,256,256]{2,1,0:T(8,128)(2,1)S(1)} %copy-done.3, bf16[16,256,256]{2,1,0:T(8,128)(2,1)S(1)} %bitcast.20, ...), custom_call_target="tpu_custom_call" | custom-call | flops 1073741824 | bytes 1048576 | tf_op jit(solution)/shard_map/pallas_call | solution.py:164
  61.4 20.5 %all_to_all.16.received_ref = bf16[32,16,384]{2,1,0:T(8,128)(2,1)S(1)} all-to-all(bf16[32,16,384]{2,1,0:T(8,128)(2,1)S(1)} %get-tuple-element.9), channel_id=1, replica_groups=mesh['ops'=32,'sec'=16] {'ops'}, dimensions={0} | all-to-all | bytes 786432 | tf_op jit(solution)/shard_map/all_to_all | solution.py:183
  82.0 0.7 shard_map.70
  82.6 12.6 %all_to_all.17.both_ref = f32[16,8,128]{2,1,0:T(8,128)S(1)} all-to-all(f32[16,8,128]{2,1,0:T(8,128)S(1)} %get-tuple-element.13), channel_id=1, replica_groups=mesh['ops'=32,'sec'=16] {'sec'}, dimensions={0} | all-to-all | bytes 131072 | tf_op jit(solution)/shard_map/all_to_all | solution.py:196
  95.2 0.7 shard_map.71
  (5 shorter events, 0.2 us)
Async XLA Ops:
  0.6 1.0 copy-start.2
  1.6 0.7 copy-start.4
  29.6 13.8 %collective-permute-start = (bf16[16,64,256]{2,1,0:T(8,128)(2,1)S(1)}, bf16[16,64,256]{2,1,0:T(8,128)(2,1)S(1)}, u32[]{:S(2)}, u32[]{:S(2)}) collective-permute-start(bf16[16,64,256]{2,1,0:T(8,128)(2,1)S(1)} %bitcast.21), channel_id=1, source_target_pairs={{16,0},{32,16},{48,32},{0,48},{80,64},{96,80},{112,96},{64,112},{1... | collective-permute-start | bytes 1572872 | tf_op jit(solution)/shard_map/ppermute | solution.py:150
  34.0 13.8 %collective-permute-start.1 = (bf16[16,64,256]{2,1,0:T(8,128)(2,1)S(1)}, bf16[16,64,256]{2,1,0:T(8,128)(2,1)S(1)}, u32[]{:S(2)}, u32[]{:S(2)}) collective-permute-start(bf16[16,64,256]{2,1,0:T(8,128)(2,1)S(1)} %bitcast.22), channel_id=1, source_target_pairs={{48,0},{0,16},{16,32},{32,48},{112,64},{64,80},{80,96},{96,112},{1... | collective-permute-start | bytes 1572872 | tf_op jit(solution)/shard_map/ppermute | solution.py:151
  36.0 11.9 %collective-permute-start.2 = (bf16[16,32,256]{2,1,0:T(8,128)(2,1)S(1)}, bf16[16,32,256]{2,1,0:T(8,128)(2,1)S(1)}, u32[]{:S(2)}, u32[]{:S(2)}) collective-permute-start(bf16[16,32,256]{2,1,0:T(8,128)(2,1)S(1)} %get-tuple-element.17), channel_id=1, source_target_pairs={{64,0},{80,16},{96,32},{112,48},{128,64},{144,80},{160,96},{176,11... | collective-permute-start | bytes 786440 | tf_op jit(solution)/shard_map/ppermute | solution.py:152
  41.1 8.6 %collective-permute-start.3 = (bf16[16,32,256]{2,1,0:T(8,128)(2,1)S(1)}, bf16[16,32,256]{2,1,0:T(8,128)(2,1)S(1)}, u32[]{:S(2)}, u32[]{:S(2)}) collective-permute-start(bf16[16,32,256]{2,1,0:T(8,128)(2,1)S(1)} %get-tuple-element.16), channel_id=1, source_target_pairs={{448,0},{464,16},{480,32},{496,48},{0,64},{16,80},{32,96},{48,112}... | collective-permute-start | bytes 786440 | tf_op jit(solution)/shard_map/ppermute | solution.py:153
  43.0 16.3 %copy-start.3 = (bf16[2,256,256]{2,1,0:T(8,128)(2,1)S(1)}, bf16[2,256,256]{2,1,0:T(8,128)(2,1)}, u32[]{:S(2)}) copy-start(bf16[2,256,256]{2,1,0:T(8,128)(2,1)} %psi_ref.3) | copy-start | bytes 786436
  43.3 16.0 %copy-start = (bf16[8,2,256,256]{3,2,1,0:T(8,128)(2,1)S(1)}, bf16[8,2,256,256]{3,2,1,0:T(8,128)(2,1)}, u32[]{:S(2)}) copy-start(bf16[8,2,256,256]{3,2,1,0:T(8,128)(2,1)} %left_ref.1) | copy-start | bytes 6291460
  43.3 16.0 %copy-start.1 = (bf16[8,2,256,256]{3,2,1,0:T(8,128)(2,1)S(1)}, bf16[8,2,256,256]{3,2,1,0:T(8,128)(2,1)}, u32[]{:S(2)}) copy-start(bf16[8,2,256,256]{3,2,1,0:T(8,128)(2,1)} %right_ref.1) | copy-start | bytes 6291460
  43.3 16.0 %copy-start.5 = (s32[32]{0:T(128)S(1)}, s32[32]{0:T(128)}, u32[]{:S(2)}) copy-start(s32[32]{0:T(128)} %sizes_ref.3) | copy-start | bytes 388
  43.3 16.0 %copy-start.6 = (s32[8]{0:T(128)S(1)}, s32[8]{0:T(128)}, u32[]{:S(2)}) copy-start(s32[8]{0:T(128)} %charge_ref.1) | copy-start | bytes 100
  49.7 9.6 %collective-permute-start.4 = (bf16[16,256,256]{2,1,0:T(8,128)(2,1)S(1)}, bf16[16,256,256]{2,1,0:T(8,128)(2,1)S(1)}, u32[]{:S(2)}, u32[]{:S(2)}) collective-permute-start(bf16[16,256,256]{2,1,0:T(8,128)(2,1)S(1)} %bitcast.19), channel_id=1, source_target_pairs={{0,1},{1,0},{2,3},{3,2},{4,5},{5,4},{6,7},{7,6},{8,9},{9,8},{10,11... | collective-permute-start | bytes 6291464 | tf_op jit(solution)/shard_map/ppermute | solution.py:161

commit v4 on v3

--- a/solution.py
+++ b/solution.py
@@ -17,24 +17,9 @@
     return lax.rem(lax.rem(slot, X_SIZE) + 2 * lax.div(slot, X_SIZE), COLOURS)
 
 
-def spread_kernel(sizes_ref, psi_ref, out_ref, buf, sem):
-    copies, here, quarter, block = out_ref.shape
-    first = lax.axis_index("sec") * here
-    start = pl.multiple_of(colour_of(lax.axis_index("ops")) * quarter, quarter)
-    copy = pltpu.make_async_copy(psi_ref.at[:, pl.ds(start, quarter)], buf, sem)
-    copy.start()
-    row = lax.broadcasted_iota(jnp.int32, (quarter, block), 0) + start
-    farthest = jnp.maximum(row, lax.broadcasted_iota(jnp.int32, (quarter, block), 1))
-    copy.wait()
-    for k in range(here):
-        part = jnp.where(farthest < sizes_ref[first + k], buf[k], 0)
-        for copy_at in range(copies):
-            out_ref[copy_at, k] = part
-
-
 def sigma_kernel(sectors, rows, factor):
     def body(
-        charge_ref, sizes_ref, psi_ref, mine_ref, other_ref, left_ref, right_ref,
+        charge_ref, sizes_ref, live_all_ref, psi_ref, mine_ref, other_ref, left_ref, right_ref,
         out_ref, norm_ref, own_ref, live_ref, half_buf, own_buf,
     ):
         pairs, here, block, _ = left_ref.shape
@@ -48,9 +33,10 @@
                 place = lax.div(source, 2 * here) * here + lax.rem(source, here)
                 across = lax.rem(lax.div(source, here), 2) != core
                 psi = jnp.where(across, other_ref[place], mine_ref[place])
-                half_buf[k, :, p * block : (p + 1) * block] = jnp.dot(
-                    left_ref[p, k], psi, preferred_element_type=jnp.float32
-                ).astype(jnp.bfloat16)
+                live = live_all_ref[pl.ds(source, 1), :]
+                left = left_ref[p, k] * live.astype(jnp.bfloat16)
+                half = jnp.dot(left, psi, preferred_element_type=jnp.float32) * live
+                half_buf[k, :, p * block : (p + 1) * block] = half.astype(jnp.bfloat16)
         row = lax.broadcasted_iota(jnp.int32, (block, block), 0)
         column = lax.broadcasted_iota(jnp.int32, (block, block), 1)
         farthest = jnp.maximum(row, column)
@@ -71,21 +57,23 @@
             own_buf[k] = psi
             correlation += jnp.sum(psi * total, keepdims=True)
             norm += jnp.sum(psi * psi, keepdims=True)
-            out_ref[:, k * rows : (k + 1) * rows, :block] = total.reshape(
-                block // rows, rows, block
-            ).astype(jnp.bfloat16)
+            cut = total.reshape(block // rows, rows, block).astype(jnp.bfloat16)
+            for part in range(block // LANES):
+                at = (part * here + k) * rows
+                out_ref[:, at : at + rows, :] = cut[:, :, part * LANES : (part + 1) * LANES]
             own_ref[k] = own_buf[k, pl.ds(start, rows)]
             live_ref[k] = jnp.where(part_farthest < size, 1.0, 0.0)
         high = correlation.astype(jnp.bfloat16).astype(jnp.float32)
         middle = (correlation - high).astype(jnp.bfloat16).astype(jnp.float32)
         low = correlation - high - middle
-        lane = lax.broadcasted_iota(jnp.int32, (here * rows, LANES), 1)
-        up = lax.broadcasted_iota(jnp.int32, (here * rows, LANES), 0)
+        lane = lax.broadcasted_iota(jnp.int32, (rows, LANES), 1)
+        up = lax.broadcasted_iota(jnp.int32, (rows, LANES), 0)
         words = jnp.where(
             lane == 0, high, jnp.where(lane == 1, middle, jnp.where(lane == 2, low, 0.0))
         )
         words = jnp.where(up == 0, words, 0.0).astype(jnp.bfloat16)
-        out_ref[:, :, block:] = jnp.broadcast_to(words[None], (block // rows, *words.shape))
+        body_rows = here * rows * (block // LANES)
+        out_ref[:, body_rows:, :] = jnp.broadcast_to(words[None], (block // rows, *words.shape))
         norm_ref[...] = jnp.broadcast_to(norm, norm_ref.shape)
 
     return body
@@ -94,14 +82,17 @@
 def sum_kernel(received_ref, norm_ref, live_ref, sigma_ref, wide_ref, both_ref):
     here, rows, block = wide_ref.shape
     summed = jnp.sum(received_ref[...].astype(jnp.float32), axis=0)
-    correlation = jnp.sum(summed[:, block:], keepdims=True)
+    parts = block // LANES
+    correlation = jnp.sum(summed[parts * here * rows :], keepdims=True)
     up = lax.broadcasted_iota(jnp.int32, both_ref.shape[1:], 0)
     both = jnp.where(up == 0, correlation, norm_ref[...])
     both_ref[...] = jnp.broadcast_to(both[None], both_ref.shape)
     for k in range(here):
-        part = jnp.where(live_ref[k] > 0, summed[k * rows : (k + 1) * rows, :block], 0.0)
-        wide_ref[k] = part
-        sigma_ref[k] = part.astype(jnp.bfloat16)
+        for part in range(parts):
+            at, lanes = (part * here + k) * rows, slice(part * LANES, (part + 1) * LANES)
+            kept = jnp.where(live_ref[k, :, lanes] > 0, summed[at : at + rows], 0.0)
+            wide_ref[k, :, lanes] = kept
+            sigma_ref[k, :, lanes] = kept.astype(jnp.bfloat16)
 
 
 def residual_kernel(both_ref, wide_ref, own_ref, out_ref):
@@ -127,14 +118,10 @@
     vmem = pl.BlockSpec(memory_space=pltpu.VMEM)
     bf16, f32 = jnp.bfloat16, jnp.float32
 
-    spread = pl.pallas_call(
-        spread_kernel,
-        out_shape=jax.ShapeDtypeStruct((chips_z, here, quarter, block), bf16),
-        in_specs=[smem, pl.BlockSpec(memory_space=pl.ANY)],
-        out_specs=vmem,
-        scratch_shapes=[pltpu.VMEM((here, quarter, block), bf16), pltpu.SemaphoreType.DMA],
-        compiler_params=SMALL,
-    )(block_sizes, wavefunction)
+    own_quarter = lax.dynamic_slice_in_dim(wavefunction, colour * quarter, quarter, 1)
+    spread = jnp.broadcast_to(own_quarter[None], (chips_z, *own_quarter.shape))
+    positions = jnp.arange(block, dtype=jnp.int32)
+    live_all = (positions[None, :] < block_sizes[:, None]).astype(f32)
     same_core = [[2 * z + core for z in range(chips_z)] for core in range(2)]
     near = lax.all_to_all(spread, "sec", 0, 0, axis_index_groups=same_core)
     near = near.reshape(chips_z * here, quarter, block)
@@ -161,15 +148,16 @@
     other = lax.ppermute(mine, "sec", [(s, s ^ 1) for s in range(sec_total)])
 
     part = (here, rows, block)
+    pack_rows = here * rows * (block // LANES) + rows
     pieces, norm, own_rows, live = pl.pallas_call(
         sigma_kernel(sectors, rows, factor),
         out_shape=(
-            jax.ShapeDtypeStruct((ops_count, here * rows, block + LANES), bf16),
+            jax.ShapeDtypeStruct((ops_count, pack_rows, LANES), bf16),
             jax.ShapeDtypeStruct((SUBLANES, LANES), f32),
             jax.ShapeDtypeStruct(part, f32),
             jax.ShapeDtypeStruct(part, f32),
         ),
-        in_specs=[smem] * 2 + [vmem] * 5,
+        in_specs=[smem] * 2 + [vmem] * 6,
         out_specs=(vmem,) * 4,
         scratch_shapes=[
             pltpu.VMEM((here, block, pairs * block), bf16),
@@ -179,7 +167,7 @@
         cost_estimate=pl.CostEstimate(
             flops=4 * pairs * here * block**3, bytes_accessed=2**20, transcendentals=0
         ),
-    )(charge, block_sizes, wavefunction, mine, other, left_ops, right_ops)
+    )(charge, block_sizes, live_all, wavefunction, mine, other, left_ops, right_ops)
     received = lax.all_to_all(pieces, "ops", 0, 0)
 
     sigma, wide, both = pl.pallas_call(

time: 96.2 us -> 93.9 us (0.976)
  blocking collectives: 59.8 us -> 58.7 us
    unnamed x14 -> x10, local copies, waits for them, and re-layouts: 1.63 us -> 0.03 us
    all_to_all x1, blocking collectives: 20.5 us -> 19.4 us  [local(): received = lax.all_to_all(pieces, 'ops', 0, 0)]
  transfers between devices with their start and end apart: 5 -> 5, of which waited for: 3 -> 3; matrix products, arithmetic and copies ran while one was open for 0% -> 1% of each run, Pallas kernels for 0% -> 0%
where the time goes in v4:
time: 93.9 us; the launch traced here: 93.5 us
  blocking collectives  58.7 us (63%)
  starting transfers between devices  19.1 us (20%)
  waiting for transfers between devices  9.85 us (10%)
  Pallas kernels  3.51 us (4%)
  local copies, waits for them, and re-layouts  1.39 us (1%)
    all_to_all x1, blocking collectives, local(): near = lax.all_to_all(spread, 'sec', 0, 0, axis_index_groups=same_core)  26.7 us
    all_to_all x1, blocking collectives, local(): received = lax.all_to_all(pieces, 'ops', 0, 0)  19.4 us
    all_to_all x1, blocking collectives, local(): both = lax.all_to_all(both, 'sec', 0, 0)  12.6 us
    ppermute x1, starting transfers between devices, local(): other = lax.ppermute(mine, 'sec', [(s, s ^ 1) for s in range(sec_total)])  5.78 us
    ppermute x1, starting transfers between devices, local(): y_next = lax.ppermute(near[:, :quarter // 2], 'ops', from_y(1))  5.1 us
    ppermute x1, starting transfers between devices, local(): x_next = lax.ppermute(near, 'ops', from_x(1))  4.38 us
    ppermute x1, waiting for transfers between devices, local(): x_last = lax.ppermute(near, 'ops', from_x(-1))  4.34 us
    ppermute x1, waiting for transfers between devices, local(): other = lax.ppermute(mine, 'sec', [(s, s ^ 1) for s in range(sec_total)])  3.68 us
  transfers between devices with their start and end apart: 5, of which 3 were waited for; matrix products, arithmetic and copies ran while one was open for 1% of the time, Pallas kernels for 0%

profile of v4, /device:TPU:1, one launch (start us, length us, event | category | flops | bytes accessed | tf_op | source)
XLA Modules:
  0.0 93.5 jit_solution(10923397641470252670)
XLA Ops:
  0.6 0.9 constant_dynamic-slice_fusion
  1.6 26.7 %all_to_all.15 = bf16[8,2,64,256]{3,2,1,0:T(8,128)(2,1)S(1)} all-to-all(bf16[8,2,64,256]{3,2,1,0:T(8,128)(2,1)S(1)} %broadcast_in_dim.24), channel_id=1, replica_groups={{0,2,4,6,8,10,12,14},{1,3,5,7,9,11,13,15},{16,18,20,22,24,26,28,30},{17..., dimensions={0} | all-to-all | bytes 1048576 | tf_op jit(solution)/shard_map/all_to_all | solution.py:126
  28.2 4.4 %collective-permute-start = (bf16[16,64,256]{2,1,0:T(8,128)(2,1)S(1)}, bf16[16,64,256]{2,1,0:T(8,128)(2,1)S(1)}, u32[]{:S(2)}, u32[]{:S(2)}) collective-permute-start(bf16[16,64,256]{2,1,0:T(8,128)(2,1)S(1)} %bitcast.19), channel_id=1, source_target_pairs={{16,0},{32,16},{48,32},{0,48},{80,64},{96,80},{112,96},{64,112},{1... | collective-permute-start | bytes 1572872 | tf_op jit(solution)/shard_map/ppermute | solution.py:137
  32.6 1.9 %collective-permute-start.1 = (bf16[16,64,256]{2,1,0:T(8,128)(2,1)S(1)}, bf16[16,64,256]{2,1,0:T(8,128)(2,1)S(1)}, u32[]{:S(2)}, u32[]{:S(2)}) collective-permute-start(bf16[16,64,256]{2,1,0:T(8,128)(2,1)S(1)} %bitcast.20), channel_id=1, source_target_pairs={{48,0},{0,16},{16,32},{32,48},{112,64},{64,80},{80,96},{96,112},{1... | collective-permute-start | bytes 1572872 | tf_op jit(solution)/shard_map/ppermute | solution.py:138
  34.6 5.1 %collective-permute-start.2 = (bf16[16,32,256]{2,1,0:T(8,128)(2,1)S(1)}, bf16[16,32,256]{2,1,0:T(8,128)(2,1)S(1)}, u32[]{:S(2)}, u32[]{:S(2)}) collective-permute-start(bf16[16,32,256]{2,1,0:T(8,128)(2,1)S(1)} %get-tuple-element.17), channel_id=1, source_target_pairs={{64,0},{80,16},{96,32},{112,48},{128,64},{144,80},{160,96},{176,11... | collective-permute-start | bytes 786440 | tf_op jit(solution)/shard_map/ppermute | solution.py:139
  39.7 1.9 %collective-permute-start.3 = (bf16[16,32,256]{2,1,0:T(8,128)(2,1)S(1)}, bf16[16,32,256]{2,1,0:T(8,128)(2,1)S(1)}, u32[]{:S(2)}, u32[]{:S(2)}) collective-permute-start(bf16[16,32,256]{2,1,0:T(8,128)(2,1)S(1)} %get-tuple-element.16), channel_id=1, source_target_pairs={{448,0},{464,16},{480,32},{496,48},{0,64},{16,80},{32,96},{48,112}... | collective-permute-start | bytes 786440 | tf_op jit(solution)/shard_map/ppermute | solution.py:140
  41.6 0.0 copy-start.2
  41.7 0.2 broadcast_in_dim.23
  41.9 0.0 copy-start.3
  41.9 0.0 copy-start
  41.9 0.0 copy-start.1
  41.9 0.0 copy-start.4
  42.0 0.0 collective-permute-done
  42.1 4.3 %collective-permute-done.1 = bf16[16,64,256]{2,1,0:T(8,128)(2,1)S(1)} collective-permute-done((bf16[16,64,256]{2,1,0:T(8,128)(2,1)S(1)}, bf16[16,64,256]{2,1,0:T(8,128)(2,1)S(1)}, u32[]{:S(2)}, u32[]{:S(2)}) %collective-permute-start.1) | collective-permute-done | bytes 524320 | tf_op jit(solution)/shard_map/ppermute | solution.py:138
  46.5 0.0 collective-permute-done.2
  46.5 1.8 %collective-permute-done.3 = bf16[16,32,256]{2,1,0:T(8,128)(2,1)S(1)} collective-permute-done((bf16[16,32,256]{2,1,0:T(8,128)(2,1)S(1)}, bf16[16,32,256]{2,1,0:T(8,128)(2,1)S(1)}, u32[]{:S(2)}, u32[]{:S(2)}) %collective-permute-start.3) | collective-permute-done | bytes 262176 | tf_op jit(solution)/shard_map/ppermute | solution.py:140
  48.4 5.8 %collective-permute-start.4 = (bf16[16,256,256]{2,1,0:T(8,128)(2,1)S(1)}, bf16[16,256,256]{2,1,0:T(8,128)(2,1)S(1)}, u32[]{:S(2)}, u32[]{:S(2)}) collective-permute-start(bf16[16,256,256]{2,1,0:T(8,128)(2,1)S(1)} %bitcast.17), channel_id=1, source_target_pairs={{0,1},{1,0},{2,3},{3,2},{4,5},{5,4},{6,7},{7,6},{8,9},{9,8},{10,11... | collective-permute-start | bytes 6291464 | tf_op jit(solution)/shard_map/ppermute | solution.py:148
  54.2 0.0 copy-done.3
  54.2 0.1 fusion.live_all_ref
  54.2 3.7 %collective-permute-done.4.other_ref = bf16[16,256,256]{2,1,0:T(8,128)(2,1)S(1)} collective-permute-done((bf16[16,256,256]{2,1,0:T(8,128)(2,1)S(1)}, bf16[16,256,256]{2,1,0:T(8,128)(2,1)S(1)}, u32[]{:S(2)}, u32[]{:S(2)}) %collective-permute-start.4) | collective-permute-done | bytes 2097184 | tf_op jit(solution)/shard_map/ppermute | solution.py:148
  57.9 0.0 copy-done.2
  57.9 0.0 copy-done
  57.9 0.0 copy-done.1
  57.9 0.0 copy-done.4
  57.9 2.2 %shard_map.68 = (bf16[32,40,128]{2,1,0:T(8,128)(2,1)S(1)}, f32[8,128]{1,0:T(8,128)S(1)}, f32[2,8,256]{2,1,0:T(8,128)S(1)}, f32[2,8,256]{2,1,0:T(8,128)S(1)}) custom-call(s32[8]{0:T(128)S(1)} %copy-done.4, s32[32]{0:T(128)S(1)} %copy-done.3, f32[32,256]{1,0:T(8,128)S(1)} %fusion.live_all_ref, bf16[2,256,256]{2,1,0:T(8,128)(2,1)S(1)} %copy-done.2, ...), custom_call_target="tpu_custom_call" | custom-call | flops 1073741824 | bytes 1048576 | tf_op jit(solution)/shard_map/pallas_call | solution.py:152
  60.1 19.4 %all_to_all.16.received_ref = bf16[32,40,128]{2,1,0:T(8,128)(2,1)S(1)} all-to-all(bf16[32,40,128]{2,1,0:T(8,128)(2,1)S(1)} %get-tuple-element.9), channel_id=1, replica_groups=mesh['ops'=32,'sec'=16] {'ops'}, dimensions={0} | all-to-all | bytes 655360 | tf_op jit(solution)/shard_map/all_to_all | solution.py:171
  79.5 0.7 shard_map.69
  80.2 12.6 %all_to_all.17.both_ref = f32[16,8,128]{2,1,0:T(8,128)S(1)} all-to-all(f32[16,8,128]{2,1,0:T(8,128)S(1)} %get-tuple-element.13), channel_id=1, replica_groups=mesh['ops'=32,'sec'=16] {'sec'}, dimensions={0} | all-to-all | bytes 131072 | tf_op jit(solution)/shard_map/all_to_all | solution.py:184
  92.8 0.7 shard_map.70
  (7 shorter events, 0.3 us)
Async XLA Ops:
  28.2 13.8 %collective-permute-start = (bf16[16,64,256]{2,1,0:T(8,128)(2,1)S(1)}, bf16[16,64,256]{2,1,0:T(8,128)(2,1)S(1)}, u32[]{:S(2)}, u32[]{:S(2)}) collective-permute-start(bf16[16,64,256]{2,1,0:T(8,128)(2,1)S(1)} %bitcast.19), channel_id=1, source_target_pairs={{16,0},{32,16},{48,32},{0,48},{80,64},{96,80},{112,96},{64,112},{1... | collective-permute-start | bytes 1572872 | tf_op jit(solution)/shard_map/ppermute | solution.py:137
  32.6 13.8 %collective-permute-start.1 = (bf16[16,64,256]{2,1,0:T(8,128)(2,1)S(1)}, bf16[16,64,256]{2,1,0:T(8,128)(2,1)S(1)}, u32[]{:S(2)}, u32[]{:S(2)}) collective-permute-start(bf16[16,64,256]{2,1,0:T(8,128)(2,1)S(1)} %bitcast.20), channel_id=1, source_target_pairs={{48,0},{0,16},{16,32},{32,48},{112,64},{64,80},{80,96},{96,112},{1... | collective-permute-start | bytes 1572872 | tf_op jit(solution)/shard_map/ppermute | solution.py:138
  34.6 11.9 %collective-permute-start.2 = (bf16[16,32,256]{2,1,0:T(8,128)(2,1)S(1)}, bf16[16,32,256]{2,1,0:T(8,128)(2,1)S(1)}, u32[]{:S(2)}, u32[]{:S(2)}) collective-permute-start(bf16[16,32,256]{2,1,0:T(8,128)(2,1)S(1)} %get-tuple-element.17), channel_id=1, source_target_pairs={{64,0},{80,16},{96,32},{112,48},{128,64},{144,80},{160,96},{176,11... | collective-permute-start | bytes 786440 | tf_op jit(solution)/shard_map/ppermute | solution.py:139
  39.7 8.6 %collective-permute-start.3 = (bf16[16,32,256]{2,1,0:T(8,128)(2,1)S(1)}, bf16[16,32,256]{2,1,0:T(8,128)(2,1)S(1)}, u32[]{:S(2)}, u32[]{:S(2)}) collective-permute-start(bf16[16,32,256]{2,1,0:T(8,128)(2,1)S(1)} %get-tuple-element.16), channel_id=1, source_target_pairs={{448,0},{464,16},{480,32},{496,48},{0,64},{16,80},{32,96},{48,112}... | collective-permute-start | bytes 786440 | tf_op jit(solution)/shard_map/ppermute | solution.py:140
  41.6 16.3 %copy-start.2 = (bf16[2,256,256]{2,1,0:T(8,128)(2,1)S(1)}, bf16[2,256,256]{2,1,0:T(8,128)(2,1)}, u32[]{:S(2)}) copy-start(bf16[2,256,256]{2,1,0:T(8,128)(2,1)} %psi_ref.1) | copy-start | bytes 786436
  41.9 12.2 %copy-start.3 = (s32[32]{0:T(128)S(1)}, s32[32]{0:T(128)}, u32[]{:S(2)}) copy-start(s32[32]{0:T(128)} %sizes_ref.1) | copy-start | bytes 388
  41.9 16.0 %copy-start = (bf16[8,2,256,256]{3,2,1,0:T(8,128)(2,1)S(1)}, bf16[8,2,256,256]{3,2,1,0:T(8,128)(2,1)}, u32[]{:S(2)}) copy-start(bf16[8,2,256,256]{3,2,1,0:T(8,128)(2,1)} %left_ref.1) | copy-start | bytes 6291460
  41.9 16.0 %copy-start.1 = (bf16[8,2,256,256]{3,2,1,0:T(8,128)(2,1)S(1)}, bf16[8,2,256,256]{3,2,1,0:T(8,128)(2,1)}, u32[]{:S(2)}) copy-start(bf16[8,2,256,256]{3,2,1,0:T(8,128)(2,1)} %right_ref.1) | copy-start | bytes 6291460
  41.9 16.0 %copy-start.4 = (s32[8]{0:T(128)S(1)}, s32[8]{0:T(128)}, u32[]{:S(2)}) copy-start(s32[8]{0:T(128)} %charge_ref.1) | copy-start | bytes 100
  48.4 9.6 %collective-permute-start.4 = (bf16[16,256,256]{2,1,0:T(8,128)(2,1)S(1)}, bf16[16,256,256]{2,1,0:T(8,128)(2,1)S(1)}, u32[]{:S(2)}, u32[]{:S(2)}) collective-permute-start(bf16[16,256,256]{2,1,0:T(8,128)(2,1)S(1)} %bitcast.17), channel_id=1, source_target_pairs={{0,1},{1,0},{2,3},{3,2},{4,5},{5,4},{6,7},{7,6},{8,9},{9,8},{10,11... | collective-permute-start | bytes 6291464 | tf_op jit(solution)/shard_map/ppermute | solution.py:148

commit v5 on v4

--- a/solution.py
+++ b/solution.py
@@ -19,7 +19,7 @@
 
 def sigma_kernel(sectors, rows, factor):
     def body(
-        charge_ref, sizes_ref, live_all_ref, psi_ref, mine_ref, other_ref, left_ref, right_ref,
+        charge_ref, sizes_ref, mine_ref, other_ref, left_ref, right_ref,
         out_ref, norm_ref, own_ref, live_ref, half_buf, own_buf,
     ):
         pairs, here, block, _ = left_ref.shape
@@ -27,15 +27,21 @@
         first = sec * here
         start = pl.multiple_of(lax.axis_index("ops") * rows, rows)
         core = lax.rem(sec, 2)
+        lane = lax.broadcasted_iota(jnp.int32, (1, block), 1)
+
+        def block_of(source):
+            mine, other = mine_ref[source], other_ref[source]
+            upper = jnp.where(core == 0, mine, other)
+            lower = jnp.where(core == 0, other, mine)
+            eighths = [part[q] for q in range(COLOURS) for part in (upper, lower)]
+            return jnp.concatenate(eighths, axis=0)
+
         for p in range(pairs):
             for k in range(here):
                 source = lax.rem(first + k + charge_ref[p], sectors)
-                place = lax.div(source, 2 * here) * here + lax.rem(source, here)
-                across = lax.rem(lax.div(source, here), 2) != core
-                psi = jnp.where(across, other_ref[place], mine_ref[place])
-                live = live_all_ref[pl.ds(source, 1), :]
+                live = jnp.where(lane < sizes_ref[source], 1.0, 0.0)
                 left = left_ref[p, k] * live.astype(jnp.bfloat16)
-                half = jnp.dot(left, psi, preferred_element_type=jnp.float32) * live
+                half = jnp.dot(left, block_of(source), preferred_element_type=jnp.float32) * live
                 half_buf[k, :, p * block : (p + 1) * block] = half.astype(jnp.bfloat16)
         row = lax.broadcasted_iota(jnp.int32, (block, block), 0)
         column = lax.broadcasted_iota(jnp.int32, (block, block), 1)
@@ -53,7 +59,7 @@
                     (((1,), (1,)), ((), ())), preferred_element_type=jnp.float32,
                 )
             total = total * factor
-            psi = jnp.where(farthest < size, psi_ref[k], 0).astype(jnp.float32)
+            psi = jnp.where(farthest < size, block_of(first + k), 0).astype(jnp.float32)
             own_buf[k] = psi
             correlation += jnp.sum(psi * total, keepdims=True)
             norm += jnp.sum(psi * psi, keepdims=True)
@@ -110,42 +116,42 @@
     sectors = block_sizes.shape[0]
     rows = block // ops_count
     quarter = block // COLOURS
+    eighth = quarter // 2
     factor = float(pairs * ops_count) ** (-0.5)
-    chips_z = sec_total // 2
     y_size = ops_count // X_SIZE
     colour = colour_of(lax.axis_index("ops"))
     smem = pl.BlockSpec(memory_space=pltpu.SMEM)
     vmem = pl.BlockSpec(memory_space=pltpu.VMEM)
     bf16, f32 = jnp.bfloat16, jnp.float32
 
-    own_quarter = lax.dynamic_slice_in_dim(wavefunction, colour * quarter, quarter, 1)
-    spread = jnp.broadcast_to(own_quarter[None], (chips_z, *own_quarter.shape))
-    positions = jnp.arange(block, dtype=jnp.int32)
-    live_all = (positions[None, :] < block_sizes[:, None]).astype(f32)
-    same_core = [[2 * z + core for z in range(chips_z)] for core in range(2)]
-    near = lax.all_to_all(spread, "sec", 0, 0, axis_index_groups=same_core)
-    near = near.reshape(chips_z * here, quarter, block)
-
-    def from_x(step):
-        return [(y * X_SIZE + (x + step) % X_SIZE, y * X_SIZE + x)
-                for y in range(y_size) for x in range(X_SIZE)]
-
-    def from_y(step):
-        return [((y + step) % y_size * X_SIZE + x, y * X_SIZE + x)
-                for y in range(y_size) for x in range(X_SIZE)]
-
-    x_next = lax.ppermute(near, "ops", from_x(1))
-    x_last = lax.ppermute(near, "ops", from_x(-1))
-    y_next = lax.ppermute(near[:, : quarter // 2], "ops", from_y(1))
-    y_last = lax.ppermute(near[:, quarter // 2 :], "ops", from_y(-1))
-    mine = jnp.zeros((chips_z * here, COLOURS, quarter, block), bf16)
-    for piece, relative, at in (
-        (near, 0, 0), (x_next, 1, 0), (x_last, 3, 0), (y_next, 2, 0), (y_last, 2, quarter // 2)
-    ):
-        where = (0, lax.rem(colour + relative, COLOURS), at, 0)
+    core = lax.axis_index("sec") % 2
+    own = lax.dynamic_slice_in_dim(wavefunction, colour * quarter, quarter, 1)
+    halves = own.reshape(here, 2, eighth, block).transpose(1, 0, 2, 3)
+    spread = jnp.broadcast_to(halves[None], (sec_total // 2, *halves.shape))
+    spread = spread.reshape(sec_total, here, eighth, block)
+    own = lax.all_to_all(spread, "sec", 0, 0).reshape(sectors, eighth, block)
+
+    def device(x, y, s):
+        return ((y % y_size) * X_SIZE + x % X_SIZE) * sec_total + s
+
+    def fetch(step_x, step_y):
+        pairs = []
+        for y in range(y_size):
+            for x in range(X_SIZE):
+                for s in range(sec_total):
+                    way = 1 - 2 * (s % 2)
+                    pairs.append((device(x + way * step_x, y + way * step_y, s), device(x, y, s)))
+        return lax.ppermute(own, ("ops", "sec"), pairs)
+
+    swap = [(s, s ^ 1) for s in range(sec_total)]
+    mine = jnp.zeros((sectors, COLOURS, eighth, block), bf16)
+    other = mine
+    pieces = ((own, 0, 0), (fetch(1, 0), 1, 2), (fetch(0, 1), 2, 0), (fetch(-1, 0), 3, -2))
+    for piece, relative, way in pieces:
+        where = (0, lax.rem(colour + relative + way * core, COLOURS), 0, 0)
         mine = lax.dynamic_update_slice(mine, piece[:, None], where)
-    mine = mine.reshape(chips_z * here, block, block)
-    other = lax.ppermute(mine, "sec", [(s, s ^ 1) for s in range(sec_total)])
+        where = (0, lax.rem(colour + relative + way * (1 - core), COLOURS), 0, 0)
+        other = lax.dynamic_update_slice(other, lax.ppermute(piece, "sec", swap)[:, None], where)
 
     part = (here, rows, block)
     pack_rows = here * rows * (block // LANES) + rows
@@ -157,7 +163,7 @@
             jax.ShapeDtypeStruct(part, f32),
             jax.ShapeDtypeStruct(part, f32),
         ),
-        in_specs=[smem] * 2 + [vmem] * 6,
+        in_specs=[smem] * 2 + [vmem] * 4,
         out_specs=(vmem,) * 4,
         scratch_shapes=[
             pltpu.VMEM((here, block, pairs * block), bf16),
@@ -167,7 +173,7 @@
         cost_estimate=pl.CostEstimate(
             flops=4 * pairs * here * block**3, bytes_accessed=2**20, transcendentals=0
         ),
-    )(charge, block_sizes, live_all, wavefunction, mine, other, left_ops, right_ops)
+    )(charge, block_sizes, mine, other, left_ops, right_ops)
     received = lax.all_to_all(pieces, "ops", 0, 0)
 
     sigma, wide, both = pl.pallas_call(

time: 93.9 us -> 93.2 us (level)
  waiting for transfers between devices: 9.85 us -> 0.88 us
  starting transfers between devices: 19.1 us -> 22.6 us
  blocking collectives: 58.7 us -> 61.9 us
  local copies, waits for them, and re-layouts: 1.39 us -> 2.95 us
    ppermute x5 -> x7, waiting for transfers between devices: 9.85 us -> 0.88 us  [the longest x4 0.87 us: local(): lax.ppermute(piece, 'sec', swap)[:, None]]
    ppermute x5 -> x7, starting transfers between devices: 19.1 us -> 22.6 us  [the longest x4 12.9 us: local(): lax.ppermute(piece, 'sec', swap)[:, None]]
    all_to_all x1, blocking collectives: 12.6 us -> 15.3 us  [local(): both = lax.all_to_all(both, 'sec', 0, 0)]
    all_to_all x1, blocking collectives: 26.7 us -> 28.9 us  [local(): own = lax.all_to_all(spread, 'sec', 0, 0).reshape(sectors, eighth, block)]
    unnamed x10, local copies, waits for them, and re-layouts: 0.03 us -> 2.03 us
    all_to_all x1, blocking collectives: 19.4 us -> 17.7 us  [local(): received = lax.all_to_all(pieces, 'ops', 0, 0)]
  transfers between devices with their start and end apart: 5 -> 7, of which waited for: 3 -> 1; matrix products, arithmetic and copies ran while one was open for 1% -> 1% of each run, Pallas kernels for 0% -> 0%
where the time goes in v5:
time: 93.2 us; the launch traced here: 92.8 us
  blocking collectives  61.9 us (66%)
  starting transfers between devices  22.6 us (24%)
  Pallas kernels  3.46 us (4%)
  local copies, waits for them, and re-layouts  2.95 us (3%)
  between operations  0.98 us (1%)
    all_to_all x1, blocking collectives, local(): own = lax.all_to_all(spread, 'sec', 0, 0).reshape(sectors, eighth, block)  28.9 us
    all_to_all x1, blocking collectives, local(): received = lax.all_to_all(pieces, 'ops', 0, 0)  17.7 us
    all_to_all x1, blocking collectives, local(): both = lax.all_to_all(both, 'sec', 0, 0)  15.3 us
    ppermute x4, starting transfers between devices, local(): lax.ppermute(piece, 'sec', swap)[:, None]  12.9 us
    ppermute x3, starting transfers between devices, fetch(): return lax.ppermute(own, ('ops', 'sec'), pairs)  9.69 us
    pallas_call x1, Pallas kernels, local(): pl.pallas_call(sigma_kernel(sectors, rows, factor), out_shape=(jax.ShapeD...  2.15 us
    unnamed x10, local copies, waits for them, and re-layouts  2.03 us
  transfers between devices with their start and end apart: 7, of which 1 were waited for; matrix products, arithmetic and copies ran while one was open for 1% of the time, Pallas kernels for 0%

profile of v5, /device:TPU:1, one launch (start us, length us, event | category | flops | bytes accessed | tf_op | source)
XLA Modules:
  0.0 92.8 jit_solution(6635112795451424055)
XLA Ops:
  0.6 0.0 copy-start
  0.7 0.9 copy-done
  1.6 0.1 broadcast_in_dim.31
  1.7 28.9 %all_to_all.15 = bf16[16,2,32,256]{3,2,1,0:T(8,128)(2,1)S(1)} all-to-all(bf16[16,2,32,256]{3,2,1,0:T(8,128)(2,1)S(1)} %bitcast.37), channel_id=1, replica_groups=mesh['ops'=32,'sec'=16] {'sec'}, dimensions={0} | all-to-all | bytes 1048576 | tf_op jit(solution)/shard_map/all_to_all | solution.py:132
  30.6 3.1 %collective-permute-start = (bf16[32,32,256]{2,1,0:T(8,128)(2,1)S(1)}, bf16[32,32,256]{2,1,0:T(8,128)(2,1)S(1)}, u32[]{:S(2)}, u32[]{:S(2)}) collective-permute-start(bf16[32,32,256]{2,1,0:T(8,128)(2,1)S(1)} %bitcast.32), channel_id=1, source_target_pairs={{16,0},{49,1},{18,2},{51,3},{20,4},{53,5},{22,6},{55,7},{24,8},{57... | collective-permute-start | bytes 1572872 | tf_op jit(solution)/shard_map/ppermute | solution.py:144
  33.7 3.2 %collective-permute-start.1 = (bf16[32,32,256]{2,1,0:T(8,128)(2,1)S(1)}, bf16[32,32,256]{2,1,0:T(8,128)(2,1)S(1)}, u32[]{:S(2)}, u32[]{:S(2)}) collective-permute-start(bf16[32,32,256]{2,1,0:T(8,128)(2,1)S(1)} %bitcast.33), channel_id=1, source_target_pairs={{64,0},{449,1},{66,2},{451,3},{68,4},{453,5},{70,6},{455,7},{72,8}... | collective-permute-start | bytes 1572872 | tf_op jit(solution)/shard_map/ppermute | solution.py:144
  36.9 3.4 %collective-permute-start.2 = (bf16[32,32,256]{2,1,0:T(8,128)(2,1)S(1)}, bf16[32,32,256]{2,1,0:T(8,128)(2,1)S(1)}, u32[]{:S(2)}, u32[]{:S(2)}) collective-permute-start(bf16[32,32,256]{2,1,0:T(8,128)(2,1)S(1)} %bitcast.34), channel_id=1, source_target_pairs={{48,0},{17,1},{50,2},{19,3},{52,4},{21,5},{54,6},{23,7},{56,8},{25... | collective-permute-start | bytes 1572872 | tf_op jit(solution)/shard_map/ppermute | solution.py:144
  40.3 3.0 %collective-permute-start.3 = (bf16[32,32,256]{2,1,0:T(8,128)(2,1)S(1)}, bf16[32,32,256]{2,1,0:T(8,128)(2,1)S(1)}, u32[]{:S(2)}, u32[]{:S(2)}) collective-permute-start(bf16[32,32,256]{2,1,0:T(8,128)(2,1)S(1)} %bitcast.35), channel_id=1, source_target_pairs={{0,1},{1,0},{2,3},{3,2},{4,5},{5,4},{6,7},{7,6},{8,9},{9,8},{10,11... | collective-permute-start | bytes 1572872 | tf_op jit(solution)/shard_map/ppermute | solution.py:154
  43.4 0.3 broadcast_in_dim.30.clone
  43.7 0.0 collective-permute-done
  43.7 1.9 %collective-permute-start.4 = (bf16[32,32,256]{2,1,0:T(8,128)(2,1)S(1)}, bf16[32,32,256]{2,1,0:T(8,128)(2,1)S(1)}, u32[]{:S(2)}, u32[]{:S(2)}) collective-permute-start(bf16[32,32,256]{2,1,0:T(8,128)(2,1)S(1)} %collective-permute-done), channel_id=1, source_target_pairs={{0,1},{1,0},{2,3},{3,2},{4,5},{5,4},{6,7},{7,6},{8,9},{9,8},{10,11... | collective-permute-start | bytes 1572872 | tf_op jit(solution)/shard_map/ppermute | solution.py:154
  45.6 0.0 collective-permute-done.1
  45.7 2.4 %collective-permute-start.5 = (bf16[32,32,256]{2,1,0:T(8,128)(2,1)S(1)}, bf16[32,32,256]{2,1,0:T(8,128)(2,1)S(1)}, u32[]{:S(2)}, u32[]{:S(2)}) collective-permute-start(bf16[32,32,256]{2,1,0:T(8,128)(2,1)S(1)} %collective-permute-done.1), channel_id=1, source_target_pairs={{0,1},{1,0},{2,3},{3,2},{4,5},{5,4},{6,7},{7,6},{8,9},{9,8},{10,11... | collective-permute-start | bytes 1572872 | tf_op jit(solution)/shard_map/ppermute | solution.py:154
  48.1 0.0 collective-permute-done.2
  48.1 5.6 %collective-permute-start.6 = (bf16[32,32,256]{2,1,0:T(8,128)(2,1)S(1)}, bf16[32,32,256]{2,1,0:T(8,128)(2,1)S(1)}, u32[]{:S(2)}, u32[]{:S(2)}) collective-permute-start(bf16[32,32,256]{2,1,0:T(8,128)(2,1)S(1)} %collective-permute-done.2), channel_id=1, source_target_pairs={{0,1},{1,0},{2,3},{3,2},{4,5},{5,4},{6,7},{7,6},{8,9},{9,8},{10,11... | collective-permute-start | bytes 1572872 | tf_op jit(solution)/shard_map/ppermute | solution.py:154
  53.6 0.0 collective-permute-done.3
  53.7 0.3 broadcast_in_dim.30.clone.1
  54.1 0.0 copy-start.1
  54.1 0.0 copy-start.2
  54.1 0.0 copy-start.3
  54.1 0.0 copy-start.4
  54.2 0.0 collective-permute-done.4
  54.2 0.0 collective-permute-done.5
  54.3 0.9 collective-permute-done.6
  55.2 0.5 copy-done.1
  55.7 0.6 copy-done.2
  56.3 0.0 copy-done.3
  56.3 0.0 copy-done.4
  56.3 2.2 %shard_map.68 = (bf16[32,40,128]{2,1,0:T(8,128)(2,1)S(1)}, f32[8,128]{1,0:T(8,128)S(1)}, f32[2,8,256]{2,1,0:T(8,128)S(1)}, f32[2,8,256]{2,1,0:T(8,128)S(1)}) custom-call(s32[8]{0:T(128)S(1)} %copy-done.3, s32[32]{0:T(128)S(1)} %copy-done.4, bf16[32,4,32,256]{3,2,1,0:T(8,128)(2,1)S(1)} %bitcast_dynamic-update-slice_fusion.3.mine_ref, ...), custom_call_target="tpu_custom_call" | custom-call | flops 1073741824 | bytes 1048576 | tf_op jit(solution)/shard_map/pallas_call | solution.py:158
  58.5 17.7 %all_to_all.16.received_ref = bf16[32,40,128]{2,1,0:T(8,128)(2,1)S(1)} all-to-all(bf16[32,40,128]{2,1,0:T(8,128)(2,1)S(1)} %get-tuple-element.9), channel_id=1, replica_groups=mesh['ops'=32,'sec'=16] {'ops'}, dimensions={0} | all-to-all | bytes 655360 | tf_op jit(solution)/shard_map/all_to_all | solution.py:177
  76.1 0.7 shard_map.69
  76.8 15.3 %all_to_all.17.both_ref = f32[16,8,128]{2,1,0:T(8,128)S(1)} all-to-all(f32[16,8,128]{2,1,0:T(8,128)S(1)} %get-tuple-element.13), channel_id=1, replica_groups=mesh['ops'=32,'sec'=16] {'sec'}, dimensions={0} | all-to-all | bytes 131072 | tf_op jit(solution)/shard_map/all_to_all | solution.py:190
  92.1 0.7 shard_map.70
  (10 shorter events, 0.4 us)
Async XLA Ops:
  0.6 1.0 %copy-start = (bf16[2,256,256]{2,1,0:T(8,128)(2,1)S(1)}, bf16[2,256,256]{2,1,0:T(8,128)(2,1)}, u32[]{:S(2)}) copy-start(bf16[2,256,256]{2,1,0:T(8,128)(2,1)} %param.5) | copy-start | bytes 786436
  30.6 13.1 %collective-permute-start = (bf16[32,32,256]{2,1,0:T(8,128)(2,1)S(1)}, bf16[32,32,256]{2,1,0:T(8,128)(2,1)S(1)}, u32[]{:S(2)}, u32[]{:S(2)}) collective-permute-start(bf16[32,32,256]{2,1,0:T(8,128)(2,1)S(1)} %bitcast.32), channel_id=1, source_target_pairs={{16,0},{49,1},{18,2},{51,3},{20,4},{53,5},{22,6},{55,7},{24,8},{57... | collective-permute-start | bytes 1572872 | tf_op jit(solution)/shard_map/ppermute | solution.py:144
  33.7 11.9 %collective-permute-start.1 = (bf16[32,32,256]{2,1,0:T(8,128)(2,1)S(1)}, bf16[32,32,256]{2,1,0:T(8,128)(2,1)S(1)}, u32[]{:S(2)}, u32[]{:S(2)}) collective-permute-start(bf16[32,32,256]{2,1,0:T(8,128)(2,1)S(1)} %bitcast.33), channel_id=1, source_target_pairs={{64,0},{449,1},{66,2},{451,3},{68,4},{453,5},{70,6},{455,7},{72,8}... | collective-permute-start | bytes 1572872 | tf_op jit(solution)/shard_map/ppermute | solution.py:144
  36.9 11.1 %collective-permute-start.2 = (bf16[32,32,256]{2,1,0:T(8,128)(2,1)S(1)}, bf16[32,32,256]{2,1,0:T(8,128)(2,1)S(1)}, u32[]{:S(2)}, u32[]{:S(2)}) collective-permute-start(bf16[32,32,256]{2,1,0:T(8,128)(2,1)S(1)} %bitcast.34), channel_id=1, source_target_pairs={{48,0},{17,1},{50,2},{19,3},{52,4},{21,5},{54,6},{23,7},{56,8},{25... | collective-permute-start | bytes 1572872 | tf_op jit(solution)/shard_map/ppermute | solution.py:144
  40.3 13.3 %collective-permute-start.3 = (bf16[32,32,256]{2,1,0:T(8,128)(2,1)S(1)}, bf16[32,32,256]{2,1,0:T(8,128)(2,1)S(1)}, u32[]{:S(2)}, u32[]{:S(2)}) collective-permute-start(bf16[32,32,256]{2,1,0:T(8,128)(2,1)S(1)} %bitcast.35), channel_id=1, source_target_pairs={{0,1},{1,0},{2,3},{3,2},{4,5},{5,4},{6,7},{7,6},{8,9},{9,8},{10,11... | collective-permute-start | bytes 1572872 | tf_op jit(solution)/shard_map/ppermute | solution.py:154
  43.7 10.5 %collective-permute-start.4 = (bf16[32,32,256]{2,1,0:T(8,128)(2,1)S(1)}, bf16[32,32,256]{2,1,0:T(8,128)(2,1)S(1)}, u32[]{:S(2)}, u32[]{:S(2)}) collective-permute-start(bf16[32,32,256]{2,1,0:T(8,128)(2,1)S(1)} %collective-permute-done), channel_id=1, source_target_pairs={{0,1},{1,0},{2,3},{3,2},{4,5},{5,4},{6,7},{7,6},{8,9},{9,8},{10,11... | collective-permute-start | bytes 1572872 | tf_op jit(solution)/shard_map/ppermute | solution.py:154
  45.7 8.6 %collective-permute-start.5 = (bf16[32,32,256]{2,1,0:T(8,128)(2,1)S(1)}, bf16[32,32,256]{2,1,0:T(8,128)(2,1)S(1)}, u32[]{:S(2)}, u32[]{:S(2)}) collective-permute-start(bf16[32,32,256]{2,1,0:T(8,128)(2,1)S(1)} %collective-permute-done.1), channel_id=1, source_target_pairs={{0,1},{1,0},{2,3},{3,2},{4,5},{5,4},{6,7},{7,6},{8,9},{9,8},{10,11... | collective-permute-start | bytes 1572872 | tf_op jit(solution)/shard_map/ppermute | solution.py:154
  48.1 7.1 %collective-permute-start.6 = (bf16[32,32,256]{2,1,0:T(8,128)(2,1)S(1)}, bf16[32,32,256]{2,1,0:T(8,128)(2,1)S(1)}, u32[]{:S(2)}, u32[]{:S(2)}) collective-permute-start(bf16[32,32,256]{2,1,0:T(8,128)(2,1)S(1)} %collective-permute-done.2), channel_id=1, source_target_pairs={{0,1},{1,0},{2,3},{3,2},{4,5},{5,4},{6,7},{7,6},{8,9},{9,8},{10,11... | collective-permute-start | bytes 1572872 | tf_op jit(solution)/shard_map/ppermute | solution.py:154
  54.1 1.6 %copy-start.1 = (bf16[8,2,256,256]{3,2,1,0:T(8,128)(2,1)S(1)}, bf16[8,2,256,256]{3,2,1,0:T(8,128)(2,1)}, u32[]{:S(2)}) copy-start(bf16[8,2,256,256]{3,2,1,0:T(8,128)(2,1)} %left_ref.1) | copy-start | bytes 6291460
  54.1 2.2 %copy-start.2 = (bf16[8,2,256,256]{3,2,1,0:T(8,128)(2,1)S(1)}, bf16[8,2,256,256]{3,2,1,0:T(8,128)(2,1)}, u32[]{:S(2)}) copy-start(bf16[8,2,256,256]{3,2,1,0:T(8,128)(2,1)} %right_ref.1) | copy-start | bytes 6291460
  54.1 2.2 %copy-start.3 = (s32[8]{0:T(128)S(1)}, s32[8]{0:T(128)}, u32[]{:S(2)}) copy-start(s32[8]{0:T(128)} %charge_ref.1) | copy-start | bytes 100
  54.1 2.2 %copy-start.4 = (s32[32]{0:T(128)S(1)}, s32[32]{0:T(128)}, u32[]{:S(2)}) copy-start(s32[32]{0:T(128)} %sizes_ref.1) | copy-start | bytes 388

commit v6 on v5

--- a/solution.py
+++ b/solution.py
@@ -14,7 +14,7 @@
 
 
 def colour_of(slot):
-    return lax.rem(lax.rem(slot, X_SIZE) + 2 * lax.div(slot, X_SIZE), COLOURS)
+    return lax.rem(2 * lax.rem(slot, X_SIZE) + lax.div(slot, X_SIZE), COLOURS)
 
 
 def sigma_kernel(sectors, rows, factor):
@@ -85,7 +85,7 @@
     return body
 
 
-def sum_kernel(received_ref, norm_ref, live_ref, sigma_ref, wide_ref, both_ref):
+def sum_kernel(received_ref, norm_ref, live_ref, wide_ref, both_ref):
     here, rows, block = wide_ref.shape
     summed = jnp.sum(received_ref[...].astype(jnp.float32), axis=0)
     parts = block // LANES
@@ -98,12 +98,12 @@
             at, lanes = (part * here + k) * rows, slice(part * LANES, (part + 1) * LANES)
             kept = jnp.where(live_ref[k, :, lanes] > 0, summed[at : at + rows], 0.0)
             wide_ref[k, :, lanes] = kept
-            sigma_ref[k, :, lanes] = kept.astype(jnp.bfloat16)
-
-
-def residual_kernel(both_ref, wide_ref, own_ref, out_ref):
+
+
+def residual_kernel(both_ref, wide_ref, own_ref, sigma_ref, out_ref):
     both = jnp.sum(both_ref[...], axis=0)
     ritz_value = both[0:1, 0:1] / both[1:2, 0:1]
+    sigma_ref[...] = wide_ref[...].astype(jnp.bfloat16)
     for k in range(wide_ref.shape[0]):
         out_ref[k] = (wide_ref[k] - ritz_value * own_ref[k]).astype(jnp.bfloat16)
 
@@ -146,7 +146,7 @@
     swap = [(s, s ^ 1) for s in range(sec_total)]
     mine = jnp.zeros((sectors, COLOURS, eighth, block), bf16)
     other = mine
-    pieces = ((own, 0, 0), (fetch(1, 0), 1, 2), (fetch(0, 1), 2, 0), (fetch(-1, 0), 3, -2))
+    pieces = ((own, 0, 0), (fetch(0, 1), 1, 2), (fetch(1, 0), 2, 0), (fetch(0, -1), 3, -2))
     for piece, relative, way in pieces:
         where = (0, lax.rem(colour + relative + way * core, COLOURS), 0, 0)
         mine = lax.dynamic_update_slice(mine, piece[:, None], where)
@@ -176,26 +176,24 @@
     )(charge, block_sizes, mine, other, left_ops, right_ops)
     received = lax.all_to_all(pieces, "ops", 0, 0)
 
-    sigma, wide, both = pl.pallas_call(
+    wide, both = pl.pallas_call(
         sum_kernel,
         out_shape=(
-            jax.ShapeDtypeStruct(part, bf16),
             jax.ShapeDtypeStruct(part, f32),
             jax.ShapeDtypeStruct((sec_total, SUBLANES, LANES), f32),
         ),
         in_specs=[vmem] * 3,
-        out_specs=(vmem,) * 3,
+        out_specs=(vmem,) * 2,
         compiler_params=SMALL,
     )(received, norm, live)
     both = lax.all_to_all(both, "sec", 0, 0)
-    residual = pl.pallas_call(
+    return pl.pallas_call(
         residual_kernel,
-        out_shape=jax.ShapeDtypeStruct(part, bf16),
+        out_shape=(jax.ShapeDtypeStruct(part, bf16),) * 2,
         in_specs=[vmem] * 3,
-        out_specs=vmem,
+        out_specs=(vmem,) * 2,
         compiler_params=SMALL,
     )(both, wide, own_rows)
-    return sigma, residual
 
 
 def solution(mesh):

time: 93.2 us -> 91.5 us (0.982)
  blocking collectives: 61.9 us -> 60.8 us
    all_to_all x1, blocking collectives: 15.3 us -> 13.3 us  [local(): both = lax.all_to_all(both, 'sec', 0, 0)]
where the time goes in v6:
time: 91.5 us; the launch traced here: 91.1 us
  blocking collectives  60.8 us (66%)
  starting transfers between devices  22.6 us (25%)
  Pallas kernels  2.97 us (3%)
  local copies, waits for them, and re-layouts  2.95 us (3%)
  between operations  0.99 us (1%)
    all_to_all x1, blocking collectives, local(): own = lax.all_to_all(spread, 'sec', 0, 0).reshape(sectors, eighth, block)  28.9 us
    all_to_all x1, blocking collectives, local(): received = lax.all_to_all(pieces, 'ops', 0, 0)  18.6 us
    all_to_all x1, blocking collectives, local(): both = lax.all_to_all(both, 'sec', 0, 0)  13.3 us
    ppermute x4, starting transfers between devices, local(): lax.ppermute(piece, 'sec', swap)[:, None]  12.4 us
    ppermute x3, starting transfers between devices, fetch(): return lax.ppermute(own, ('ops', 'sec'), pairs)  10.1 us
    pallas_call x1, Pallas kernels, local(): pl.pallas_call(sigma_kernel(sectors, rows, factor), out_shape=(jax.ShapeD...  2.15 us
    unnamed x10, local copies, waits for them, and re-layouts  2.03 us
  transfers between devices with their start and end apart: 7, of which 1 were waited for; matrix products, arithmetic and copies ran while one was open for 1% of the time, Pallas kernels for 0%

profile of v6, /device:TPU:1, one launch (start us, length us, event | category | flops | bytes accessed | tf_op | source)
XLA Modules:
  0.0 91.1 jit_solution(16984063432953042010)
XLA Ops:
  0.6 0.0 copy-start
  0.7 0.9 %copy-done = bf16[2,256,256]{2,1,0:T(8,128)(2,1)S(1)} copy-done((bf16[2,256,256]{2,1,0:T(8,128)(2,1)S(1)}, bf16[2,256,256]{2,1,0:T(8,128)(2,1)}, u32[]{:S(2)}) %copy-start) | copy-done | bytes 262168
  1.6 0.1 broadcast_in_dim.31
  1.7 28.9 %all_to_all.15 = bf16[16,2,32,256]{3,2,1,0:T(8,128)(2,1)S(1)} all-to-all(bf16[16,2,32,256]{3,2,1,0:T(8,128)(2,1)S(1)} %bitcast.37), channel_id=1, replica_groups=mesh['ops'=32,'sec'=16] {'sec'}, dimensions={0} | all-to-all | bytes 1048576 | tf_op jit(solution)/shard_map/all_to_all | solution.py:132
  30.6 3.2 %collective-permute-start = (bf16[32,32,256]{2,1,0:T(8,128)(2,1)S(1)}, bf16[32,32,256]{2,1,0:T(8,128)(2,1)S(1)}, u32[]{:S(2)}, u32[]{:S(2)}) collective-permute-start(bf16[32,32,256]{2,1,0:T(8,128)(2,1)S(1)} %bitcast.32), channel_id=1, source_target_pairs={{64,0},{449,1},{66,2},{451,3},{68,4},{453,5},{70,6},{455,7},{72,8}... | collective-permute-start | bytes 1572872 | tf_op jit(solution)/shard_map/ppermute | solution.py:144
  33.8 3.1 %collective-permute-start.1 = (bf16[32,32,256]{2,1,0:T(8,128)(2,1)S(1)}, bf16[32,32,256]{2,1,0:T(8,128)(2,1)S(1)}, u32[]{:S(2)}, u32[]{:S(2)}) collective-permute-start(bf16[32,32,256]{2,1,0:T(8,128)(2,1)S(1)} %bitcast.33), channel_id=1, source_target_pairs={{16,0},{49,1},{18,2},{51,3},{20,4},{53,5},{22,6},{55,7},{24,8},{57... | collective-permute-start | bytes 1572872 | tf_op jit(solution)/shard_map/ppermute | solution.py:144
  36.9 3.8 %collective-permute-start.2 = (bf16[32,32,256]{2,1,0:T(8,128)(2,1)S(1)}, bf16[32,32,256]{2,1,0:T(8,128)(2,1)S(1)}, u32[]{:S(2)}, u32[]{:S(2)}) collective-permute-start(bf16[32,32,256]{2,1,0:T(8,128)(2,1)S(1)} %bitcast.34), channel_id=1, source_target_pairs={{448,0},{65,1},{450,2},{67,3},{452,4},{69,5},{454,6},{71,7},{456,8... | collective-permute-start | bytes 1572872 | tf_op jit(solution)/shard_map/ppermute | solution.py:144
  40.8 2.5 %collective-permute-start.3 = (bf16[32,32,256]{2,1,0:T(8,128)(2,1)S(1)}, bf16[32,32,256]{2,1,0:T(8,128)(2,1)S(1)}, u32[]{:S(2)}, u32[]{:S(2)}) collective-permute-start(bf16[32,32,256]{2,1,0:T(8,128)(2,1)S(1)} %bitcast.35), channel_id=1, source_target_pairs={{0,1},{1,0},{2,3},{3,2},{4,5},{5,4},{6,7},{7,6},{8,9},{9,8},{10,11... | collective-permute-start | bytes 1572872 | tf_op jit(solution)/shard_map/ppermute | solution.py:154
  43.4 0.3 broadcast_in_dim.30.clone
  43.7 0.0 collective-permute-done
  43.7 1.9 %collective-permute-start.4 = (bf16[32,32,256]{2,1,0:T(8,128)(2,1)S(1)}, bf16[32,32,256]{2,1,0:T(8,128)(2,1)S(1)}, u32[]{:S(2)}, u32[]{:S(2)}) collective-permute-start(bf16[32,32,256]{2,1,0:T(8,128)(2,1)S(1)} %collective-permute-done), channel_id=1, source_target_pairs={{0,1},{1,0},{2,3},{3,2},{4,5},{5,4},{6,7},{7,6},{8,9},{9,8},{10,11... | collective-permute-start | bytes 1572872 | tf_op jit(solution)/shard_map/ppermute | solution.py:154
  45.6 0.0 collective-permute-done.1
  45.7 2.4 %collective-permute-start.5 = (bf16[32,32,256]{2,1,0:T(8,128)(2,1)S(1)}, bf16[32,32,256]{2,1,0:T(8,128)(2,1)S(1)}, u32[]{:S(2)}, u32[]{:S(2)}) collective-permute-start(bf16[32,32,256]{2,1,0:T(8,128)(2,1)S(1)} %collective-permute-done.1), channel_id=1, source_target_pairs={{0,1},{1,0},{2,3},{3,2},{4,5},{5,4},{6,7},{7,6},{8,9},{9,8},{10,11... | collective-permute-start | bytes 1572872 | tf_op jit(solution)/shard_map/ppermute | solution.py:154
  48.1 0.0 collective-permute-done.2
  48.1 5.6 %collective-permute-start.6 = (bf16[32,32,256]{2,1,0:T(8,128)(2,1)S(1)}, bf16[32,32,256]{2,1,0:T(8,128)(2,1)S(1)}, u32[]{:S(2)}, u32[]{:S(2)}) collective-permute-start(bf16[32,32,256]{2,1,0:T(8,128)(2,1)S(1)} %collective-permute-done.2), channel_id=1, source_target_pairs={{0,1},{1,0},{2,3},{3,2},{4,5},{5,4},{6,7},{7,6},{8,9},{9,8},{10,11... | collective-permute-start | bytes 1572872 | tf_op jit(solution)/shard_map/ppermute | solution.py:154
  53.6 0.0 collective-permute-done.3
  53.7 0.3 broadcast_in_dim.30.clone.1
  54.1 0.0 copy-start.1
  54.1 0.0 copy-start.2
  54.1 0.0 copy-start.3
  54.1 0.0 copy-start.4
  54.2 0.0 collective-permute-done.4
  54.2 0.0 collective-permute-done.5
  54.3 0.9 collective-permute-done.6
  55.2 0.5 copy-done.1
  55.7 0.6 copy-done.2
  56.3 0.0 copy-done.3
  56.3 0.0 copy-done.4
  56.3 2.2 %shard_map.68 = (bf16[32,40,128]{2,1,0:T(8,128)(2,1)S(1)}, f32[8,128]{1,0:T(8,128)S(1)}, f32[2,8,256]{2,1,0:T(8,128)S(1)}, f32[2,8,256]{2,1,0:T(8,128)S(1)}) custom-call(s32[8]{0:T(128)S(1)} %copy-done.3, s32[32]{0:T(128)S(1)} %copy-done.4, bf16[32,4,32,256]{3,2,1,0:T(8,128)(2,1)S(1)} %bitcast_dynamic-update-slice_fusion.3.mine_ref, ...), custom_call_target="tpu_custom_call" | custom-call | flops 1073741824 | bytes 1048576 | tf_op jit(solution)/shard_map/pallas_call | solution.py:158
  58.5 18.6 %all_to_all.16.received_ref = bf16[32,40,128]{2,1,0:T(8,128)(2,1)S(1)} all-to-all(bf16[32,40,128]{2,1,0:T(8,128)(2,1)S(1)} %get-tuple-element.8), channel_id=1, replica_groups=mesh['ops'=32,'sec'=16] {'ops'}, dimensions={0} | all-to-all | bytes 655360 | tf_op jit(solution)/shard_map/all_to_all | solution.py:177
  77.0 0.2 shard_map.69
  77.2 13.3 %all_to_all.17.both_ref = f32[16,8,128]{2,1,0:T(8,128)S(1)} all-to-all(f32[16,8,128]{2,1,0:T(8,128)S(1)} %get-tuple-element.11), channel_id=1, replica_groups=mesh['ops'=32,'sec'=16] {'sec'}, dimensions={0} | all-to-all | bytes 131072 | tf_op jit(solution)/shard_map/all_to_all | solution.py:189
  90.4 0.7 shard_map.70
  (10 shorter events, 0.4 us)
Async XLA Ops:
  0.6 1.0 %copy-start = (bf16[2,256,256]{2,1,0:T(8,128)(2,1)S(1)}, bf16[2,256,256]{2,1,0:T(8,128)(2,1)}, u32[]{:S(2)}) copy-start(bf16[2,256,256]{2,1,0:T(8,128)(2,1)} %param.5) | copy-start | bytes 786436
  30.6 13.1 %collective-permute-start = (bf16[32,32,256]{2,1,0:T(8,128)(2,1)S(1)}, bf16[32,32,256]{2,1,0:T(8,128)(2,1)S(1)}, u32[]{:S(2)}, u32[]{:S(2)}) collective-permute-start(bf16[32,32,256]{2,1,0:T(8,128)(2,1)S(1)} %bitcast.32), channel_id=1, source_target_pairs={{64,0},{449,1},{66,2},{451,3},{68,4},{453,5},{70,6},{455,7},{72,8}... | collective-permute-start | bytes 1572872 | tf_op jit(solution)/shard_map/ppermute | solution.py:144
  33.8 11.8 %collective-permute-start.1 = (bf16[32,32,256]{2,1,0:T(8,128)(2,1)S(1)}, bf16[32,32,256]{2,1,0:T(8,128)(2,1)S(1)}, u32[]{:S(2)}, u32[]{:S(2)}) collective-permute-start(bf16[32,32,256]{2,1,0:T(8,128)(2,1)S(1)} %bitcast.33), channel_id=1, source_target_pairs={{16,0},{49,1},{18,2},{51,3},{20,4},{53,5},{22,6},{55,7},{24,8},{57... | collective-permute-start | bytes 1572872 | tf_op jit(solution)/shard_map/ppermute | solution.py:144
  36.9 11.1 %collective-permute-start.2 = (bf16[32,32,256]{2,1,0:T(8,128)(2,1)S(1)}, bf16[32,32,256]{2,1,0:T(8,128)(2,1)S(1)}, u32[]{:S(2)}, u32[]{:S(2)}) collective-permute-start(bf16[32,32,256]{2,1,0:T(8,128)(2,1)S(1)} %bitcast.34), channel_id=1, source_target_pairs={{448,0},{65,1},{450,2},{67,3},{452,4},{69,5},{454,6},{71,7},{456,8... | collective-permute-start | bytes 1572872 | tf_op jit(solution)/shard_map/ppermute | solution.py:144
  40.8 12.9 %collective-permute-start.3 = (bf16[32,32,256]{2,1,0:T(8,128)(2,1)S(1)}, bf16[32,32,256]{2,1,0:T(8,128)(2,1)S(1)}, u32[]{:S(2)}, u32[]{:S(2)}) collective-permute-start(bf16[32,32,256]{2,1,0:T(8,128)(2,1)S(1)} %bitcast.35), channel_id=1, source_target_pairs={{0,1},{1,0},{2,3},{3,2},{4,5},{5,4},{6,7},{7,6},{8,9},{9,8},{10,11... | collective-permute-start | bytes 1572872 | tf_op jit(solution)/shard_map/ppermute | solution.py:154
  43.7 10.5 %collective-permute-start.4 = (bf16[32,32,256]{2,1,0:T(8,128)(2,1)S(1)}, bf16[32,32,256]{2,1,0:T(8,128)(2,1)S(1)}, u32[]{:S(2)}, u32[]{:S(2)}) collective-permute-start(bf16[32,32,256]{2,1,0:T(8,128)(2,1)S(1)} %collective-permute-done), channel_id=1, source_target_pairs={{0,1},{1,0},{2,3},{3,2},{4,5},{5,4},{6,7},{7,6},{8,9},{9,8},{10,11... | collective-permute-start | bytes 1572872 | tf_op jit(solution)/shard_map/ppermute | solution.py:154
  45.7 8.6 %collective-permute-start.5 = (bf16[32,32,256]{2,1,0:T(8,128)(2,1)S(1)}, bf16[32,32,256]{2,1,0:T(8,128)(2,1)S(1)}, u32[]{:S(2)}, u32[]{:S(2)}) collective-permute-start(bf16[32,32,256]{2,1,0:T(8,128)(2,1)S(1)} %collective-permute-done.1), channel_id=1, source_target_pairs={{0,1},{1,0},{2,3},{3,2},{4,5},{5,4},{6,7},{7,6},{8,9},{9,8},{10,11... | collective-permute-start | bytes 1572872 | tf_op jit(solution)/shard_map/ppermute | solution.py:154
  48.1 7.1 %collective-permute-start.6 = (bf16[32,32,256]{2,1,0:T(8,128)(2,1)S(1)}, bf16[32,32,256]{2,1,0:T(8,128)(2,1)S(1)}, u32[]{:S(2)}, u32[]{:S(2)}) collective-permute-start(bf16[32,32,256]{2,1,0:T(8,128)(2,1)S(1)} %collective-permute-done.2), channel_id=1, source_target_pairs={{0,1},{1,0},{2,3},{3,2},{4,5},{5,4},{6,7},{7,6},{8,9},{9,8},{10,11... | collective-permute-start | bytes 1572872 | tf_op jit(solution)/shard_map/ppermute | solution.py:154
  54.1 1.6 %copy-start.1 = (bf16[8,2,256,256]{3,2,1,0:T(8,128)(2,1)S(1)}, bf16[8,2,256,256]{3,2,1,0:T(8,128)(2,1)}, u32[]{:S(2)}) copy-start(bf16[8,2,256,256]{3,2,1,0:T(8,128)(2,1)} %left_ref.1) | copy-start | bytes 6291460
  54.1 2.2 %copy-start.2 = (bf16[8,2,256,256]{3,2,1,0:T(8,128)(2,1)S(1)}, bf16[8,2,256,256]{3,2,1,0:T(8,128)(2,1)}, u32[]{:S(2)}) copy-start(bf16[8,2,256,256]{3,2,1,0:T(8,128)(2,1)} %right_ref.1) | copy-start | bytes 6291460
  54.1 2.2 %copy-start.3 = (s32[8]{0:T(128)S(1)}, s32[8]{0:T(128)}, u32[]{:S(2)}) copy-start(s32[8]{0:T(128)} %charge_ref.1) | copy-start | bytes 100
  54.1 2.2 %copy-start.4 = (s32[32]{0:T(128)S(1)}, s32[32]{0:T(128)}, u32[]{:S(2)}) copy-start(s32[32]{0:T(128)} %sizes_ref.1) | copy-start | bytes 388

commit v7 on v6

--- a/solution.py
+++ b/solution.py
@@ -9,7 +9,7 @@
 SUBLANES = 8
 X_SIZE = 4
 COLOURS = 4
-VMEM_LIMIT = 24 * 2**20
+VMEM_LIMIT = 16 * 2**20
 SMALL = pltpu.CompilerParams(vmem_limit_bytes=4 * 2**20)
 
 
@@ -17,10 +17,10 @@
     return lax.rem(2 * lax.rem(slot, X_SIZE) + lax.div(slot, X_SIZE), COLOURS)
 
 
-def sigma_kernel(sectors, rows, factor):
+def left_kernel(sectors, rows):
     def body(
-        charge_ref, sizes_ref, mine_ref, other_ref, left_ref, right_ref,
-        out_ref, norm_ref, own_ref, live_ref, half_buf, own_buf,
+        charge_ref, sizes_ref, mine_ref, other_ref, left_ref,
+        half_ref, psi_ref, norm_ref, own_ref, live_ref, own_buf,
     ):
         pairs, here, block, _ = left_ref.shape
         sec = lax.axis_index("sec")
@@ -42,33 +42,44 @@
                 live = jnp.where(lane < sizes_ref[source], 1.0, 0.0)
                 left = left_ref[p, k] * live.astype(jnp.bfloat16)
                 half = jnp.dot(left, block_of(source), preferred_element_type=jnp.float32) * live
-                half_buf[k, :, p * block : (p + 1) * block] = half.astype(jnp.bfloat16)
+                half_ref[k, :, p * block : (p + 1) * block] = half.astype(jnp.bfloat16)
         row = lax.broadcasted_iota(jnp.int32, (block, block), 0)
         column = lax.broadcasted_iota(jnp.int32, (block, block), 1)
         farthest = jnp.maximum(row, column)
         part_row = lax.broadcasted_iota(jnp.int32, (rows, block), 0) + start
         part_farthest = jnp.maximum(part_row, lax.broadcasted_iota(jnp.int32, (rows, block), 1))
-        correlation = jnp.zeros((1, 1), jnp.float32)
         norm = jnp.zeros((1, 1), jnp.float32)
         for k in range(here):
             size = sizes_ref[first + k]
+            psi = jnp.where(farthest < size, block_of(first + k), 0)
+            psi_ref[k] = psi
+            psi = psi.astype(jnp.float32)
+            own_buf[...] = psi
+            norm += jnp.sum(psi * psi, keepdims=True)
+            own_ref[k] = own_buf[pl.ds(start, rows), :]
+            live_ref[k] = jnp.where(part_farthest < size, 1.0, 0.0)
+        norm_ref[...] = jnp.broadcast_to(norm, norm_ref.shape)
+
+    return body
+
+
+def right_kernel(rows, factor):
+    def body(half_ref, psi_ref, right_ref, out_ref):
+        pairs, here, block, _ = right_ref.shape
+        correlation = jnp.zeros((1, 1), jnp.float32)
+        for k in range(here):
             total = jnp.zeros((block, block), jnp.float32)
             for p in range(pairs):
                 total += lax.dot_general(
-                    half_buf[k, :, p * block : (p + 1) * block], right_ref[p, k],
+                    half_ref[k, :, p * block : (p + 1) * block], right_ref[p, k],
                     (((1,), (1,)), ((), ())), preferred_element_type=jnp.float32,
                 )
             total = total * factor
-            psi = jnp.where(farthest < size, block_of(first + k), 0).astype(jnp.float32)
-            own_buf[k] = psi
-            correlation += jnp.sum(psi * total, keepdims=True)
-            norm += jnp.sum(psi * psi, keepdims=True)
+            correlation += jnp.sum(psi_ref[k].astype(jnp.float32) * total, keepdims=True)
             cut = total.reshape(block // rows, rows, block).astype(jnp.bfloat16)
             for part in range(block // LANES):
                 at = (part * here + k) * rows
                 out_ref[:, at : at + rows, :] = cut[:, :, part * LANES : (part + 1) * LANES]
-            own_ref[k] = own_buf[k, pl.ds(start, rows)]
-            live_ref[k] = jnp.where(part_farthest < size, 1.0, 0.0)
         high = correlation.astype(jnp.bfloat16).astype(jnp.float32)
         middle = (correlation - high).astype(jnp.bfloat16).astype(jnp.float32)
         low = correlation - high - middle
@@ -80,7 +91,6 @@
         words = jnp.where(up == 0, words, 0.0).astype(jnp.bfloat16)
         body_rows = here * rows * (block // LANES)
         out_ref[:, body_rows:, :] = jnp.broadcast_to(words[None], (block // rows, *words.shape))
-        norm_ref[...] = jnp.broadcast_to(norm, norm_ref.shape)
 
     return body
 
@@ -155,25 +165,33 @@
 
     part = (here, rows, block)
     pack_rows = here * rows * (block // LANES) + rows
-    pieces, norm, own_rows, live = pl.pallas_call(
-        sigma_kernel(sectors, rows, factor),
+    half, psi, norm, own_rows, live = pl.pallas_call(
+        left_kernel(sectors, rows),
         out_shape=(
-            jax.ShapeDtypeStruct((ops_count, pack_rows, LANES), bf16),
+            jax.ShapeDtypeStruct((here, block, pairs * block), bf16),
+            jax.ShapeDtypeStruct(wavefunction.shape, bf16),
             jax.ShapeDtypeStruct((SUBLANES, LANES), f32),
             jax.ShapeDtypeStruct(part, f32),
             jax.ShapeDtypeStruct(part, f32),
         ),
-        in_specs=[smem] * 2 + [vmem] * 4,
-        out_specs=(vmem,) * 4,
-        scratch_shapes=[
-            pltpu.VMEM((here, block, pairs * block), bf16),
-            pltpu.VMEM((here, block, block), f32),
-        ],
+        in_specs=[smem] * 2 + [vmem] * 3,
+        out_specs=(vmem,) * 5,
+        scratch_shapes=[pltpu.VMEM((block, block), f32)],
         compiler_params=pltpu.CompilerParams(vmem_limit_bytes=VMEM_LIMIT),
         cost_estimate=pl.CostEstimate(
-            flops=4 * pairs * here * block**3, bytes_accessed=2**20, transcendentals=0
-        ),
-    )(charge, block_sizes, mine, other, left_ops, right_ops)
+            flops=2 * pairs * here * block**3, bytes_accessed=2**20, transcendentals=0
+        ),
+    )(charge, block_sizes, mine, other, left_ops)
+    pieces = pl.pallas_call(
+        right_kernel(rows, factor),
+        out_shape=jax.ShapeDtypeStruct((ops_count, pack_rows, LANES), bf16),
+        in_specs=[vmem] * 3,
+        out_specs=vmem,
+        compiler_params=pltpu.CompilerParams(vmem_limit_bytes=VMEM_LIMIT),
+        cost_estimate=pl.CostEstimate(
+            flops=2 * pairs * here * block**3, bytes_accessed=2**20, transcendentals=0
+        ),
+    )(half, psi, right_ops)
     received = lax.all_to_all(pieces, "ops", 0, 0)
 
     wide, both = pl.pallas_call(

time: 91.5 us -> 91.3 us (level)
    pallas_call x1 -> x2, Pallas kernels: 2.15 us -> 2.46 us  [the longest x1 1.56 us: local(): pl.pallas_call(left_kernel(sectors, rows), out_shape=(jax.ShapeDtypeStruc...]
where the time goes in v7:
time: 91.3 us; the launch traced here: 90.8 us
  blocking collectives  60.8 us (67%)
  starting transfers between devices  22.6 us (25%)
  Pallas kernels  3.28 us (4%)
  local copies, waits for them, and re-layouts  2.35 us (3%)
  between operations  0.99 us (1%)
    all_to_all x1, blocking collectives, local(): own = lax.all_to_all(spread, 'sec', 0, 0).reshape(sectors, eighth, block)  28.9 us
    all_to_all x1, blocking collectives, local(): received = lax.all_to_all(pieces, 'ops', 0, 0)  18.6 us
    all_to_all x1, blocking collectives, local(): both = lax.all_to_all(both, 'sec', 0, 0)  13.3 us
    ppermute x4, starting transfers between devices, local(): lax.ppermute(piece, 'sec', swap)[:, None]  12.4 us
    ppermute x3, starting transfers between devices, fetch(): return lax.ppermute(own, ('ops', 'sec'), pairs)  10.1 us
  transfers between devices with their start and end apart: 7, of which 1 were waited for; matrix products, arithmetic and copies ran while one was open for 1% of the time, Pallas kernels for 0%

profile of v7, /device:TPU:1, one launch (start us, length us, event | category | flops | bytes accessed | tf_op | source)
XLA Modules:
  0.0 90.8 jit_solution(484684390482100720)
XLA Ops:
  0.6 0.0 copy-start
  0.7 0.9 %copy-done = bf16[2,256,256]{2,1,0:T(8,128)(2,1)S(1)} copy-done((bf16[2,256,256]{2,1,0:T(8,128)(2,1)S(1)}, bf16[2,256,256]{2,1,0:T(8,128)(2,1)}, u32[]{:S(2)}) %copy-start) | copy-done | bytes 262168
  1.6 0.1 broadcast_in_dim.31
  1.7 28.9 %all_to_all.15 = bf16[16,2,32,256]{3,2,1,0:T(8,128)(2,1)S(1)} all-to-all(bf16[16,2,32,256]{3,2,1,0:T(8,128)(2,1)S(1)} %bitcast.37), channel_id=1, replica_groups=mesh['ops'=32,'sec'=16] {'sec'}, dimensions={0} | all-to-all | bytes 1048576 | tf_op jit(solution)/shard_map/all_to_all | solution.py:142
  30.6 3.2 %collective-permute-start = (bf16[32,32,256]{2,1,0:T(8,128)(2,1)S(1)}, bf16[32,32,256]{2,1,0:T(8,128)(2,1)S(1)}, u32[]{:S(2)}, u32[]{:S(2)}) collective-permute-start(bf16[32,32,256]{2,1,0:T(8,128)(2,1)S(1)} %bitcast.32), channel_id=1, source_target_pairs={{64,0},{449,1},{66,2},{451,3},{68,4},{453,5},{70,6},{455,7},{72,8}... | collective-permute-start | bytes 1572872 | tf_op jit(solution)/shard_map/ppermute | solution.py:154
  33.8 3.1 %collective-permute-start.1 = (bf16[32,32,256]{2,1,0:T(8,128)(2,1)S(1)}, bf16[32,32,256]{2,1,0:T(8,128)(2,1)S(1)}, u32[]{:S(2)}, u32[]{:S(2)}) collective-permute-start(bf16[32,32,256]{2,1,0:T(8,128)(2,1)S(1)} %bitcast.33), channel_id=1, source_target_pairs={{16,0},{49,1},{18,2},{51,3},{20,4},{53,5},{22,6},{55,7},{24,8},{57... | collective-permute-start | bytes 1572872 | tf_op jit(solution)/shard_map/ppermute | solution.py:154
  36.9 3.8 %collective-permute-start.2 = (bf16[32,32,256]{2,1,0:T(8,128)(2,1)S(1)}, bf16[32,32,256]{2,1,0:T(8,128)(2,1)S(1)}, u32[]{:S(2)}, u32[]{:S(2)}) collective-permute-start(bf16[32,32,256]{2,1,0:T(8,128)(2,1)S(1)} %bitcast.34), channel_id=1, source_target_pairs={{448,0},{65,1},{450,2},{67,3},{452,4},{69,5},{454,6},{71,7},{456,8... | collective-permute-start | bytes 1572872 | tf_op jit(solution)/shard_map/ppermute | solution.py:154
  40.8 2.5 %collective-permute-start.3 = (bf16[32,32,256]{2,1,0:T(8,128)(2,1)S(1)}, bf16[32,32,256]{2,1,0:T(8,128)(2,1)S(1)}, u32[]{:S(2)}, u32[]{:S(2)}) collective-permute-start(bf16[32,32,256]{2,1,0:T(8,128)(2,1)S(1)} %bitcast.35), channel_id=1, source_target_pairs={{0,1},{1,0},{2,3},{3,2},{4,5},{5,4},{6,7},{7,6},{8,9},{9,8},{10,11... | collective-permute-start | bytes 1572872 | tf_op jit(solution)/shard_map/ppermute | solution.py:164
  43.4 0.3 broadcast_in_dim.30.clone
  43.7 0.0 collective-permute-done
  43.7 1.9 %collective-permute-start.4 = (bf16[32,32,256]{2,1,0:T(8,128)(2,1)S(1)}, bf16[32,32,256]{2,1,0:T(8,128)(2,1)S(1)}, u32[]{:S(2)}, u32[]{:S(2)}) collective-permute-start(bf16[32,32,256]{2,1,0:T(8,128)(2,1)S(1)} %collective-permute-done), channel_id=1, source_target_pairs={{0,1},{1,0},{2,3},{3,2},{4,5},{5,4},{6,7},{7,6},{8,9},{9,8},{10,11... | collective-permute-start | bytes 1572872 | tf_op jit(solution)/shard_map/ppermute | solution.py:164
  45.6 0.0 collective-permute-done.1
  45.7 2.4 %collective-permute-start.5 = (bf16[32,32,256]{2,1,0:T(8,128)(2,1)S(1)}, bf16[32,32,256]{2,1,0:T(8,128)(2,1)S(1)}, u32[]{:S(2)}, u32[]{:S(2)}) collective-permute-start(bf16[32,32,256]{2,1,0:T(8,128)(2,1)S(1)} %collective-permute-done.1), channel_id=1, source_target_pairs={{0,1},{1,0},{2,3},{3,2},{4,5},{5,4},{6,7},{7,6},{8,9},{9,8},{10,11... | collective-permute-start | bytes 1572872 | tf_op jit(solution)/shard_map/ppermute | solution.py:164
  48.1 0.0 collective-permute-done.2
  48.1 5.6 %collective-permute-start.6 = (bf16[32,32,256]{2,1,0:T(8,128)(2,1)S(1)}, bf16[32,32,256]{2,1,0:T(8,128)(2,1)S(1)}, u32[]{:S(2)}, u32[]{:S(2)}) collective-permute-start(bf16[32,32,256]{2,1,0:T(8,128)(2,1)S(1)} %collective-permute-done.2), channel_id=1, source_target_pairs={{0,1},{1,0},{2,3},{3,2},{4,5},{5,4},{6,7},{7,6},{8,9},{9,8},{10,11... | collective-permute-start | bytes 1572872 | tf_op jit(solution)/shard_map/ppermute | solution.py:164
  53.6 0.0 collective-permute-done.3
  53.7 0.3 broadcast_in_dim.30.clone.1
  54.1 0.0 copy-start.2
  54.1 0.0 copy-start.3
  54.1 0.0 copy-start.4
  54.2 0.0 collective-permute-done.4
  54.2 0.0 collective-permute-done.5
  54.3 0.9 collective-permute-done.6
  55.2 0.5 copy-done.2
  55.7 0.0 copy-done.3
  55.7 0.0 copy-done.4
  55.7 0.0 copy-start.1
  55.7 1.6 %shard_map.68 = (bf16[2,256,2048]{2,1,0:T(8,128)(2,1)S(1)}, bf16[2,256,256]{2,1,0:T(8,128)(2,1)S(1)}, f32[8,128]{1,0:T(8,128)S(1)}, f32[2,8,256]{2,1,0:T(8,128)S(1)}, f32[2,8,256]{2,1,0:T(8,128)S(1)}) custom-call(s32[8]{0:T(128)S(1)} %copy-done.3, s32[32]{0:T(128)S(1)} %copy-done.4, bf16[32,4,32,256]{3,2,1,0:T(8,128)(2,1)S(1)} %bitcast_dynamic-update-slice_fusion.3.mine_ref, ...), custom_call_target="tpu_custom_call" | custom-call | flops 536870912 | bytes 1048576 | tf_op jit(solution)/shard_map/pallas_call | solution.py:168
  57.2 0.0 copy-done.1
  57.3 0.9 shard_map.69
  58.2 18.6 %all_to_all.16.received_ref = bf16[32,40,128]{2,1,0:T(8,128)(2,1)S(1)} all-to-all(bf16[32,40,128]{2,1,0:T(8,128)(2,1)S(1)} %shard_map.69), channel_id=1, replica_groups=mesh['ops'=32,'sec'=16] {'ops'}, dimensions={0} | all-to-all | bytes 655360 | tf_op jit(solution)/shard_map/all_to_all | solution.py:195
  76.7 0.2 shard_map.70
  76.9 13.3 %all_to_all.17.both_ref = f32[16,8,128]{2,1,0:T(8,128)S(1)} all-to-all(f32[16,8,128]{2,1,0:T(8,128)S(1)} %get-tuple-element.13), channel_id=1, replica_groups=mesh['ops'=32,'sec'=16] {'sec'}, dimensions={0} | all-to-all | bytes 131072 | tf_op jit(solution)/shard_map/all_to_all | solution.py:207
  90.1 0.7 shard_map.71
  (10 shorter events, 0.4 us)
Async XLA Ops:
  0.6 1.0 %copy-start = (bf16[2,256,256]{2,1,0:T(8,128)(2,1)S(1)}, bf16[2,256,256]{2,1,0:T(8,128)(2,1)}, u32[]{:S(2)}) copy-start(bf16[2,256,256]{2,1,0:T(8,128)(2,1)} %param.5) | copy-start | bytes 786436
  30.6 13.1 %collective-permute-start = (bf16[32,32,256]{2,1,0:T(8,128)(2,1)S(1)}, bf16[32,32,256]{2,1,0:T(8,128)(2,1)S(1)}, u32[]{:S(2)}, u32[]{:S(2)}) collective-permute-start(bf16[32,32,256]{2,1,0:T(8,128)(2,1)S(1)} %bitcast.32), channel_id=1, source_target_pairs={{64,0},{449,1},{66,2},{451,3},{68,4},{453,5},{70,6},{455,7},{72,8}... | collective-permute-start | bytes 1572872 | tf_op jit(solution)/shard_map/ppermute | solution.py:154
  33.8 11.8 %collective-permute-start.1 = (bf16[32,32,256]{2,1,0:T(8,128)(2,1)S(1)}, bf16[32,32,256]{2,1,0:T(8,128)(2,1)S(1)}, u32[]{:S(2)}, u32[]{:S(2)}) collective-permute-start(bf16[32,32,256]{2,1,0:T(8,128)(2,1)S(1)} %bitcast.33), channel_id=1, source_target_pairs={{16,0},{49,1},{18,2},{51,3},{20,4},{53,5},{22,6},{55,7},{24,8},{57... | collective-permute-start | bytes 1572872 | tf_op jit(solution)/shard_map/ppermute | solution.py:154
  36.9 11.1 %collective-permute-start.2 = (bf16[32,32,256]{2,1,0:T(8,128)(2,1)S(1)}, bf16[32,32,256]{2,1,0:T(8,128)(2,1)S(1)}, u32[]{:S(2)}, u32[]{:S(2)}) collective-permute-start(bf16[32,32,256]{2,1,0:T(8,128)(2,1)S(1)} %bitcast.34), channel_id=1, source_target_pairs={{448,0},{65,1},{450,2},{67,3},{452,4},{69,5},{454,6},{71,7},{456,8... | collective-permute-start | bytes 1572872 | tf_op jit(solution)/shard_map/ppermute | solution.py:154
  40.8 12.9 %collective-permute-start.3 = (bf16[32,32,256]{2,1,0:T(8,128)(2,1)S(1)}, bf16[32,32,256]{2,1,0:T(8,128)(2,1)S(1)}, u32[]{:S(2)}, u32[]{:S(2)}) collective-permute-start(bf16[32,32,256]{2,1,0:T(8,128)(2,1)S(1)} %bitcast.35), channel_id=1, source_target_pairs={{0,1},{1,0},{2,3},{3,2},{4,5},{5,4},{6,7},{7,6},{8,9},{9,8},{10,11... | collective-permute-start | bytes 1572872 | tf_op jit(solution)/shard_map/ppermute | solution.py:164
  43.7 10.4 %collective-permute-start.4 = (bf16[32,32,256]{2,1,0:T(8,128)(2,1)S(1)}, bf16[32,32,256]{2,1,0:T(8,128)(2,1)S(1)}, u32[]{:S(2)}, u32[]{:S(2)}) collective-permute-start(bf16[32,32,256]{2,1,0:T(8,128)(2,1)S(1)} %collective-permute-done), channel_id=1, source_target_pairs={{0,1},{1,0},{2,3},{3,2},{4,5},{5,4},{6,7},{7,6},{8,9},{9,8},{10,11... | collective-permute-start | bytes 1572872 | tf_op jit(solution)/shard_map/ppermute | solution.py:164
  45.7 8.6 %collective-permute-start.5 = (bf16[32,32,256]{2,1,0:T(8,128)(2,1)S(1)}, bf16[32,32,256]{2,1,0:T(8,128)(2,1)S(1)}, u32[]{:S(2)}, u32[]{:S(2)}) collective-permute-start(bf16[32,32,256]{2,1,0:T(8,128)(2,1)S(1)} %collective-permute-done.1), channel_id=1, source_target_pairs={{0,1},{1,0},{2,3},{3,2},{4,5},{5,4},{6,7},{7,6},{8,9},{9,8},{10,11... | collective-permute-start | bytes 1572872 | tf_op jit(solution)/shard_map/ppermute | solution.py:164
  48.1 7.1 %collective-permute-start.6 = (bf16[32,32,256]{2,1,0:T(8,128)(2,1)S(1)}, bf16[32,32,256]{2,1,0:T(8,128)(2,1)S(1)}, u32[]{:S(2)}, u32[]{:S(2)}) collective-permute-start(bf16[32,32,256]{2,1,0:T(8,128)(2,1)S(1)} %collective-permute-done.2), channel_id=1, source_target_pairs={{0,1},{1,0},{2,3},{3,2},{4,5},{5,4},{6,7},{7,6},{8,9},{9,8},{10,11... | collective-permute-start | bytes 1572872 | tf_op jit(solution)/shard_map/ppermute | solution.py:164
  54.1 1.6 %copy-start.2 = (bf16[8,2,256,256]{3,2,1,0:T(8,128)(2,1)S(1)}, bf16[8,2,256,256]{3,2,1,0:T(8,128)(2,1)}, u32[]{:S(2)}) copy-start(bf16[8,2,256,256]{3,2,1,0:T(8,128)(2,1)} %left_ref.1) | copy-start | bytes 6291460
  54.1 1.6 %copy-start.3 = (s32[8]{0:T(128)S(1)}, s32[8]{0:T(128)}, u32[]{:S(2)}) copy-start(s32[8]{0:T(128)} %charge_ref.1) | copy-start | bytes 100
  54.1 1.6 %copy-start.4 = (s32[32]{0:T(128)S(1)}, s32[32]{0:T(128)}, u32[]{:S(2)}) copy-start(s32[32]{0:T(128)} %sizes_ref.1) | copy-start | bytes 388
  55.7 1.6 %copy-start.1 = (bf16[8,2,256,256]{3,2,1,0:T(8,128)(2,1)S(1)}, bf16[8,2,256,256]{3,2,1,0:T(8,128)(2,1)}, u32[]{:S(2)}) copy-start(bf16[8,2,256,256]{3,2,1,0:T(8,128)(2,1)} %right_ref.1) | copy-start | bytes 6291460

commit v8 on v7

--- a/solution.py
+++ b/solution.py
@@ -100,8 +100,8 @@
     summed = jnp.sum(received_ref[...].astype(jnp.float32), axis=0)
     parts = block // LANES
     correlation = jnp.sum(summed[parts * here * rows :], keepdims=True)
-    up = lax.broadcasted_iota(jnp.int32, both_ref.shape[1:], 0)
-    both = jnp.where(up == 0, correlation, norm_ref[...])
+    lane = lax.broadcasted_iota(jnp.int32, (1, LANES), 1)
+    both = jnp.where(lane == 0, correlation, norm_ref[0:1, :])
     both_ref[...] = jnp.broadcast_to(both[None], both_ref.shape)
     for k in range(here):
         for part in range(parts):
@@ -112,7 +112,7 @@
 
 def residual_kernel(both_ref, wide_ref, own_ref, sigma_ref, out_ref):
     both = jnp.sum(both_ref[...], axis=0)
-    ritz_value = both[0:1, 0:1] / both[1:2, 0:1]
+    ritz_value = both[0:1, 0:1] / both[0:1, 1:2]
     sigma_ref[...] = wide_ref[...].astype(jnp.bfloat16)
     for k in range(wide_ref.shape[0]):
         out_ref[k] = (wide_ref[k] - ritz_value * own_ref[k]).astype(jnp.bfloat16)
@@ -198,7 +198,7 @@
         sum_kernel,
         out_shape=(
             jax.ShapeDtypeStruct(part, f32),
-            jax.ShapeDtypeStruct((sec_total, SUBLANES, LANES), f32),
+            jax.ShapeDtypeStruct((sec_total, 1, LANES), f32),
         ),
         in_specs=[vmem] * 3,
         out_specs=(vmem,) * 2,

time: 91.3 us -> 90.6 us (level)
  no operation moved by 1% of the time
where the time goes in v8:
time: 90.6 us; the launch traced here: 90.1 us
  blocking collectives  60 us (66%)
  starting transfers between devices  22.6 us (25%)
  Pallas kernels  3.34 us (4%)
  local copies, waits for them, and re-layouts  2.35 us (3%)
  between operations  0.99 us (1%)
    all_to_all x1, blocking collectives, local(): own = lax.all_to_all(spread, 'sec', 0, 0).reshape(sectors, eighth, block)  28.9 us
    all_to_all x1, blocking collectives, local(): received = lax.all_to_all(pieces, 'ops', 0, 0)  18.6 us
    all_to_all x1, blocking collectives, local(): both = lax.all_to_all(both, 'sec', 0, 0)  12.5 us
    ppermute x4, starting transfers between devices, local(): lax.ppermute(piece, 'sec', swap)[:, None]  12.4 us
    ppermute x3, starting transfers between devices, fetch(): return lax.ppermute(own, ('ops', 'sec'), pairs)  10.1 us
  transfers between devices with their start and end apart: 7, of which 1 were waited for; matrix products, arithmetic and copies ran while one was open for 1% of the time, Pallas kernels for 0%

profile of v8, /device:TPU:1, one launch (start us, length us, event | category | flops | bytes accessed | tf_op | source)
XLA Modules:
  0.0 90.1 jit_solution(2944775526917126357)
XLA Ops:
  0.6 0.0 copy-start
  0.7 0.9 %copy-done = bf16[2,256,256]{2,1,0:T(8,128)(2,1)S(1)} copy-done((bf16[2,256,256]{2,1,0:T(8,128)(2,1)S(1)}, bf16[2,256,256]{2,1,0:T(8,128)(2,1)}, u32[]{:S(2)}) %copy-start) | copy-done | bytes 262168
  1.6 0.1 broadcast_in_dim.31
  1.7 28.9 %all_to_all.15 = bf16[16,2,32,256]{3,2,1,0:T(8,128)(2,1)S(1)} all-to-all(bf16[16,2,32,256]{3,2,1,0:T(8,128)(2,1)S(1)} %bitcast.37), channel_id=1, replica_groups=mesh['ops'=32,'sec'=16] {'sec'}, dimensions={0} | all-to-all | bytes 1048576 | tf_op jit(solution)/shard_map/all_to_all | solution.py:142
  30.6 3.2 %collective-permute-start = (bf16[32,32,256]{2,1,0:T(8,128)(2,1)S(1)}, bf16[32,32,256]{2,1,0:T(8,128)(2,1)S(1)}, u32[]{:S(2)}, u32[]{:S(2)}) collective-permute-start(bf16[32,32,256]{2,1,0:T(8,128)(2,1)S(1)} %bitcast.32), channel_id=1, source_target_pairs={{64,0},{449,1},{66,2},{451,3},{68,4},{453,5},{70,6},{455,7},{72,8}... | collective-permute-start | bytes 1572872 | tf_op jit(solution)/shard_map/ppermute | solution.py:154
  33.8 3.1 %collective-permute-start.1 = (bf16[32,32,256]{2,1,0:T(8,128)(2,1)S(1)}, bf16[32,32,256]{2,1,0:T(8,128)(2,1)S(1)}, u32[]{:S(2)}, u32[]{:S(2)}) collective-permute-start(bf16[32,32,256]{2,1,0:T(8,128)(2,1)S(1)} %bitcast.33), channel_id=1, source_target_pairs={{16,0},{49,1},{18,2},{51,3},{20,4},{53,5},{22,6},{55,7},{24,8},{57... | collective-permute-start | bytes 1572872 | tf_op jit(solution)/shard_map/ppermute | solution.py:154
  36.9 3.8 %collective-permute-start.2 = (bf16[32,32,256]{2,1,0:T(8,128)(2,1)S(1)}, bf16[32,32,256]{2,1,0:T(8,128)(2,1)S(1)}, u32[]{:S(2)}, u32[]{:S(2)}) collective-permute-start(bf16[32,32,256]{2,1,0:T(8,128)(2,1)S(1)} %bitcast.34), channel_id=1, source_target_pairs={{448,0},{65,1},{450,2},{67,3},{452,4},{69,5},{454,6},{71,7},{456,8... | collective-permute-start | bytes 1572872 | tf_op jit(solution)/shard_map/ppermute | solution.py:154
  40.8 2.5 %collective-permute-start.3 = (bf16[32,32,256]{2,1,0:T(8,128)(2,1)S(1)}, bf16[32,32,256]{2,1,0:T(8,128)(2,1)S(1)}, u32[]{:S(2)}, u32[]{:S(2)}) collective-permute-start(bf16[32,32,256]{2,1,0:T(8,128)(2,1)S(1)} %bitcast.35), channel_id=1, source_target_pairs={{0,1},{1,0},{2,3},{3,2},{4,5},{5,4},{6,7},{7,6},{8,9},{9,8},{10,11... | collective-permute-start | bytes 1572872 | tf_op jit(solution)/shard_map/ppermute | solution.py:164
  43.4 0.3 broadcast_in_dim.30.clone
  43.7 0.0 collective-permute-done
  43.7 1.9 %collective-permute-start.4 = (bf16[32,32,256]{2,1,0:T(8,128)(2,1)S(1)}, bf16[32,32,256]{2,1,0:T(8,128)(2,1)S(1)}, u32[]{:S(2)}, u32[]{:S(2)}) collective-permute-start(bf16[32,32,256]{2,1,0:T(8,128)(2,1)S(1)} %collective-permute-done), channel_id=1, source_target_pairs={{0,1},{1,0},{2,3},{3,2},{4,5},{5,4},{6,7},{7,6},{8,9},{9,8},{10,11... | collective-permute-start | bytes 1572872 | tf_op jit(solution)/shard_map/ppermute | solution.py:164
  45.6 0.0 collective-permute-done.1
  45.7 2.4 %collective-permute-start.5 = (bf16[32,32,256]{2,1,0:T(8,128)(2,1)S(1)}, bf16[32,32,256]{2,1,0:T(8,128)(2,1)S(1)}, u32[]{:S(2)}, u32[]{:S(2)}) collective-permute-start(bf16[32,32,256]{2,1,0:T(8,128)(2,1)S(1)} %collective-permute-done.1), channel_id=1, source_target_pairs={{0,1},{1,0},{2,3},{3,2},{4,5},{5,4},{6,7},{7,6},{8,9},{9,8},{10,11... | collective-permute-start | bytes 1572872 | tf_op jit(solution)/shard_map/ppermute | solution.py:164
  48.1 0.0 collective-permute-done.2
  48.1 5.6 %collective-permute-start.6 = (bf16[32,32,256]{2,1,0:T(8,128)(2,1)S(1)}, bf16[32,32,256]{2,1,0:T(8,128)(2,1)S(1)}, u32[]{:S(2)}, u32[]{:S(2)}) collective-permute-start(bf16[32,32,256]{2,1,0:T(8,128)(2,1)S(1)} %collective-permute-done.2), channel_id=1, source_target_pairs={{0,1},{1,0},{2,3},{3,2},{4,5},{5,4},{6,7},{7,6},{8,9},{9,8},{10,11... | collective-permute-start | bytes 1572872 | tf_op jit(solution)/shard_map/ppermute | solution.py:164
  53.6 0.0 collective-permute-done.3
  53.7 0.3 broadcast_in_dim.30.clone.1
  54.1 0.0 copy-start.2
  54.1 0.0 copy-start.3
  54.1 0.0 copy-start.4
  54.2 0.0 collective-permute-done.4
  54.2 0.0 collective-permute-done.5
  54.3 0.9 collective-permute-done.6
  55.2 0.5 copy-done.2
  55.7 0.0 copy-done.3
  55.7 0.0 copy-done.4
  55.7 0.0 copy-start.1
  55.7 1.6 %shard_map.68 = (bf16[2,256,2048]{2,1,0:T(8,128)(2,1)S(1)}, bf16[2,256,256]{2,1,0:T(8,128)(2,1)S(1)}, f32[8,128]{1,0:T(8,128)S(1)}, f32[2,8,256]{2,1,0:T(8,128)S(1)}, f32[2,8,256]{2,1,0:T(8,128)S(1)}) custom-call(s32[8]{0:T(128)S(1)} %copy-done.3, s32[32]{0:T(128)S(1)} %copy-done.4, bf16[32,4,32,256]{3,2,1,0:T(8,128)(2,1)S(1)} %bitcast_dynamic-update-slice_fusion.3.mine_ref, ...), custom_call_target="tpu_custom_call" | custom-call | flops 536870912 | bytes 1048576 | tf_op jit(solution)/shard_map/pallas_call | solution.py:168
  57.2 0.0 copy-done.1
  57.3 0.9 %shard_map.69 = bf16[32,40,128]{2,1,0:T(8,128)(2,1)S(1)} custom-call(bf16[2,256,2048]{2,1,0:T(8,128)(2,1)S(1)} %get-tuple-element.9.half_ref, bf16[2,256,256]{2,1,0:T(8,128)(2,1)S(1)} %get-tuple-element.10.psi_ref, bf16[8,2,256,256]{3,2,1,0:T(8,128)(2,1)S(1)} %copy-done.1), custom_call_target="tpu_custom_call" | custom-call | flops 536870912 | bytes 1048576 | tf_op jit(solution)/shard_map/pallas_call | solution.py:185
  58.2 18.6 %all_to_all.16.received_ref = bf16[32,40,128]{2,1,0:T(8,128)(2,1)S(1)} all-to-all(bf16[32,40,128]{2,1,0:T(8,128)(2,1)S(1)} %shard_map.69), channel_id=1, replica_groups=mesh['ops'=32,'sec'=16] {'ops'}, dimensions={0} | all-to-all | bytes 655360 | tf_op jit(solution)/shard_map/all_to_all | solution.py:195
  76.7 0.2 shard_map.70
  76.9 12.5 %all_to_all.17.both_ref = f32[16,1,128]{2,1,0:T(1,128)S(1)} all-to-all(f32[16,1,128]{2,1,0:T(1,128)S(1)} %get-tuple-element.13), channel_id=1, replica_groups=mesh['ops'=32,'sec'=16] {'sec'}, dimensions={0} | all-to-all | bytes 16384 | tf_op jit(solution)/shard_map/all_to_all | solution.py:207
  89.4 0.7 shard_map.71
  (10 shorter events, 0.4 us)
Async XLA Ops:
  0.6 1.0 %copy-start = (bf16[2,256,256]{2,1,0:T(8,128)(2,1)S(1)}, bf16[2,256,256]{2,1,0:T(8,128)(2,1)}, u32[]{:S(2)}) copy-start(bf16[2,256,256]{2,1,0:T(8,128)(2,1)} %param.5) | copy-start | bytes 786436
  30.6 13.1 %collective-permute-start = (bf16[32,32,256]{2,1,0:T(8,128)(2,1)S(1)}, bf16[32,32,256]{2,1,0:T(8,128)(2,1)S(1)}, u32[]{:S(2)}, u32[]{:S(2)}) collective-permute-start(bf16[32,32,256]{2,1,0:T(8,128)(2,1)S(1)} %bitcast.32), channel_id=1, source_target_pairs={{64,0},{449,1},{66,2},{451,3},{68,4},{453,5},{70,6},{455,7},{72,8}... | collective-permute-start | bytes 1572872 | tf_op jit(solution)/shard_map/ppermute | solution.py:154
  33.8 11.8 %collective-permute-start.1 = (bf16[32,32,256]{2,1,0:T(8,128)(2,1)S(1)}, bf16[32,32,256]{2,1,0:T(8,128)(2,1)S(1)}, u32[]{:S(2)}, u32[]{:S(2)}) collective-permute-start(bf16[32,32,256]{2,1,0:T(8,128)(2,1)S(1)} %bitcast.33), channel_id=1, source_target_pairs={{16,0},{49,1},{18,2},{51,3},{20,4},{53,5},{22,6},{55,7},{24,8},{57... | collective-permute-start | bytes 1572872 | tf_op jit(solution)/shard_map/ppermute | solution.py:154
  36.9 11.1 %collective-permute-start.2 = (bf16[32,32,256]{2,1,0:T(8,128)(2,1)S(1)}, bf16[32,32,256]{2,1,0:T(8,128)(2,1)S(1)}, u32[]{:S(2)}, u32[]{:S(2)}) collective-permute-start(bf16[32,32,256]{2,1,0:T(8,128)(2,1)S(1)} %bitcast.34), channel_id=1, source_target_pairs={{448,0},{65,1},{450,2},{67,3},{452,4},{69,5},{454,6},{71,7},{456,8... | collective-permute-start | bytes 1572872 | tf_op jit(solution)/shard_map/ppermute | solution.py:154
  40.8 12.9 %collective-permute-start.3 = (bf16[32,32,256]{2,1,0:T(8,128)(2,1)S(1)}, bf16[32,32,256]{2,1,0:T(8,128)(2,1)S(1)}, u32[]{:S(2)}, u32[]{:S(2)}) collective-permute-start(bf16[32,32,256]{2,1,0:T(8,128)(2,1)S(1)} %bitcast.35), channel_id=1, source_target_pairs={{0,1},{1,0},{2,3},{3,2},{4,5},{5,4},{6,7},{7,6},{8,9},{9,8},{10,11... | collective-permute-start | bytes 1572872 | tf_op jit(solution)/shard_map/ppermute | solution.py:164
  43.7 10.4 %collective-permute-start.4 = (bf16[32,32,256]{2,1,0:T(8,128)(2,1)S(1)}, bf16[32,32,256]{2,1,0:T(8,128)(2,1)S(1)}, u32[]{:S(2)}, u32[]{:S(2)}) collective-permute-start(bf16[32,32,256]{2,1,0:T(8,128)(2,1)S(1)} %collective-permute-done), channel_id=1, source_target_pairs={{0,1},{1,0},{2,3},{3,2},{4,5},{5,4},{6,7},{7,6},{8,9},{9,8},{10,11... | collective-permute-start | bytes 1572872 | tf_op jit(solution)/shard_map/ppermute | solution.py:164
  45.7 8.6 %collective-permute-start.5 = (bf16[32,32,256]{2,1,0:T(8,128)(2,1)S(1)}, bf16[32,32,256]{2,1,0:T(8,128)(2,1)S(1)}, u32[]{:S(2)}, u32[]{:S(2)}) collective-permute-start(bf16[32,32,256]{2,1,0:T(8,128)(2,1)S(1)} %collective-permute-done.1), channel_id=1, source_target_pairs={{0,1},{1,0},{2,3},{3,2},{4,5},{5,4},{6,7},{7,6},{8,9},{9,8},{10,11... | collective-permute-start | bytes 1572872 | tf_op jit(solution)/shard_map/ppermute | solution.py:164
  48.1 7.1 %collective-permute-start.6 = (bf16[32,32,256]{2,1,0:T(8,128)(2,1)S(1)}, bf16[32,32,256]{2,1,0:T(8,128)(2,1)S(1)}, u32[]{:S(2)}, u32[]{:S(2)}) collective-permute-start(bf16[32,32,256]{2,1,0:T(8,128)(2,1)S(1)} %collective-permute-done.2), channel_id=1, source_target_pairs={{0,1},{1,0},{2,3},{3,2},{4,5},{5,4},{6,7},{7,6},{8,9},{9,8},{10,11... | collective-permute-start | bytes 1572872 | tf_op jit(solution)/shard_map/ppermute | solution.py:164
  54.1 1.6 %copy-start.2 = (bf16[8,2,256,256]{3,2,1,0:T(8,128)(2,1)S(1)}, bf16[8,2,256,256]{3,2,1,0:T(8,128)(2,1)}, u32[]{:S(2)}) copy-start(bf16[8,2,256,256]{3,2,1,0:T(8,128)(2,1)} %left_ref.1) | copy-start | bytes 6291460
  54.1 1.6 %copy-start.3 = (s32[8]{0:T(128)S(1)}, s32[8]{0:T(128)}, u32[]{:S(2)}) copy-start(s32[8]{0:T(128)} %charge_ref.1) | copy-start | bytes 100
  54.1 1.6 %copy-start.4 = (s32[32]{0:T(128)S(1)}, s32[32]{0:T(128)}, u32[]{:S(2)}) copy-start(s32[32]{0:T(128)} %sizes_ref.1) | copy-start | bytes 388
  55.7 1.6 %copy-start.1 = (bf16[8,2,256,256]{3,2,1,0:T(8,128)(2,1)S(1)}, bf16[8,2,256,256]{3,2,1,0:T(8,128)(2,1)}, u32[]{:S(2)}) copy-start(bf16[8,2,256,256]{3,2,1,0:T(8,128)(2,1)} %right_ref.1) | copy-start | bytes 6291460

commit v9 on v8

--- a/solution.py
+++ b/solution.py
@@ -19,29 +19,21 @@
 
 def left_kernel(sectors, rows):
     def body(
-        charge_ref, sizes_ref, mine_ref, other_ref, left_ref,
+        charge_ref, sizes_ref, all_ref, left_ref,
         half_ref, psi_ref, norm_ref, own_ref, live_ref, own_buf,
     ):
         pairs, here, block, _ = left_ref.shape
         sec = lax.axis_index("sec")
         first = sec * here
         start = pl.multiple_of(lax.axis_index("ops") * rows, rows)
-        core = lax.rem(sec, 2)
         lane = lax.broadcasted_iota(jnp.int32, (1, block), 1)
-
-        def block_of(source):
-            mine, other = mine_ref[source], other_ref[source]
-            upper = jnp.where(core == 0, mine, other)
-            lower = jnp.where(core == 0, other, mine)
-            eighths = [part[q] for q in range(COLOURS) for part in (upper, lower)]
-            return jnp.concatenate(eighths, axis=0)
 
         for p in range(pairs):
             for k in range(here):
                 source = lax.rem(first + k + charge_ref[p], sectors)
                 live = jnp.where(lane < sizes_ref[source], 1.0, 0.0)
                 left = left_ref[p, k] * live.astype(jnp.bfloat16)
-                half = jnp.dot(left, block_of(source), preferred_element_type=jnp.float32) * live
+                half = jnp.dot(left, all_ref[source], preferred_element_type=jnp.float32) * live
                 half_ref[k, :, p * block : (p + 1) * block] = half.astype(jnp.bfloat16)
         row = lax.broadcasted_iota(jnp.int32, (block, block), 0)
         column = lax.broadcasted_iota(jnp.int32, (block, block), 1)
@@ -51,7 +43,7 @@
         norm = jnp.zeros((1, 1), jnp.float32)
         for k in range(here):
             size = sizes_ref[first + k]
-            psi = jnp.where(farthest < size, block_of(first + k), 0)
+            psi = jnp.where(farthest < size, all_ref[first + k], 0)
             psi_ref[k] = psi
             psi = psi.astype(jnp.float32)
             own_buf[...] = psi
@@ -154,14 +146,13 @@
         return lax.ppermute(own, ("ops", "sec"), pairs)
 
     swap = [(s, s ^ 1) for s in range(sec_total)]
-    mine = jnp.zeros((sectors, COLOURS, eighth, block), bf16)
-    other = mine
+    everything = jnp.zeros((sectors, COLOURS, 2, eighth, block), bf16)
     pieces = ((own, 0, 0), (fetch(0, 1), 1, 2), (fetch(1, 0), 2, 0), (fetch(0, -1), 3, -2))
     for piece, relative, way in pieces:
-        where = (0, lax.rem(colour + relative + way * core, COLOURS), 0, 0)
-        mine = lax.dynamic_update_slice(mine, piece[:, None], where)
-        where = (0, lax.rem(colour + relative + way * (1 - core), COLOURS), 0, 0)
-        other = lax.dynamic_update_slice(other, lax.ppermute(piece, "sec", swap)[:, None], where)
+        for part, side in ((piece, core), (lax.ppermute(piece, "sec", swap), 1 - core)):
+            where = (0, lax.rem(colour + relative + way * side, COLOURS), side, 0, 0)
+            everything = lax.dynamic_update_slice(everything, part[:, None, None], where)
+    everything = everything.reshape(sectors, block, block)
 
     part = (here, rows, block)
     pack_rows = here * rows * (block // LANES) + rows
@@ -174,14 +165,14 @@
             jax.ShapeDtypeStruct(part, f32),
             jax.ShapeDtypeStruct(part, f32),
         ),
-        in_specs=[smem] * 2 + [vmem] * 3,
+        in_specs=[smem] * 2 + [vmem] * 2,
         out_specs=(vmem,) * 5,
         scratch_shapes=[pltpu.VMEM((block, block), f32)],
         compiler_params=pltpu.CompilerParams(vmem_limit_bytes=VMEM_LIMIT),
         cost_estimate=pl.CostEstimate(
             flops=2 * pairs * here * block**3, bytes_accessed=2**20, transcendentals=0
         ),
-    )(charge, block_sizes, mine, other, left_ops)
+    )(charge, block_sizes, everything, left_ops)
     pieces = pl.pallas_call(
         right_kernel(rows, factor),
         out_shape=jax.ShapeDtypeStruct((ops_count, pack_rows, LANES), bf16),

time: 90.6 us -> 90.7 us (level)
    all_to_all x1, blocking collectives: 18.6 us -> 19.7 us  [local(): received = lax.all_to_all(pieces, 'ops', 0, 0)]
where the time goes in v9:
time: 90.7 us; the launch traced here: 90.3 us
  blocking collectives  60.7 us (67%)
  starting transfers between devices  22.2 us (24%)
  Pallas kernels  3.24 us (4%)
  local copies, waits for them, and re-layouts  1.95 us (2%)
  waiting for transfers between devices  1.13 us (1%)
  between operations  1.03 us (1%)
    all_to_all x1, blocking collectives, local(): own = lax.all_to_all(spread, 'sec', 0, 0).reshape(sectors, eighth, block)  28.9 us
    all_to_all x1, blocking collectives, local(): received = lax.all_to_all(pieces, 'ops', 0, 0)  19.7 us
    ppermute x4, starting transfers between devices, local(): lax.ppermute(piece, 'sec', swap)  12.1 us
    all_to_all x1, blocking collectives, local(): both = lax.all_to_all(both, 'sec', 0, 0)  12.1 us
    ppermute x3, starting transfers between devices, fetch(): return lax.ppermute(own, ('ops', 'sec'), pairs)  10.1 us
  transfers between devices with their start and end apart: 7, of which 1 were waited for; matrix products, arithmetic and copies ran while one was open for 1% of the time, Pallas kernels for 0%

profile of v9, /device:TPU:1, one launch (start us, length us, event | category | flops | bytes accessed | tf_op | source)
XLA Modules:
  0.0 90.3 jit_solution(6147821315717660132)
XLA Ops:
  0.6 0.0 copy-start
  0.7 0.9 %copy-done = bf16[2,256,256]{2,1,0:T(8,128)(2,1)S(1)} copy-done((bf16[2,256,256]{2,1,0:T(8,128)(2,1)S(1)}, bf16[2,256,256]{2,1,0:T(8,128)(2,1)}, u32[]{:S(2)}) %copy-start) | copy-done | bytes 262168
  1.6 0.1 broadcast_in_dim.31
  1.7 28.9 %all_to_all.15 = bf16[16,2,32,256]{3,2,1,0:T(8,128)(2,1)S(1)} all-to-all(bf16[16,2,32,256]{3,2,1,0:T(8,128)(2,1)S(1)} %bitcast.39), channel_id=1, replica_groups=mesh['ops'=32,'sec'=16] {'sec'}, dimensions={0} | all-to-all | bytes 1048576 | tf_op jit(solution)/shard_map/all_to_all | solution.py:134
  30.6 3.2 %collective-permute-start.1 = (bf16[32,32,256]{2,1,0:T(8,128)(2,1)S(1)}, bf16[32,32,256]{2,1,0:T(8,128)(2,1)S(1)}, u32[]{:S(2)}, u32[]{:S(2)}) collective-permute-start(bf16[32,32,256]{2,1,0:T(8,128)(2,1)S(1)} %bitcast.34), channel_id=1, source_target_pairs={{64,0},{449,1},{66,2},{451,3},{68,4},{453,5},{70,6},{455,7},{72,8}... | collective-permute-start | bytes 1572872 | tf_op jit(solution)/shard_map/ppermute | solution.py:146
  33.8 3.1 %collective-permute-start.3 = (bf16[32,32,256]{2,1,0:T(8,128)(2,1)S(1)}, bf16[32,32,256]{2,1,0:T(8,128)(2,1)S(1)}, u32[]{:S(2)}, u32[]{:S(2)}) collective-permute-start(bf16[32,32,256]{2,1,0:T(8,128)(2,1)S(1)} %bitcast.35), channel_id=1, source_target_pairs={{16,0},{49,1},{18,2},{51,3},{20,4},{53,5},{22,6},{55,7},{24,8},{57... | collective-permute-start | bytes 1572872 | tf_op jit(solution)/shard_map/ppermute | solution.py:146
  36.9 3.8 %collective-permute-start.5 = (bf16[32,32,256]{2,1,0:T(8,128)(2,1)S(1)}, bf16[32,32,256]{2,1,0:T(8,128)(2,1)S(1)}, u32[]{:S(2)}, u32[]{:S(2)}) collective-permute-start(bf16[32,32,256]{2,1,0:T(8,128)(2,1)S(1)} %bitcast.36), channel_id=1, source_target_pairs={{448,0},{65,1},{450,2},{67,3},{452,4},{69,5},{454,6},{71,7},{456,8... | collective-permute-start | bytes 1572872 | tf_op jit(solution)/shard_map/ppermute | solution.py:146
  40.8 2.5 %collective-permute-start = (bf16[32,32,256]{2,1,0:T(8,128)(2,1)S(1)}, bf16[32,32,256]{2,1,0:T(8,128)(2,1)S(1)}, u32[]{:S(2)}, u32[]{:S(2)}) collective-permute-start(bf16[32,32,256]{2,1,0:T(8,128)(2,1)S(1)} %bitcast.37), channel_id=1, source_target_pairs={{0,1},{1,0},{2,3},{3,2},{4,5},{5,4},{6,7},{7,6},{8,9},{9,8},{10,11... | collective-permute-start | bytes 1572872 | tf_op jit(solution)/shard_map/ppermute | solution.py:152
  43.4 0.0 collective-permute-done.1
  43.4 1.9 %collective-permute-start.2 = (bf16[32,32,256]{2,1,0:T(8,128)(2,1)S(1)}, bf16[32,32,256]{2,1,0:T(8,128)(2,1)S(1)}, u32[]{:S(2)}, u32[]{:S(2)}) collective-permute-start(bf16[32,32,256]{2,1,0:T(8,128)(2,1)S(1)} %collective-permute-done.1), channel_id=1, source_target_pairs={{0,1},{1,0},{2,3},{3,2},{4,5},{5,4},{6,7},{7,6},{8,9},{9,8},{10,11... | collective-permute-start | bytes 1572872 | tf_op jit(solution)/shard_map/ppermute | solution.py:152
  45.3 0.5 broadcast_in_dim.30
  45.9 0.0 copy-start.2
  45.9 0.0 copy-start.3
  45.9 0.0 copy-start.4
  45.9 0.1 constant_dynamic-update-slice_fusion
  46.0 0.0 collective-permute-done.3
  46.0 2.5 %collective-permute-start.4 = (bf16[32,32,256]{2,1,0:T(8,128)(2,1)S(1)}, bf16[32,32,256]{2,1,0:T(8,128)(2,1)S(1)}, u32[]{:S(2)}, u32[]{:S(2)}) collective-permute-start(bf16[32,32,256]{2,1,0:T(8,128)(2,1)S(1)} %collective-permute-done.3), channel_id=1, source_target_pairs={{0,1},{1,0},{2,3},{3,2},{4,5},{5,4},{6,7},{7,6},{8,9},{9,8},{10,11... | collective-permute-start | bytes 1572872 | tf_op jit(solution)/shard_map/ppermute | solution.py:152
  48.5 0.0 collective-permute-done.5
  48.5 5.1 %collective-permute-start.6 = (bf16[32,32,256]{2,1,0:T(8,128)(2,1)S(1)}, bf16[32,32,256]{2,1,0:T(8,128)(2,1)S(1)}, u32[]{:S(2)}, u32[]{:S(2)}) collective-permute-start(bf16[32,32,256]{2,1,0:T(8,128)(2,1)S(1)} %collective-permute-done.5), channel_id=1, source_target_pairs={{0,1},{1,0},{2,3},{3,2},{4,5},{5,4},{6,7},{7,6},{8,9},{9,8},{10,11... | collective-permute-start | bytes 1572872 | tf_op jit(solution)/shard_map/ppermute | solution.py:152
  53.6 0.0 collective-permute-done
  53.7 0.1 bitcast_dynamic-update-slice_fusion.5
  53.7 0.1 bitcast_dynamic-update-slice_fusion.4
  53.8 0.0 collective-permute-done.2
  53.8 0.1 bitcast_dynamic-update-slice_fusion.3
  53.9 0.1 bitcast_dynamic-update-slice_fusion.2
  53.9 0.0 collective-permute-done.4
  54.0 0.0 copy-start.1
  54.0 0.1 bitcast_dynamic-update-slice_fusion
  54.1 1.1 %collective-permute-done.6 = bf16[32,32,256]{2,1,0:T(8,128)(2,1)S(1)} collective-permute-done((bf16[32,32,256]{2,1,0:T(8,128)(2,1)S(1)}, bf16[32,32,256]{2,1,0:T(8,128)(2,1)S(1)}, u32[]{:S(2)}, u32[]{:S(2)}) %collective-permute-start.6) | collective-permute-done | bytes 524320 | tf_op jit(solution)/shard_map/ppermute | solution.py:152
  55.2 0.0 copy-done.2
  55.2 0.0 copy-done.3
  55.2 0.0 copy-done.4
  55.2 1.4 %shard_map.68 = (bf16[2,256,2048]{2,1,0:T(8,128)(2,1)S(1)}, bf16[2,256,256]{2,1,0:T(8,128)(2,1)S(1)}, f32[8,128]{1,0:T(8,128)S(1)}, f32[2,8,256]{2,1,0:T(8,128)S(1)}, f32[2,8,256]{2,1,0:T(8,128)S(1)}) custom-call(s32[8]{0:T(128)S(1)} %copy-done.3, s32[32]{0:T(128)S(1)} %copy-done.4, bf16[32,256,256]{2,1,0:T(8,128)(2,1)S(1)} %bitcast.33, ...), custom_call_target="tpu_custom_call" | custom-call | flops 536870912 | bytes 1048576 | tf_op jit(solution)/shard_map/pallas_call | solution.py:159
  56.7 0.0 copy-done.1
  56.7 0.9 %shard_map.69 = bf16[32,40,128]{2,1,0:T(8,128)(2,1)S(1)} custom-call(bf16[2,256,2048]{2,1,0:T(8,128)(2,1)S(1)} %get-tuple-element.9.half_ref, bf16[2,256,256]{2,1,0:T(8,128)(2,1)S(1)} %get-tuple-element.10.psi_ref, bf16[8,2,256,256]{3,2,1,0:T(8,128)(2,1)S(1)} %copy-done.1), custom_call_target="tpu_custom_call" | custom-call | flops 536870912 | bytes 1048576 | tf_op jit(solution)/shard_map/pallas_call | solution.py:176
  57.6 19.7 %all_to_all.16.received_ref = bf16[32,40,128]{2,1,0:T(8,128)(2,1)S(1)} all-to-all(bf16[32,40,128]{2,1,0:T(8,128)(2,1)S(1)} %shard_map.69), channel_id=1, replica_groups=mesh['ops'=32,'sec'=16] {'ops'}, dimensions={0} | all-to-all | bytes 655360 | tf_op jit(solution)/shard_map/all_to_all | solution.py:186
  77.3 0.2 shard_map.70
  77.5 12.1 %all_to_all.17.both_ref = f32[16,1,128]{2,1,0:T(1,128)S(1)} all-to-all(f32[16,1,128]{2,1,0:T(1,128)S(1)} %get-tuple-element.13), channel_id=1, replica_groups=mesh['ops'=32,'sec'=16] {'sec'}, dimensions={0} | all-to-all | bytes 16384 | tf_op jit(solution)/shard_map/all_to_all | solution.py:198
  89.6 0.7 shard_map.71
  (4 shorter events, 0.1 us)
Async XLA Ops:
  0.6 1.0 %copy-start = (bf16[2,256,256]{2,1,0:T(8,128)(2,1)S(1)}, bf16[2,256,256]{2,1,0:T(8,128)(2,1)}, u32[]{:S(2)}) copy-start(bf16[2,256,256]{2,1,0:T(8,128)(2,1)} %param.5) | copy-start | bytes 786436
  30.6 12.8 %collective-permute-start.1 = (bf16[32,32,256]{2,1,0:T(8,128)(2,1)S(1)}, bf16[32,32,256]{2,1,0:T(8,128)(2,1)S(1)}, u32[]{:S(2)}, u32[]{:S(2)}) collective-permute-start(bf16[32,32,256]{2,1,0:T(8,128)(2,1)S(1)} %bitcast.34), channel_id=1, source_target_pairs={{64,0},{449,1},{66,2},{451,3},{68,4},{453,5},{70,6},{455,7},{72,8}... | collective-permute-start | bytes 1572872 | tf_op jit(solution)/shard_map/ppermute | solution.py:146
  33.8 12.2 %collective-permute-start.3 = (bf16[32,32,256]{2,1,0:T(8,128)(2,1)S(1)}, bf16[32,32,256]{2,1,0:T(8,128)(2,1)S(1)}, u32[]{:S(2)}, u32[]{:S(2)}) collective-permute-start(bf16[32,32,256]{2,1,0:T(8,128)(2,1)S(1)} %bitcast.35), channel_id=1, source_target_pairs={{16,0},{49,1},{18,2},{51,3},{20,4},{53,5},{22,6},{55,7},{24,8},{57... | collective-permute-start | bytes 1572872 | tf_op jit(solution)/shard_map/ppermute | solution.py:146
  36.9 11.6 %collective-permute-start.5 = (bf16[32,32,256]{2,1,0:T(8,128)(2,1)S(1)}, bf16[32,32,256]{2,1,0:T(8,128)(2,1)S(1)}, u32[]{:S(2)}, u32[]{:S(2)}) collective-permute-start(bf16[32,32,256]{2,1,0:T(8,128)(2,1)S(1)} %bitcast.36), channel_id=1, source_target_pairs={{448,0},{65,1},{450,2},{67,3},{452,4},{69,5},{454,6},{71,7},{456,8... | collective-permute-start | bytes 1572872 | tf_op jit(solution)/shard_map/ppermute | solution.py:146
  40.8 12.9 %collective-permute-start = (bf16[32,32,256]{2,1,0:T(8,128)(2,1)S(1)}, bf16[32,32,256]{2,1,0:T(8,128)(2,1)S(1)}, u32[]{:S(2)}, u32[]{:S(2)}) collective-permute-start(bf16[32,32,256]{2,1,0:T(8,128)(2,1)S(1)} %bitcast.37), channel_id=1, source_target_pairs={{0,1},{1,0},{2,3},{3,2},{4,5},{5,4},{6,7},{7,6},{8,9},{9,8},{10,11... | collective-permute-start | bytes 1572872 | tf_op jit(solution)/shard_map/ppermute | solution.py:152
  43.4 10.4 %collective-permute-start.2 = (bf16[32,32,256]{2,1,0:T(8,128)(2,1)S(1)}, bf16[32,32,256]{2,1,0:T(8,128)(2,1)S(1)}, u32[]{:S(2)}, u32[]{:S(2)}) collective-permute-start(bf16[32,32,256]{2,1,0:T(8,128)(2,1)S(1)} %collective-permute-done.1), channel_id=1, source_target_pairs={{0,1},{1,0},{2,3},{3,2},{4,5},{5,4},{6,7},{7,6},{8,9},{9,8},{10,11... | collective-permute-start | bytes 1572872 | tf_op jit(solution)/shard_map/ppermute | solution.py:152
  45.9 9.3 %copy-start.2 = (bf16[8,2,256,256]{3,2,1,0:T(8,128)(2,1)S(1)}, bf16[8,2,256,256]{3,2,1,0:T(8,128)(2,1)}, u32[]{:S(2)}) copy-start(bf16[8,2,256,256]{3,2,1,0:T(8,128)(2,1)} %left_ref.1) | copy-start | bytes 6291460
  45.9 9.3 %copy-start.3 = (s32[8]{0:T(128)S(1)}, s32[8]{0:T(128)}, u32[]{:S(2)}) copy-start(s32[8]{0:T(128)} %charge_ref.1) | copy-start | bytes 100
  45.9 9.3 %copy-start.4 = (s32[32]{0:T(128)S(1)}, s32[32]{0:T(128)}, u32[]{:S(2)}) copy-start(s32[32]{0:T(128)} %sizes_ref.1) | copy-start | bytes 388
  46.0 7.9 %collective-permute-start.4 = (bf16[32,32,256]{2,1,0:T(8,128)(2,1)S(1)}, bf16[32,32,256]{2,1,0:T(8,128)(2,1)S(1)}, u32[]{:S(2)}, u32[]{:S(2)}) collective-permute-start(bf16[32,32,256]{2,1,0:T(8,128)(2,1)S(1)} %collective-permute-done.3), channel_id=1, source_target_pairs={{0,1},{1,0},{2,3},{3,2},{4,5},{5,4},{6,7},{7,6},{8,9},{9,8},{10,11... | collective-permute-start | bytes 1572872 | tf_op jit(solution)/shard_map/ppermute | solution.py:152
  48.5 6.6 %collective-permute-start.6 = (bf16[32,32,256]{2,1,0:T(8,128)(2,1)S(1)}, bf16[32,32,256]{2,1,0:T(8,128)(2,1)S(1)}, u32[]{:S(2)}, u32[]{:S(2)}) collective-permute-start(bf16[32,32,256]{2,1,0:T(8,128)(2,1)S(1)} %collective-permute-done.5), channel_id=1, source_target_pairs={{0,1},{1,0},{2,3},{3,2},{4,5},{5,4},{6,7},{7,6},{8,9},{9,8},{10,11... | collective-permute-start | bytes 1572872 | tf_op jit(solution)/shard_map/ppermute | solution.py:152
  54.0 2.7 %copy-start.1 = (bf16[8,2,256,256]{3,2,1,0:T(8,128)(2,1)S(1)}, bf16[8,2,256,256]{3,2,1,0:T(8,128)(2,1)}, u32[]{:S(2)}) copy-start(bf16[8,2,256,256]{3,2,1,0:T(8,128)(2,1)} %right_ref.1) | copy-start | bytes 6291460
